TPU v7x, 512 devices: a whole 4x8x8 slice. The times are simulated.
512 devices in a mesh: row: 16 (over z, y_hi), col: 32 (over x, y_lo, core).
Axes of the slice: x: 4, y: 8 (y_hi: 2, y_lo: 4; y = y_hi * 4 + y_lo), z: 8, core: 2. Of those that a mesh axis runs over, the one named last changes fastest.
Arguments:
- fine_queries: bfloat16 [16, 32, 128, 512], P('row', 'col'), may hold values from -288 to 288
- fine_keys: bfloat16 [16, 32, 128, 512], P('row', 'col'), may hold values from -6 to 6
- fine_values: bfloat16 [16, 32, 128, 512], P('row', 'col'), may hold values from -6 to 6
- grad_out: bfloat16 [16, 32, 128, 512], P('row', 'col'), may hold values from -6 to 6
- coarse_keys: bfloat16 [512, 512], P(('row', 'col')), may hold values from -6 to 6
- coarse_values: bfloat16 [512, 512], P(('row', 'col')), may hold values from -6 to 6
- tile_counts: int32 [16, 32], replicated, may hold values from 1 to 128, as said below
Outputs:
- grad_q: bfloat16 [16, 32, 128, 512], P('row', 'col')
- grad_k: bfloat16 [16, 32, 128, 512], P('row', 'col')
- grad_v: bfloat16 [16, 32, 128, 512], P('row', 'col')
- grad_coarse_k: float32 [512, 512], P(('row', 'col'))
- grad_coarse_v: float32 [512, 512], P(('row', 'col'))
Inputs may be any that keep to these rules, and one draw needn't show every extreme that they name: `tile_counts`: live fine tokens of each tile; some tile has all 128 slots live.
All inputs are finite; a program needn't handle non-finite values.
Results may differ from a plain program's by a relative error of at most 0.0075.
Values may be sent and summed in bfloat16 or wider, within the bound.
No kernel may reach another device: no remote copies, remote signals or barrier semaphores. Data moves between devices by JAX's collectives and lax.ppermute only.
A program may use at most 64 MiB of HBM per device.

v0:
```python
import jax
import jax.numpy as jnp
from jax import lax
from jax.sharding import PartitionSpec as P

HEADS = 8
HEAD_DIM = 64


def shifted(block, axis, distance):
    devices = range(lax.axis_size(axis))
    route = [(i - distance, i) for i in devices if i - distance in devices]
    return lax.ppermute(block, axis, route)


def with_halo(block, sides, width):
    for axis, dim in sides:
        count = lax.axis_size(axis)
        forward = [(i, i + 1) for i in range(count - 1)]
        backward = [(target, source) for source, target in forward]
        low = lax.ppermute(
            lax.slice_in_dim(block, block.shape[dim] - width, None, axis=dim), axis, forward
        )
        high = lax.ppermute(lax.slice_in_dim(block, 0, width, axis=dim), axis, backward)
        block = jnp.concatenate([low, block, high], axis=dim)
    return block


def return_cols_first(key_block, value_block):
    lower = shifted((key_block[:, 0], value_block[:, 0]), "col", -1)
    higher = shifted((key_block[:, 2], value_block[:, 2]), "col", 1)
    key_line = key_block[:, 1] + lower[0] + higher[0]
    value_line = value_block[:, 1] + lower[1] + higher[1]
    below = shifted((key_line[0], value_line[0]), "row", -1)
    above = shifted((key_line[2], value_line[2]), "row", 1)
    return (key_line[1] + below[0] + above[0], value_line[1] + below[1] + above[1])


def per_device(
    fine_queries, fine_keys, fine_values, grad_out, coarse_keys, coarse_values, tile_counts
):
    rows = fine_queries.shape[2]
    width = fine_queries.shape[3]
    heads = HEADS
    head_dim = HEAD_DIM
    scale = head_dim ** (-0.5)
    group = min(4, heads)
    span = group * head_dim
    row_at = lax.axis_index("row")
    col_at = lax.axis_index("col")
    padded_counts = jnp.pad(tile_counts, 1)
    near_counts = lax.dynamic_slice(padded_counts, (row_at, col_at), (3, 3)).reshape(9)
    own_count = lax.dynamic_slice(tile_counts, (row_at, col_at), (1, 1)).reshape(())
    positions = jnp.arange(rows, dtype=jnp.int32)
    near_live = (positions[None, :] < near_counts[:, None]).reshape(-1)
    own_live = positions < own_count
    near_keys, near_values = (
        with_halo(fine_keys, (("row", 0), ("col", 1)), 1),
        with_halo(fine_values, (("row", 0), ("col", 1)), 1),
    )
    every_keys, every_values = (
        lax.all_gather(coarse_keys, ("row", "col"), axis=0, tiled=True),
        lax.all_gather(coarse_values, ("row", "col"), axis=0, tiled=True),
    )
    fine_count = 9 * rows
    coarse_count = every_keys.shape[0]
    keys = jnp.concatenate([near_keys.reshape(fine_count, width), every_keys], axis=0)
    values = jnp.concatenate([near_values.reshape(fine_count, width), every_values], axis=0)
    key_live = jnp.concatenate([near_live, jnp.ones((coarse_count,), dtype=bool)])
    query = fine_queries[0, 0]
    upstream = grad_out[0, 0]
    query_grads = []
    key_parts = []
    value_parts = []
    for number in range(heads // group):
        lower = number * span
        upper = lower + span
        query_part = query[:, lower:upper].reshape(rows, group, head_dim)
        upstream_part = upstream[:, lower:upper].reshape(rows, group, head_dim)
        key_part = keys[:, lower:upper].reshape(-1, group, head_dim)
        value_part = values[:, lower:upper].reshape(-1, group, head_dim)
        scores = (
            jnp.einsum("qhd,khd->hqk", query_part, key_part, preferred_element_type=jnp.float32)
            * scale
        )
        masked = jnp.where(key_live[None, None, :], scores, -1e30)
        peak = jnp.max(masked, axis=-1, keepdims=True)
        lse = peak + jnp.log(jnp.sum(jnp.exp(masked - peak), axis=-1, keepdims=True))
        valid = own_live[None, :, None] & key_live[None, None, :]
        probs = jnp.where(valid, jnp.exp(scores - lse), 0.0)
        probs_low = probs.astype(jnp.bfloat16)
        attended = jnp.einsum(
            "hqk,khd->qhd", probs_low, value_part, preferred_element_type=jnp.float32
        )
        delta = jnp.sum(upstream_part.astype(jnp.float32) * attended, axis=-1)
        grad_probs = jnp.einsum(
            "qhd,khd->hqk", upstream_part, value_part, preferred_element_type=jnp.float32
        )
        grad_scores = probs * (grad_probs - delta.T[:, :, None])
        grad_low = grad_scores.astype(jnp.bfloat16)
        query_grads.append(
            jnp.einsum(
                "hqk,khd->qhd", grad_low, key_part, preferred_element_type=jnp.float32
            ).reshape(rows, span)
            * scale
        )
        key_parts.append(
            jnp.einsum(
                "hqk,qhd->khd", grad_low, query_part, preferred_element_type=jnp.float32
            ).reshape(-1, span)
            * scale
        )
        value_parts.append(
            jnp.einsum(
                "hqk,qhd->khd", probs_low, upstream_part, preferred_element_type=jnp.float32
            ).reshape(-1, span)
        )
    grad_q = jnp.concatenate(query_grads, axis=-1).astype(jnp.bfloat16).reshape(1, 1, rows, width)
    key_terms = jnp.concatenate(key_parts, axis=-1)
    value_terms = jnp.concatenate(value_parts, axis=-1)
    coarse_key_terms = key_terms[fine_count:]
    coarse_value_terms = value_terms[fine_count:]
    key_block = key_terms[:fine_count].reshape(3, 3, rows, width)
    value_block = value_terms[:fine_count].reshape(3, 3, rows, width)
    grad_coarse_k, grad_coarse_v = (
        lax.psum_scatter(coarse_key_terms, ("row", "col"), scatter_dimension=0, tiled=True),
        lax.psum_scatter(coarse_value_terms, ("row", "col"), scatter_dimension=0, tiled=True),
    )
    key_sum, value_sum = return_cols_first(key_block, value_block)
    grad_k = key_sum.astype(jnp.bfloat16).reshape(1, 1, rows, width)
    grad_v = value_sum.astype(jnp.bfloat16).reshape(1, 1, rows, width)
    return (grad_q, grad_k, grad_v, grad_coarse_k, grad_coarse_v)


def solution(mesh):
    return jax.shard_map(
        per_device,
        mesh=mesh,
        in_specs=(
            P("row", "col", None, None),
            P("row", "col", None, None),
            P("row", "col", None, None),
            P("row", "col", None, None),
            P(("row", "col"), None),
            P(("row", "col"), None),
            P(),
        ),
        out_specs=(
            P("row", "col", None, None),
            P("row", "col", None, None),
            P("row", "col", None, None),
            P(("row", "col"), None),
            P(("row", "col"), None),
        ),
        check_vma=False,
    )
```

profile of v0, /device:TPU:1, one launch (start us, length us, event | category | flops | bytes accessed | tf_op | source)
XLA Modules:
  0.0 1798.7 jit_solution(9429796046013365201)
XLA Ops:
  7.2 8.3 collective-permute-start
  15.5 1.3 collective-permute-start.1
  16.8 7.9 collective-permute-start.4
  24.7 1.3 collective-permute-start.5
  26.0 0.8 pad_dynamic-slice_fusion
  26.9 0.9 fusion.42
  27.8 0.9 fusion.41
  28.7 695.3 %all-gather = bf16[512,1,512]{2,1,0:T(2,128)(2,1)S(1)} all-gather(bf16[1,1,512]{2,1,0:T(2,128)(2,1)} %bitcast.209), channel_id=1, replica_groups=mesh['row'=16,'col'=32] {'row','col'}, dimensions={0}, use_global_device_ids=true | all-gather | bytes 525312 | tf_op jit(solution)/shard_map/all_gather | solution.py:62
  724.0 679.3 %all-gather.1 = bf16[512,1,512]{2,1,0:T(2,128)(2,1)S(1)} all-gather(bf16[1,1,512]{2,1,0:T(2,128)(2,1)} %bitcast.210), channel_id=1, replica_groups=mesh['row'=16,'col'=32] {'row','col'}, dimensions={0}, use_global_device_ids=true | all-gather | bytes 525312 | tf_op jit(solution)/shard_map/all_gather | solution.py:63
  1403.4 0.7 copy.96
  1404.1 0.7 copy.102
  1406.3 2.3 copy.130
  1408.6 2.3 copy.131
  1410.9 1.3 dynamic_slice.6
  1412.9 2.1 collective-permute-start.3
  1415.0 3.5 collective-permute-start.2
  1418.6 1.9 collective-permute-start.7
  1420.5 3.6 collective-permute-start.6
  1424.2 1.0 broadcast_and_fusion
  1425.3 0.9 copy.94
  1426.2 8.5 collective-permute-done.7
  1434.6 0.8 copy-done.14
  1435.4 1.4 pad_maximum_fusion.1
  1437.5 1.2 fusion.17
  1439.7 1.1 bitcast_reduce_fusion.1
  1440.8 1.5 fusion.5
  1442.4 1.2 fusion.2
  1443.6 2.0 fusion.31
  1445.6 0.9 fusion.14
  1446.5 1.3 fusion.3
  1447.8 1.1 fusion.12
  1448.9 0.7 convolution_multiply_fusion.3
  1449.8 2.1 fusion.28
  1451.8 0.9 fusion.15
  1452.7 0.8 copy.110
  1453.5 1.8 copy.117
  1455.3 3.5 fusion
  1458.8 1.2 copy-done.5
  1459.9 1.9 convolution_multiply_fusion.2
  1461.9 2.7 copy.111
  1464.6 2.7 copy.118
  1467.3 1.6 fusion.9
  1468.9 1.3 slice_bitcast_fusion.4
  1470.2 2.0 collective-permute-start.8
  1472.3 3.8 collective-permute-start.9
  1476.1 1.8 fusion.8
  1478.7 0.7 copy.106
  1479.6 2.9 slice_bitcast_fusion.1
  1482.4 2.0 collective-permute-start.12
  1484.5 3.6 collective-permute-start.13
  1488.2 1.1 pad_maximum_fusion.2
  1489.3 1.1 pad_maximum_fusion.3
  1491.1 1.9 collective-permute-done.8
  1493.1 1.9 fusion.21
  1495.0 1.3 collective-permute-start.10
  1496.3 7.9 collective-permute-start.11
  1504.2 18.1 %collective-permute-done.12 = f32[3,128,512]{2,1,0:T(8,128)} collective-permute-done((f32[3,128,512]{2,1,0:T(8,128)}, f32[3,128,512]{2,1,0:T(8,128)}, u32[]{:S(2)}, u32[]{:S(2)}) %collective-permute-start.12) | collective-permute-done | bytes 786464 | tf_op jit(solution)/shard_map/ppermute | solution.py:13
  1522.3 1.9 fusion.19
  1524.2 0.7 slice_bitcast_fusion.7
  1524.9 1.3 collective-permute-start.14
  1526.2 7.9 collective-permute-start.15
  1534.1 253.7 %all-reduce.7.cloned.1.call-done = (f32[512,512]{1,0:T(8,128)}, f32[512,512]{1,0:T(8,128)}) async-done(((f32[512,512]{1,0:T(8,128)}, f32[512,512]{1,0:T(8,128)}), (f32[512,512]{1,0:T(8,128)}, f32[512,512]{1,0:T(8,128)})) %all-reduce.7.cloned.1.call-update) | async-done | bytes 2097168
  1787.8 1.3 constant_dynamic-slice_fusion.1
  1789.1 1.3 constant_dynamic-slice_fusion
  (79 shorter events, 7.4 us)
Async XLA Ops:
  7.2 1780.6 %all-reduce.7.cloned.1.call-start = ((), (), s32[]{:S(2)}) async-start(), calls=%async_computation | async-start | bytes 4194304
  7.2 1405.6 %collective-permute-start = (bf16[1,1,128,512]{3,2,1,0:T(8,128)(2,1)}, bf16[1,1,128,512]{3,2,1,0:T(8,128)(2,1)S(1)}, u32[]{:S(2)}, u32[]{:S(2)}) collective-permute-start(bf16[1,1,128,512]{3,2,1,0:T(8,128)(2,1)} %param.8), channel_id=1, source_target_pairs={{0,32},{32,64},{64,96},{96,128},{128,160},{160,192},{192,224},{224... | collective-permute-start | bytes 393224 | tf_op jit(solution)/shard_map/ppermute | solution.py:21
  15.5 1397.4 %collective-permute-start.1 = (bf16[1,1,128,512]{3,2,1,0:T(8,128)(2,1)}, bf16[1,1,128,512]{3,2,1,0:T(8,128)(2,1)S(1)}, u32[]{:S(2)}, u32[]{:S(2)}) collective-permute-start(bf16[1,1,128,512]{3,2,1,0:T(8,128)(2,1)} %param.8), channel_id=1, source_target_pairs={{32,0},{64,32},{96,64},{128,96},{160,128},{192,160},{224,192},{256... | collective-permute-start | bytes 393224 | tf_op jit(solution)/shard_map/ppermute | solution.py:24
  16.8 1401.7 %collective-permute-start.4 = (bf16[1,1,128,512]{3,2,1,0:T(8,128)(2,1)}, bf16[1,1,128,512]{3,2,1,0:T(8,128)(2,1)S(1)}, u32[]{:S(2)}, u32[]{:S(2)}) collective-permute-start(bf16[1,1,128,512]{3,2,1,0:T(8,128)(2,1)} %param.9), channel_id=1, source_target_pairs={{0,32},{32,64},{64,96},{96,128},{128,160},{160,192},{192,224},{224... | collective-permute-start | bytes 393224 | tf_op jit(solution)/shard_map/ppermute | solution.py:21
  24.7 1393.8 %collective-permute-start.5 = (bf16[1,1,128,512]{3,2,1,0:T(8,128)(2,1)}, bf16[1,1,128,512]{3,2,1,0:T(8,128)(2,1)S(1)}, u32[]{:S(2)}, u32[]{:S(2)}) collective-permute-start(bf16[1,1,128,512]{3,2,1,0:T(8,128)(2,1)} %param.9), channel_id=1, source_target_pairs={{32,0},{64,32},{96,64},{128,96},{160,128},{192,160},{224,192},{256... | collective-permute-start | bytes 393224 | tf_op jit(solution)/shard_map/ppermute | solution.py:24
  724.0 688.9 %copy-start.20 = (bf16[1,1,128,512]{3,2,1,0:T(8,128)(2,1)S(1)}, bf16[1,1,128,512]{3,2,1,0:T(8,128)(2,1)}, u32[]{:S(2)}) copy-start(bf16[1,1,128,512]{3,2,1,0:T(8,128)(2,1)} %param.8) | copy-start | bytes 393220
  1403.4 15.1 copy-start.21
  1412.9 12.2 collective-permute-start.3
  1415.0 10.1 collective-permute-start.2
  1418.6 7.6 copy-start.12
  1418.6 16.1 collective-permute-start.7
  1420.5 14.9 collective-permute-start.6
  1434.6 0.8 copy-start.14
  1437.5 1.3 copy-start.9
  1438.7 2.1 copy-start.7
  1438.7 0.9 copy-start.13
  1438.9 12.9 copy-start.11
  1438.9 1.9 copy-start.17
  1442.3 9.5 copy-start.3
  1442.3 1.2 copy-start.10
  1442.3 1.2 copy-start.16
  1448.9 0.8 copy-start.15
  1458.7 1.2 copy-start.5
  1468.9 9.0 copy-start.4
  1468.9 7.2 copy-start.1
  1470.2 22.9 %collective-permute-start.8 = (f32[3,128,512]{2,1,0:T(8,128)}, f32[3,128,512]{2,1,0:T(8,128)}, u32[]{:S(2)}, u32[]{:S(2)}) collective-permute-start(f32[3,128,512]{2,1,0:T(8,128)} %get-tuple-element.11), channel_id=1, source_target_pairs={{1,0},{2,1},{3,2},{4,3},{5,4},{6,5},{7,6},{8,7},{9,8},{10,9},{11,1... | collective-permute-start | bytes 2359304 | tf_op jit(solution)/shard_map/ppermute | solution.py:13
  1472.2 5.6 copy-start.6
  1472.2 5.6 copy-start.8
  1472.3 20.8 %collective-permute-start.9 = (f32[3,128,512]{2,1,0:T(8,128)}, f32[3,128,512]{2,1,0:T(8,128)}, u32[]{:S(2)}, u32[]{:S(2)}) collective-permute-start(f32[3,128,512]{2,1,0:T(8,128)} %get-tuple-element.12), channel_id=1, source_target_pairs={{0,1},{1,2},{2,3},{3,4},{4,5},{5,6},{6,7},{7,8},{8,9},{9,10},{10,1... | collective-permute-start | bytes 2359304 | tf_op jit(solution)/shard_map/ppermute | solution.py:13
  1477.9 0.8 copy-start.18
  1479.6 8.6 copy-start.2
  1482.4 6.8 copy-start
  1482.4 39.9 %collective-permute-start.12 = (f32[3,128,512]{2,1,0:T(8,128)}, f32[3,128,512]{2,1,0:T(8,128)}, u32[]{:S(2)}, u32[]{:S(2)}) collective-permute-start(f32[3,128,512]{2,1,0:T(8,128)} %get-tuple-element.9), channel_id=1, source_target_pairs={{1,0},{2,1},{3,2},{4,3},{5,4},{6,5},{7,6},{8,7},{9,8},{10,9},{11,1... | collective-permute-start | bytes 2359304 | tf_op jit(solution)/shard_map/ppermute | solution.py:13
  1484.5 37.8 %collective-permute-start.13 = (f32[3,128,512]{2,1,0:T(8,128)}, f32[3,128,512]{2,1,0:T(8,128)}, u32[]{:S(2)}, u32[]{:S(2)}) collective-permute-start(f32[3,128,512]{2,1,0:T(8,128)} %get-tuple-element.10), channel_id=1, source_target_pairs={{0,1},{1,2},{2,3},{3,4},{4,5},{5,6},{6,7},{7,8},{8,9},{9,10},{10,1... | collective-permute-start | bytes 2359304 | tf_op jit(solution)/shard_map/ppermute | solution.py:13
  1489.3 1.2 copy-start.19
  1495.0 295.4 %collective-permute-start.10 = (f32[128,512]{1,0:T(8,128)S(1)}, f32[128,512]{1,0:T(8,128)S(1)}, u32[]{:S(2)}, u32[]{:S(2)}) collective-permute-start(f32[128,512]{1,0:T(8,128)S(1)} %get-tuple-element.19), channel_id=1, source_target_pairs={{32,0},{64,32},{96,64},{128,96},{160,128},{192,160},{224,192},{256... | collective-permute-start | bytes 786440 | tf_op jit(solution)/shard_map/ppermute | solution.py:13
  1496.3 294.1 %collective-permute-start.11 = (f32[128,512]{1,0:T(8,128)S(1)}, f32[128,512]{1,0:T(8,128)S(1)}, u32[]{:S(2)}, u32[]{:S(2)}) collective-permute-start(f32[128,512]{1,0:T(8,128)S(1)} %get-tuple-element.20), channel_id=1, source_target_pairs={{0,32},{32,64},{64,96},{96,128},{128,160},{160,192},{192,224},{224... | collective-permute-start | bytes 786440 | tf_op jit(solution)/shard_map/ppermute | solution.py:13
  1524.9 266.2 %collective-permute-start.14 = (f32[128,512]{1,0:T(8,128)}, f32[128,512]{1,0:T(8,128)S(1)}, u32[]{:S(2)}, u32[]{:S(2)}) collective-permute-start(f32[128,512]{1,0:T(8,128)} %get-tuple-element.17), channel_id=1, source_target_pairs={{32,0},{64,32},{96,64},{128,96},{160,128},{192,160},{224,192},{256... | collective-permute-start | bytes 786440 | tf_op jit(solution)/shard_map/ppermute | solution.py:13
  1526.2 264.9 %collective-permute-start.15 = (f32[128,512]{1,0:T(8,128)S(1)}, f32[128,512]{1,0:T(8,128)S(1)}, u32[]{:S(2)}, u32[]{:S(2)}) collective-permute-start(f32[128,512]{1,0:T(8,128)S(1)} %get-tuple-element.18), channel_id=1, source_target_pairs={{0,32},{32,64},{64,96},{96,128},{128,160},{160,192},{192,224},{224... | collective-permute-start | bytes 786440 | tf_op jit(solution)/shard_map/ppermute | solution.py:13
Sparse Core Ops, SparseCore 0:
  1490.6 297.1 all-reduce.6
where the time goes:
time: 1800 us
  blocking collectives  1370 us (76%)
  waiting for transfers between devices  282 us (16%)
  starting transfers between devices  59.8 us (3%)
  local copies, waits for them, and re-layouts  32.6 us (2%)
    all_gather x1, blocking collectives, per_device(): lax.all_gather(coarse_keys, ('row', 'col'), axis=0, tiled=True)  695 us
    all_gather x1, blocking collectives, per_device(): lax.all_gather(coarse_values, ('row', 'col'), axis=0, tiled=True)  679 us
    unnamed x2, waiting for transfers between devices  254 us
  transfers between devices with their start and end apart: 17, of which 4 were waited for; matrix products, arithmetic and copies ran while one was open for 2% of the time, Pallas kernels for 0%

commit v1 on v0

v1 whole, which is shorter than its diff:
```python
import functools

import jax
import jax.numpy as jnp
from jax import lax
from jax.experimental import pallas as pl
from jax.experimental.pallas import tpu as pltpu
from jax.sharding import PartitionSpec as P

HEAD_DIM = 64
LANES = 128
SCALE = HEAD_DIM ** (-0.5)
NEGATIVE = -1e30

GATHER_ORDER = (
    ("row", 8),
    ("row", 4),
    ("col", 16),
    ("row", 1),
    ("col", 4),
    ("row", 2),
    ("col", 8),
    ("col", 2),
    ("col", 1),
)


def exchange(block, axis, bit):
    return lax.ppermute(block, axis, [(i, i ^ bit) for i in range(lax.axis_size(axis))])


def to_far(block, axis):
    size = lax.axis_size(axis)
    return lax.ppermute(block, axis, [(i, (i + (1 if i % 2 else -1)) % size) for i in range(size)])


def skip_row(block, way):
    size = lax.axis_size("row")
    return lax.ppermute(block, "row", [(i, (i + (-way if i % 2 else way)) % size) for i in range(size)])


def gather_steps():
    return [(axis, bit) for axis, bit in GATHER_ORDER if bit < lax.axis_size(axis)]


def gather_coarse(own):
    width = own.shape[-1]
    block = own.reshape(1, 8, width // 8)
    for axis, bit in gather_steps():
        block = jnp.concatenate([block, exchange(block, axis, bit)], axis=0)
        if block.ndim == 3 and block.shape[0] == 16:
            block = block.reshape(16, width)
    return block


def scatter_coarse(lower, upper):
    steps = gather_steps()[::-1]
    for number, (axis, bit) in enumerate(steps):
        lower = lower + exchange(upper, axis, bit).astype(jnp.float32)
        if number + 1 < len(steps):
            half = lower.shape[0] // 2
            lower, upper = lower[:half], lower[half:]
            if half >= 64:
                upper = upper.astype(jnp.bfloat16)
    return lower


def attention_kernel(
    counts, q_ref, g_ref, own_ref, near_ref, far_ref, coarse_ref,
    dq_ref, own_out, near_out, far_out, low_out, high_out, p_ref, dp_ref,
):
    rows, width = q_ref.shape
    coarse_count = coarse_ref.shape[0]
    half = coarse_count // 2
    step = min(rows, half)
    tiles = []
    for column, (ref, out) in enumerate(((own_ref, own_out), (near_ref, near_out), (far_ref, far_out))):
        for line in range(3):
            tiles.append((ref.at[line], out.at[line], 0, rows, counts[column * 3 + line]))
    for start in range(0, coarse_count, step):
        out = (low_out, start) if start < half else (high_out, start - half)
        tiles.append((coarse_ref.at[start : start + step], out[0].at[out[1] : out[1] + step], 0, step, None))
    starts = []
    total = 0
    for tile in tiles:
        starts.append(total)
        total += tile[3]
    contract_last = (((1,), (1,)), ((), ()))
    contract_first = (((0,), (0,)), ((), ()))
    f32 = jnp.float32

    def stacked(block):
        first = lax.broadcasted_iota(jnp.int32, block.shape, 1) < HEAD_DIM
        zero = jnp.zeros_like(block)
        return jnp.concatenate([jnp.where(first, block, zero), jnp.where(first, zero, block)], axis=0)

    query_at = lax.broadcasted_iota(jnp.int32, (1, 2 * rows), 1)
    query_at = jnp.where(query_at >= rows, query_at - rows, query_at)
    query_live = (query_at < counts[9]).astype(f32)

    def pair(number, carry):
        lane = pl.multiple_of(number * LANES, LANES)
        at_k = pl.ds(lane, LANES)
        at_v = pl.ds(pl.multiple_of(width + number * LANES, LANES), LANES)
        query = stacked(q_ref[:, at_k] * jnp.asarray(SCALE, q_ref.dtype))
        upstream = stacked(g_ref[:, at_k])
        peak = jnp.full((1, 2 * rows), NEGATIVE, f32)
        for (ref, _, _, size, count), start in zip(tiles, starts):
            scores = lax.dot_general(ref[:, at_k], query, contract_last, preferred_element_type=f32)
            if count is not None:
                live = lax.broadcasted_iota(jnp.int32, scores.shape, 0) < count
                scores = jnp.where(live, scores, NEGATIVE)
            p_ref[start : start + size, :] = scores
            peak = jnp.maximum(peak, jnp.max(scores, axis=0, keepdims=True))
        norm = jnp.zeros((1, 2 * rows), f32)
        for (_, _, _, size, _), start in zip(tiles, starts):
            weights = jnp.exp(p_ref[start : start + size, :] - peak)
            p_ref[start : start + size, :] = weights
            norm = norm + jnp.sum(weights, axis=0, keepdims=True)
        inverse = query_live / norm
        delta = jnp.zeros((1, 2 * rows), f32)
        for (ref, out, _, size, _), start in zip(tiles, starts):
            probs = p_ref[start : start + size, :] * inverse
            probs_low = probs.astype(jnp.bfloat16)
            p_ref[start : start + size, :] = probs
            grad_probs = lax.dot_general(ref[:, at_v], upstream, contract_last, preferred_element_type=f32)
            dp_ref[start : start + size, :] = grad_probs
            delta = delta + jnp.sum(probs_low.astype(f32) * grad_probs, axis=0, keepdims=True)
            value_terms = jnp.dot(probs_low, upstream, preferred_element_type=f32)
            out[:, at_v] = value_terms.astype(out.dtype)
        grad_query = jnp.zeros((LANES, 2 * rows), f32)
        for (ref, out, _, size, _), start in zip(tiles, starts):
            span = slice(start, start + size)
            grad_low = (p_ref[span, :] * (dp_ref[span, :] - delta)).astype(jnp.bfloat16)
            key_terms = jnp.dot(grad_low, query, preferred_element_type=f32)
            out[:, at_k] = key_terms.astype(out.dtype)
            grad_query = grad_query + lax.dot_general(
                ref[:, at_k], grad_low, contract_first, preferred_element_type=f32
            )
        both = jnp.concatenate([grad_query[:HEAD_DIM, :rows], grad_query[HEAD_DIM:, rows:]], axis=0)
        dq_ref[:, at_k] = (both.T * SCALE).astype(dq_ref.dtype)
        return carry

    lax.fori_loop(0, width // LANES, pair, 0)


def attention(counts, query, upstream, own, near, far, coarse):
    rows, width = query.shape
    double = 2 * width
    coarse_count = coarse.shape[0]
    keys = 9 * rows + coarse_count
    in_vmem = pl.BlockSpec(memory_space=pltpu.VMEM)
    work = 2 * rows * keys * width
    return pl.pallas_call(
        attention_kernel,
        out_shape=(
            jax.ShapeDtypeStruct((rows, width), jnp.bfloat16),
            jax.ShapeDtypeStruct((3, rows, double), jnp.float32),
            jax.ShapeDtypeStruct((3, rows, double), jnp.bfloat16),
            jax.ShapeDtypeStruct((3, rows, double), jnp.bfloat16),
            jax.ShapeDtypeStruct((coarse_count // 2, double), jnp.float32),
            jax.ShapeDtypeStruct((coarse_count // 2, double), jnp.bfloat16),
        ),
        in_specs=[pl.BlockSpec(memory_space=pltpu.SMEM)] + [in_vmem] * 6,
        out_specs=(in_vmem,) * 6,
        scratch_shapes=[
            pltpu.VMEM((keys, 2 * rows), jnp.float32),
            pltpu.VMEM((keys, 2 * rows), jnp.float32),
        ],
        compiler_params=pltpu.CompilerParams(vmem_limit_bytes=40 * 2**20),
        cost_estimate=pl.CostEstimate(
            flops=5 * work, bytes_accessed=12 * 2**20, transcendentals=rows * keys * width // HEAD_DIM
        ),
    )(counts, query, upstream, own, near, far, coarse)


def neighbour_counts(tile_counts):
    places = []
    for axis, size in zip(("row", "col"), tile_counts.shape):
        here = lax.axis_index(axis)
        odd = here % 2
        near = here + 1 - 2 * odd
        far = here - 1 + 2 * odd
        at = jnp.stack([here, near, far])
        places.append((at.clip(0, size - 1), (at >= 0) & (at < size)))
    (row_at, row_in), (col_at, col_in) = places
    found = tile_counts[row_at[None, :], col_at[:, None]]
    found = jnp.where(row_in[None, :] & col_in[:, None], found, 0).reshape(9)
    return jnp.concatenate([found, found[:1]]).astype(jnp.int32)


def per_device(
    fine_queries, fine_keys, fine_values, grad_out, coarse_keys, coarse_values, tile_counts
):
    rows, width = fine_queries.shape[2:]
    counts = neighbour_counts(tile_counts)
    fine = jnp.concatenate([fine_keys[0, 0], fine_values[0, 0]], axis=-1)
    paired = exchange(fine, "row", 1)
    coarse = gather_coarse(jnp.concatenate([coarse_keys, coarse_values], axis=-1))
    far = skip_row(paired, 2)
    own_column = jnp.stack([fine, paired, far])
    near_column = exchange(own_column, "col", 1)
    far_column = to_far(own_column, "col")
    grad_q, own_terms, near_terms, far_terms, coarse_low, coarse_high = attention(
        counts, fine_queries[0, 0], grad_out[0, 0], own_column, near_column, far_column, coarse
    )
    coarse_sum = scatter_coarse(coarse_low, coarse_high)
    line = (
        own_terms
        + exchange(near_terms, "col", 1).astype(jnp.float32)
        + to_far(far_terms, "col").astype(jnp.float32)
    )
    low = jnp.bfloat16
    forwarded = skip_row(line[2].astype(low), -2).astype(jnp.float32)
    returned = exchange((line[1] + forwarded).astype(low), "row", 1).astype(jnp.float32)
    total = (line[0] + returned).astype(low)
    return (
        grad_q[None, None],
        total[None, None, :, :width],
        total[None, None, :, width:],
        coarse_sum[:, :width],
        coarse_sum[:, width:],
    )


def solution(mesh):
    return jax.shard_map(
        per_device,
        mesh=mesh,
        in_specs=(
            P("row", "col", None, None),
            P("row", "col", None, None),
            P("row", "col", None, None),
            P("row", "col", None, None),
            P(("row", "col"), None),
            P(("row", "col"), None),
            P(),
        ),
        out_specs=(
            P("row", "col", None, None),
            P("row", "col", None, None),
            P("row", "col", None, None),
            P(("row", "col"), None),
            P(("row", "col"), None),
        ),
        check_vma=False,
    )
```

time: 1800 us -> 197 us (0.11)
  the two profiles are of different devices: /device:TPU:1 before, /device:TPU:10 now
where the time goes in v1:
time: 197 us; the launch traced here: 196 us
  starting transfers between devices  108 us (55%)
  waiting for transfers between devices  62.3 us (32%)
  local copies, waits for them, and re-layouts  11.9 us (6%)
  Pallas kernels  9.94 us (5%)
  other arithmetic  2.92 us (1%)
    ppermute x22, starting transfers between devices, exchange(): lax.ppermute(block, axis, [(i, i ^ bit) for i in range(lax.axis_size(axis...  91.9 us
    ppermute x22, waiting for transfers between devices, exchange(): lax.ppermute(block, axis, [(i, i ^ bit) for i in range(lax.axis_size(axis...  57.1 us
    ppermute x2, starting transfers between devices, skip_row(): lax.ppermute(block, 'row', [(i, (i + (-way if i % 2 else way)) % size) fo...  10.2 us
    pallas_call x1, Pallas kernels, attention(): pl.pallas_call(attention_kernel, out_shape=(jax.ShapeDtypeStruct((rows, w...  9.94 us
    concatenate x6, local copies, waits for them, and re-layouts, gather_coarse(): block = jnp.concatenate([block, exchange(block, axis, bit)], axis=0)  7.2 us
    ppermute x2, starting transfers between devices, to_far(): lax.ppermute(block, axis, [(i, (i + (1 if i % 2 else -1)) % size) for i i...  5.67 us
    ppermute x2, waiting for transfers between devices, to_far(): lax.ppermute(block, axis, [(i, (i + (1 if i % 2 else -1)) % size) for i i...  5.12 us
  transfers between devices with their start and end apart: 26, of which 16 were waited for; matrix products, arithmetic and copies ran while one was open for 6% of the time, Pallas kernels for 0%

profile of v1, /device:TPU:10, one launch (start us, length us, event | category | flops | bytes accessed | tf_op | source)
XLA Modules:
  0.0 196.0 jit_solution(4637380037533656615)
XLA Ops:
  0.6 1.0 fusion.9
  1.7 6.8 %collective-permute-start = (bf16[128,1024]{1,0:T(8,128)(2,1)S(1)}, bf16[128,1024]{1,0:T(8,128)(2,1)S(1)}, u32[]{:S(2)}, u32[]{:S(2)}) collective-permute-start(bf16[128,1024]{1,0:T(8,128)(2,1)S(1)} %get-tuple-element.24), channel_id=1, source_target_pairs={{0,32},{32,0},{64,96},{96,64},{128,160},{160,128},{192,224},{224,1... | collective-permute-start | bytes 786440 | tf_op jit(solution)/shard_map/ppermute | solution.py:29
  8.5 0.7 constant_dynamic-update-slice_fusion.1
  9.2 0.7 constant_dynamic-update-slice_fusion
  9.9 10.9 %collective-permute-start.4 = (bf16[1,8,128]{2,0,1:T(2,128)(2,1)S(1)}, bf16[1,8,128]{2,0,1:T(2,128)(2,1)S(1)}, u32[]{:S(2)}, u32[]{:S(2)}) collective-permute-start(bf16[1,8,128]{2,0,1:T(2,128)(2,1)S(1)} %bitcast.55), channel_id=1, source_target_pairs={{0,256},{32,288},{64,320},{96,352},{128,384},{160,416},{192,448},{... | collective-permute-start | bytes 6152 | tf_op jit(solution)/shard_map/ppermute | solution.py:29
  20.8 1.6 collective-permute-done.4
  22.4 4.3 %collective-permute-start.5 = (bf16[2,8,128]{2,0,1:T(2,128)(2,1)S(1)}, bf16[2,8,128]{2,0,1:T(2,128)(2,1)S(1)}, u32[]{:S(2)}, u32[]{:S(2)}) collective-permute-start(bf16[2,8,128]{2,0,1:T(2,128)(2,1)S(1)} %pad_maximum_fusion.4), channel_id=1, source_target_pairs={{0,128},{32,160},{64,192},{96,224},{128,0},{160,32},{192,64},{224,... | collective-permute-start | bytes 12296 | tf_op jit(solution)/shard_map/ppermute | solution.py:29
  26.7 2.1 %collective-permute-done.5 = bf16[2,8,128]{2,0,1:T(2,128)(2,1)S(1)} collective-permute-done((bf16[2,8,128]{2,0,1:T(2,128)(2,1)S(1)}, bf16[2,8,128]{2,0,1:T(2,128)(2,1)S(1)}, u32[]{:S(2)}, u32[]{:S(2)}) %collective-permute-start.5) | collective-permute-done | bytes 4128 | tf_op jit(solution)/shard_map/ppermute | solution.py:29
  28.8 4.0 %collective-permute-start.6 = (bf16[4,8,128]{2,0,1:T(4,128)(2,1)S(1)}, bf16[4,8,128]{2,0,1:T(4,128)(2,1)S(1)}, u32[]{:S(2)}, u32[]{:S(2)}) collective-permute-start(bf16[4,8,128]{2,0,1:T(4,128)(2,1)S(1)} %pad_maximum_fusion.3), channel_id=1, source_target_pairs={{0,16},{1,17},{2,18},{3,19},{4,20},{5,21},{6,22},{7,23},{8,24},{9,... | collective-permute-start | bytes 24584 | tf_op jit(solution)/shard_map/ppermute | solution.py:29
  32.9 3.4 %collective-permute-start.1 = (bf16[128,1024]{1,0:T(8,128)(2,1)S(1)}, bf16[128,1024]{1,0:T(8,128)(2,1)S(1)}, u32[]{:S(2)}, u32[]{:S(2)}) collective-permute-start(bf16[128,1024]{1,0:T(8,128)(2,1)S(1)} %collective-permute-done), channel_id=1, source_target_pairs={{0,64},{32,480},{64,128},{96,32},{128,192},{160,96},{192,256},{224... | collective-permute-start | bytes 786440 | tf_op jit(solution)/shard_map/ppermute | solution.py:39
  36.3 7.4 %collective-permute-start.7 = (bf16[8,8,128]{2,0,1:T(8,128)(2,1)S(1)}, bf16[8,8,128]{2,0,1:T(8,128)(2,1)S(1)}, u32[]{:S(2)}, u32[]{:S(2)}) collective-permute-start(bf16[8,8,128]{2,0,1:T(8,128)(2,1)S(1)} %pad_maximum_fusion.2), channel_id=1, source_target_pairs={{0,32},{32,0},{64,96},{96,64},{128,160},{160,128},{192,224},{224,1... | collective-permute-start | bytes 49160 | tf_op jit(solution)/shard_map/ppermute | solution.py:29
  43.7 2.1 %collective-permute-done.7 = bf16[8,8,128]{2,0,1:T(8,128)(2,1)S(1)} collective-permute-done((bf16[8,8,128]{2,0,1:T(8,128)(2,1)S(1)}, bf16[8,8,128]{2,0,1:T(8,128)(2,1)S(1)}, u32[]{:S(2)}, u32[]{:S(2)}) %collective-permute-start.7) | collective-permute-done | bytes 16416 | tf_op jit(solution)/shard_map/ppermute | solution.py:29
  45.9 4.1 %collective-permute-start.8 = (bf16[16,1024]{1,0:T(8,128)(2,1)S(1)}, bf16[16,1024]{1,0:T(8,128)(2,1)S(1)}, u32[]{:S(2)}, u32[]{:S(2)}) collective-permute-start(bf16[16,1024]{1,0:T(8,128)(2,1)S(1)} %concatenate.92), channel_id=1, source_target_pairs={{0,4},{1,5},{2,6},{3,7},{4,0},{5,1},{6,2},{7,3},{8,12},{9,13},{10,... | collective-permute-start | bytes 98312 | tf_op jit(solution)/shard_map/ppermute | solution.py:29
  50.0 2.7 %collective-permute-done.8 = bf16[16,1024]{1,0:T(8,128)(2,1)S(1)} collective-permute-done((bf16[16,1024]{1,0:T(8,128)(2,1)S(1)}, bf16[16,1024]{1,0:T(8,128)(2,1)S(1)}, u32[]{:S(2)}, u32[]{:S(2)}) %collective-permute-start.8) | collective-permute-done | bytes 32800 | tf_op jit(solution)/shard_map/ppermute | solution.py:29
  52.8 3.4 %collective-permute-start.9 = (bf16[32,1024]{1,0:T(8,128)(2,1)S(1)}, bf16[32,1024]{1,0:T(8,128)(2,1)S(1)}, u32[]{:S(2)}, u32[]{:S(2)}) collective-permute-start(bf16[32,1024]{1,0:T(8,128)(2,1)S(1)} %concatenate.93), channel_id=1, source_target_pairs={{0,64},{32,96},{64,0},{96,32},{128,192},{160,224},{192,128},{224,1... | collective-permute-start | bytes 196616 | tf_op jit(solution)/shard_map/ppermute | solution.py:29
  56.2 2.7 %collective-permute-done.9 = bf16[32,1024]{1,0:T(8,128)(2,1)S(1)} collective-permute-done((bf16[32,1024]{1,0:T(8,128)(2,1)S(1)}, bf16[32,1024]{1,0:T(8,128)(2,1)S(1)}, u32[]{:S(2)}, u32[]{:S(2)}) %collective-permute-start.9) | collective-permute-done | bytes 65568 | tf_op jit(solution)/shard_map/ppermute | solution.py:29
  59.0 3.3 %collective-permute-start.10 = (bf16[64,1024]{1,0:T(8,128)(2,1)S(1)}, bf16[64,1024]{1,0:T(8,128)(2,1)S(1)}, u32[]{:S(2)}, u32[]{:S(2)}) collective-permute-start(bf16[64,1024]{1,0:T(8,128)(2,1)S(1)} %concatenate.94), channel_id=1, source_target_pairs={{0,8},{1,9},{2,10},{3,11},{4,12},{5,13},{6,14},{7,15},{8,0},{9,1},... | collective-permute-start | bytes 393224 | tf_op jit(solution)/shard_map/ppermute | solution.py:29
  62.3 0.6 compare_and_fusion.1
  62.9 2.9 %collective-permute-done.10 = bf16[64,1024]{1,0:T(8,128)(2,1)S(1)} collective-permute-done((bf16[64,1024]{1,0:T(8,128)(2,1)S(1)}, bf16[64,1024]{1,0:T(8,128)(2,1)S(1)}, u32[]{:S(2)}, u32[]{:S(2)}) %collective-permute-start.10) | collective-permute-done | bytes 131104 | tf_op jit(solution)/shard_map/ppermute | solution.py:29
  65.9 3.5 %collective-permute-start.11 = (bf16[128,1024]{1,0:T(8,128)(2,1)S(1)}, bf16[128,1024]{1,0:T(8,128)(2,1)S(1)}, u32[]{:S(2)}, u32[]{:S(2)}) collective-permute-start(bf16[128,1024]{1,0:T(8,128)(2,1)S(1)} %concatenate.95), channel_id=1, source_target_pairs={{0,2},{1,3},{2,0},{3,1},{4,6},{5,7},{6,4},{7,5},{8,10},{9,11},{10,... | collective-permute-start | bytes 786440 | tf_op jit(solution)/shard_map/ppermute | solution.py:29
  69.4 0.1 pad_maximum_fusion.own_ref
  69.5 1.9 collective-permute-start.3
  71.4 3.3 %collective-permute-start.2 = (bf16[3,128,1024]{2,1,0:T(8,128)(2,1)S(1)}, bf16[3,128,1024]{2,1,0:T(8,128)(2,1)S(1)}, u32[]{:S(2)}, u32[]{:S(2)}) collective-permute-start(bf16[3,128,1024]{2,1,0:T(8,128)(2,1)S(1)} %pad_maximum_fusion.own_ref), channel_id=1, source_target_pairs={{0,1},{1,0},{2,3},{3,2},{4,5},{5,4},{6,7},{7,6},{8,9},{9,8},{10,11... | collective-permute-start | bytes 2359304 | tf_op jit(solution)/shard_map/ppermute | solution.py:29
  74.7 0.1 compare_and_fusion
  74.8 0.1 concatenate.96
  75.0 1.9 collective-permute-start.12
  77.0 0.1 reshape.174
  77.1 0.7 gather_fusion
  77.8 0.1 reshape.177
  77.9 0.1 and_select_fusion
  78.0 0.1 select_n.39
  78.1 0.1 pad_add_fusion.2.counts
  78.2 0.8 collective-permute-done.12
  79.0 6.9 %concatenate.97.coarse_ref = bf16[512,1024]{1,0:T(8,128)(2,1)S(1)} concatenate(bf16[1,1024]{1,0:T(2,128)(2,1)S(1)} %constant_dynamic-update-slice_fusion, bf16[1,1024]{1,0:T(2,128)(2,1)} %bitcast.64, bf16[2,1024]{1,0:T(2,128)(2,1)} %bitcast.70, bf16[4,1024]{1,0:T(4,128)(2,1)} %bitcast.54, bf16[8,1024]{1,0:T(8,128)(2,1)} %bitcast.48, bf16[16,1024]{1,0:T(8,128)(2,1)} %copy-done.6, ...), dimensions={0} | concatenate | bytes 2097152 | tf_op jit(solution)/shard_map/concatenate | solution.py:50
  85.9 5.1 %collective-permute-done.3.far_ref = bf16[3,128,1024]{2,1,0:T(8,128)(2,1)S(1)} collective-permute-done((bf16[3,128,1024]{2,1,0:T(8,128)(2,1)S(1)}, bf16[3,128,1024]{2,1,0:T(8,128)(2,1)S(1)}, u32[]{:S(2)}, u32[]{:S(2)}) %collective-permute-start.3) | collective-permute-done | bytes 786464 | tf_op jit(solution)/shard_map/ppermute | solution.py:34
  91.0 0.9 copy-done.2
  91.9 9.9 %shard_map.110 = (bf16[128,512]{1,0:T(8,128)(2,1)}, f32[3,128,1024]{2,1,0:T(8,128)S(1)}, bf16[3,128,1024]{2,1,0:T(8,128)(2,1)S(1)}, bf16[3,128,1024]{2,1,0:T(8,1...) custom-call(s32[10]{0:T(128)S(1)} %pad_add_fusion.2.counts, bf16[128,512]{1,0:T(8,128)(2,1)S(1)} %bitcast.41, ...), custom_call_target="tpu_custom_call" | custom-call | flops 1090519040 | bytes 12582912 | tf_op jit(solution)/shard_map/pallas_call | solution.py:154
  101.8 1.9 collective-permute-start.17
  103.8 1.9 collective-permute-done.17
  105.6 0.1 convert_add_fusion.1
  105.8 4.8 %collective-permute-start.18 = (bf16[128,1024]{1,0:T(8,128)(2,1)S(1)}, bf16[128,1024]{1,0:T(8,128)(2,1)S(1)}, u32[]{:S(2)}, u32[]{:S(2)}) collective-permute-start(bf16[128,1024]{1,0:T(8,128)(2,1)S(1)} %slice.149), channel_id=1, source_target_pairs={{0,2},{1,3},{2,0},{3,1},{4,6},{5,7},{6,4},{7,5},{8,10},{9,11},{10,... | collective-permute-start | bytes 786440 | tf_op jit(solution)/shard_map/ppermute | solution.py:29
  110.6 6.6 %collective-permute-done.18 = bf16[128,1024]{1,0:T(8,128)(2,1)S(1)} collective-permute-done((bf16[128,1024]{1,0:T(8,128)(2,1)S(1)}, bf16[128,1024]{1,0:T(8,128)(2,1)S(1)}, u32[]{:S(2)}, u32[]{:S(2)}) %collective-permute-start.18) | collective-permute-done | bytes 262176 | tf_op jit(solution)/shard_map/ppermute | solution.py:29
  117.2 0.1 slice_add_fusion
  117.3 3.0 %collective-permute-start.19 = (bf16[64,1024]{1,0:T(8,128)(2,1)S(1)}, bf16[64,1024]{1,0:T(8,128)(2,1)S(1)}, u32[]{:S(2)}, u32[]{:S(2)}) collective-permute-start(bf16[64,1024]{1,0:T(8,128)(2,1)S(1)} %slice.150), channel_id=1, source_target_pairs={{0,8},{1,9},{2,10},{3,11},{4,12},{5,13},{6,14},{7,15},{8,0},{9,1},... | collective-permute-start | bytes 393224 | tf_op jit(solution)/shard_map/ppermute | solution.py:29
  120.3 1.9 collective-permute-start.13
  122.3 3.7 %collective-permute-start.14 = (bf16[3,128,1024]{2,1,0:T(8,128)(2,1)S(1)}, bf16[3,128,1024]{2,1,0:T(8,128)(2,1)S(1)}, u32[]{:S(2)}, u32[]{:S(2)}) collective-permute-start(bf16[3,128,1024]{2,1,0:T(8,128)(2,1)S(1)} %get-tuple-element.14), channel_id=1, source_target_pairs={{0,31},{1,2},{2,1},{3,4},{4,3},{5,6},{6,5},{7,8},{8,7},{9,10},{10,... | collective-permute-start | bytes 2359304 | tf_op jit(solution)/shard_map/ppermute | solution.py:34
  126.1 3.3 %collective-permute-start.20 = (f32[32,1024]{1,0:T(8,128)S(1)}, f32[32,1024]{1,0:T(8,128)S(1)}, u32[]{:S(2)}, u32[]{:S(2)}) collective-permute-start(f32[32,1024]{1,0:T(8,128)S(1)} %slice.111), channel_id=1, source_target_pairs={{0,64},{32,96},{64,0},{96,32},{128,192},{160,224},{192,128},{224,1... | collective-permute-start | bytes 393224 | tf_op jit(solution)/shard_map/ppermute | solution.py:29
  129.4 3.5 %collective-permute-done.20 = f32[32,1024]{1,0:T(8,128)S(1)} collective-permute-done((f32[32,1024]{1,0:T(8,128)S(1)}, f32[32,1024]{1,0:T(8,128)S(1)}, u32[]{:S(2)}, u32[]{:S(2)}) %collective-permute-start.20) | collective-permute-done | bytes 131104 | tf_op jit(solution)/shard_map/ppermute | solution.py:29
  133.0 3.2 %collective-permute-start.21 = (f32[16,1024]{1,0:T(8,128)S(1)}, f32[16,1024]{1,0:T(8,128)S(1)}, u32[]{:S(2)}, u32[]{:S(2)}) collective-permute-start(f32[16,1024]{1,0:T(8,128)S(1)} %slice.113), channel_id=1, source_target_pairs={{0,4},{1,5},{2,6},{3,7},{4,0},{5,1},{6,2},{7,3},{8,12},{9,13},{10,... | collective-permute-start | bytes 196616 | tf_op jit(solution)/shard_map/ppermute | solution.py:29
  136.2 9.2 %collective-permute-done.21 = f32[16,1024]{1,0:T(8,128)S(1)} collective-permute-done((f32[16,1024]{1,0:T(8,128)S(1)}, f32[16,1024]{1,0:T(8,128)S(1)}, u32[]{:S(2)}, u32[]{:S(2)}) %collective-permute-start.21) | collective-permute-done | bytes 65568 | tf_op jit(solution)/shard_map/ppermute | solution.py:29
  145.4 8.6 %collective-permute-start.22 = (f32[8,1024]{1,0:T(8,128)S(1)}, f32[8,1024]{1,0:T(8,128)S(1)}, u32[]{:S(2)}, u32[]{:S(2)}) collective-permute-start(f32[8,1024]{1,0:T(8,128)S(1)} %slice.115), channel_id=1, source_target_pairs={{0,32},{32,0},{64,96},{96,64},{128,160},{160,128},{192,224},{224,1... | collective-permute-start | bytes 98312 | tf_op jit(solution)/shard_map/ppermute | solution.py:29
  154.0 0.4 convert_add_fusion
  154.4 1.5 collective-permute-done.22
  155.9 1.9 collective-permute-start.23
  157.9 6.9 %collective-permute-start.15 = (bf16[128,1024]{1,0:T(8,128)(2,1)S(1)}, bf16[128,1024]{1,0:T(8,128)(2,1)S(1)}, u32[]{:S(2)}, u32[]{:S(2)}) collective-permute-start(bf16[128,1024]{1,0:T(8,128)(2,1)S(1)} %fusion.4), channel_id=1, source_target_pairs={{0,448},{32,96},{64,0},{96,160},{128,64},{160,224},{192,128},{224,... | collective-permute-start | bytes 786440 | tf_op jit(solution)/shard_map/ppermute | solution.py:39
  164.8 2.2 %collective-permute-start.24 = (f32[2,1024]{1,0:T(2,128)S(1)}, f32[2,1024]{1,0:T(2,128)S(1)}, u32[]{:S(2)}, u32[]{:S(2)}) collective-permute-start(f32[2,1024]{1,0:T(2,128)S(1)} %slice.119), channel_id=1, source_target_pairs={{0,128},{32,160},{64,192},{96,224},{128,0},{160,32},{192,64},{224,... | collective-permute-start | bytes 24584 | tf_op jit(solution)/shard_map/ppermute | solution.py:29
  167.0 4.3 %collective-permute-done.24 = f32[2,1024]{1,0:T(2,128)S(1)} collective-permute-done((f32[2,1024]{1,0:T(2,128)S(1)}, f32[2,1024]{1,0:T(2,128)S(1)}, u32[]{:S(2)}, u32[]{:S(2)}) %collective-permute-start.24) | collective-permute-done | bytes 8224 | tf_op jit(solution)/shard_map/ppermute | solution.py:29
  171.2 4.9 %collective-permute-start.25 = (f32[1,1024]{1,0:T(1,128)S(1)}, f32[1,1024]{1,0:T(1,128)S(1)}, u32[]{:S(2)}, u32[]{:S(2)}) collective-permute-start(f32[1,1024]{1,0:T(1,128)S(1)} %slice.121), channel_id=1, source_target_pairs={{0,256},{32,288},{64,320},{96,352},{128,384},{160,416},{192,448},{... | collective-permute-start | bytes 12296 | tf_op jit(solution)/shard_map/ppermute | solution.py:29
  176.2 0.1 fusion.1
  176.3 3.1 %collective-permute-start.16 = (bf16[128,1024]{1,0:T(8,128)(2,1)S(1)}, bf16[128,1024]{1,0:T(8,128)(2,1)S(1)}, u32[]{:S(2)}, u32[]{:S(2)}) collective-permute-start(bf16[128,1024]{1,0:T(8,128)(2,1)S(1)} %fusion.1), channel_id=1, source_target_pairs={{0,32},{32,0},{64,96},{96,64},{128,160},{160,128},{192,224},{224,1... | collective-permute-start | bytes 786440 | tf_op jit(solution)/shard_map/ppermute | solution.py:29
  179.4 1.3 collective-permute-done.25
  180.7 0.6 fusion.10
  181.3 14.0 %collective-permute-done.16 = bf16[128,1024]{1,0:T(8,128)(2,1)S(1)} collective-permute-done((bf16[128,1024]{1,0:T(8,128)(2,1)S(1)}, bf16[128,1024]{1,0:T(8,128)(2,1)S(1)}, u32[]{:S(2)}, u32[]{:S(2)}) %collective-permute-start.16) | collective-permute-done | bytes 262176 | tf_op jit(solution)/shard_map/ppermute | solution.py:29
  195.3 0.7 slice_bitcast_fusion.2
  (59 shorter events, 0.6 us)
Async XLA Ops:
  0.6 76.5 %copy-start = (s32[16,32]{1,0:T(8,128)S(1)}, s32[16,32]{1,0:T(8,128)}, u32[]{:S(2)}) copy-start(s32[16,32]{1,0:T(8,128)} %param.13) | copy-start | bytes 6148
  1.7 31.2 %collective-permute-start = (bf16[128,1024]{1,0:T(8,128)(2,1)S(1)}, bf16[128,1024]{1,0:T(8,128)(2,1)S(1)}, u32[]{:S(2)}, u32[]{:S(2)}) collective-permute-start(bf16[128,1024]{1,0:T(8,128)(2,1)S(1)} %get-tuple-element.24), channel_id=1, source_target_pairs={{0,32},{32,0},{64,96},{96,64},{128,160},{160,128},{192,224},{224,1... | collective-permute-start | bytes 786440 | tf_op jit(solution)/shard_map/ppermute | solution.py:29
  9.9 12.5 %collective-permute-start.4 = (bf16[1,8,128]{2,0,1:T(2,128)(2,1)S(1)}, bf16[1,8,128]{2,0,1:T(2,128)(2,1)S(1)}, u32[]{:S(2)}, u32[]{:S(2)}) collective-permute-start(bf16[1,8,128]{2,0,1:T(2,128)(2,1)S(1)} %bitcast.55), channel_id=1, source_target_pairs={{0,256},{32,288},{64,320},{96,352},{128,384},{160,416},{192,448},{... | collective-permute-start | bytes 6152 | tf_op jit(solution)/shard_map/ppermute | solution.py:29
  22.4 52.6 %copy-start.9 = (bf16[1,8,128]{2,0,1:T(2,128)(2,1)}, bf16[1,8,128]{2,0,1:T(2,128)(2,1)S(1)}, u32[]{:S(2)}) copy-start(bf16[1,8,128]{2,0,1:T(2,128)(2,1)S(1)} %collective-permute-done.4) | copy-start | bytes 6148
  22.4 6.4 %collective-permute-start.5 = (bf16[2,8,128]{2,0,1:T(2,128)(2,1)S(1)}, bf16[2,8,128]{2,0,1:T(2,128)(2,1)S(1)}, u32[]{:S(2)}, u32[]{:S(2)}) collective-permute-start(bf16[2,8,128]{2,0,1:T(2,128)(2,1)S(1)} %pad_maximum_fusion.4), channel_id=1, source_target_pairs={{0,128},{32,160},{64,192},{96,224},{128,0},{160,32},{192,64},{224,... | collective-permute-start | bytes 12296 | tf_op jit(solution)/shard_map/ppermute | solution.py:29
  28.8 46.2 %copy-start.10 = (bf16[2,8,128]{2,0,1:T(2,128)(2,1)}, bf16[2,8,128]{2,0,1:T(2,128)(2,1)S(1)}, u32[]{:S(2)}) copy-start(bf16[2,8,128]{2,0,1:T(2,128)(2,1)S(1)} %collective-permute-done.5) | copy-start | bytes 12292
  28.8 7.4 %collective-permute-start.6 = (bf16[4,8,128]{2,0,1:T(4,128)(2,1)S(1)}, bf16[4,8,128]{2,0,1:T(4,128)(2,1)S(1)}, u32[]{:S(2)}, u32[]{:S(2)}) collective-permute-start(bf16[4,8,128]{2,0,1:T(4,128)(2,1)S(1)} %pad_maximum_fusion.3), channel_id=1, source_target_pairs={{0,16},{1,17},{2,18},{3,19},{4,20},{5,21},{6,22},{7,23},{8,24},{9,... | collective-permute-start | bytes 24584 | tf_op jit(solution)/shard_map/ppermute | solution.py:29
  32.9 36.5 %collective-permute-start.1 = (bf16[128,1024]{1,0:T(8,128)(2,1)S(1)}, bf16[128,1024]{1,0:T(8,128)(2,1)S(1)}, u32[]{:S(2)}, u32[]{:S(2)}) collective-permute-start(bf16[128,1024]{1,0:T(8,128)(2,1)S(1)} %collective-permute-done), channel_id=1, source_target_pairs={{0,64},{32,480},{64,128},{96,32},{128,192},{160,96},{192,256},{224... | collective-permute-start | bytes 786440 | tf_op jit(solution)/shard_map/ppermute | solution.py:39
  36.3 38.7 %copy-start.8 = (bf16[4,8,128]{2,0,1:T(4,128)(2,1)}, bf16[4,8,128]{2,0,1:T(4,128)(2,1)S(1)}, u32[]{:S(2)}) copy-start(bf16[4,8,128]{2,0,1:T(4,128)(2,1)S(1)} %collective-permute-done.6) | copy-start | bytes 24580
  36.3 9.5 %collective-permute-start.7 = (bf16[8,8,128]{2,0,1:T(8,128)(2,1)S(1)}, bf16[8,8,128]{2,0,1:T(8,128)(2,1)S(1)}, u32[]{:S(2)}, u32[]{:S(2)}) collective-permute-start(bf16[8,8,128]{2,0,1:T(8,128)(2,1)S(1)} %pad_maximum_fusion.2), channel_id=1, source_target_pairs={{0,32},{32,0},{64,96},{96,64},{128,160},{160,128},{192,224},{224,1... | collective-permute-start | bytes 49160 | tf_op jit(solution)/shard_map/ppermute | solution.py:29
  45.9 29.2 %copy-start.7 = (bf16[8,8,128]{2,0,1:T(8,128)(2,1)}, bf16[8,8,128]{2,0,1:T(8,128)(2,1)S(1)}, u32[]{:S(2)}) copy-start(bf16[8,8,128]{2,0,1:T(8,128)(2,1)S(1)} %collective-permute-done.7) | copy-start | bytes 49156
  45.9 6.8 %collective-permute-start.8 = (bf16[16,1024]{1,0:T(8,128)(2,1)S(1)}, bf16[16,1024]{1,0:T(8,128)(2,1)S(1)}, u32[]{:S(2)}, u32[]{:S(2)}) collective-permute-start(bf16[16,1024]{1,0:T(8,128)(2,1)S(1)} %concatenate.92), channel_id=1, source_target_pairs={{0,4},{1,5},{2,6},{3,7},{4,0},{5,1},{6,2},{7,3},{8,12},{9,13},{10,... | collective-permute-start | bytes 98312 | tf_op jit(solution)/shard_map/ppermute | solution.py:29
  52.7 25.5 %copy-start.6 = (bf16[16,1024]{1,0:T(8,128)(2,1)}, bf16[16,1024]{1,0:T(8,128)(2,1)S(1)}, u32[]{:S(2)}) copy-start(bf16[16,1024]{1,0:T(8,128)(2,1)S(1)} %collective-permute-done.8) | copy-start | bytes 98308
  52.8 6.2 %collective-permute-start.9 = (bf16[32,1024]{1,0:T(8,128)(2,1)S(1)}, bf16[32,1024]{1,0:T(8,128)(2,1)S(1)}, u32[]{:S(2)}, u32[]{:S(2)}) collective-permute-start(bf16[32,1024]{1,0:T(8,128)(2,1)S(1)} %concatenate.93), channel_id=1, source_target_pairs={{0,64},{32,96},{64,0},{96,32},{128,192},{160,224},{192,128},{224,1... | collective-permute-start | bytes 196616 | tf_op jit(solution)/shard_map/ppermute | solution.py:29
  58.9 19.2 %copy-start.4 = (bf16[32,1024]{1,0:T(8,128)(2,1)}, bf16[32,1024]{1,0:T(8,128)(2,1)S(1)}, u32[]{:S(2)}) copy-start(bf16[32,1024]{1,0:T(8,128)(2,1)S(1)} %collective-permute-done.9) | copy-start | bytes 196612
  59.0 6.9 %collective-permute-start.10 = (bf16[64,1024]{1,0:T(8,128)(2,1)S(1)}, bf16[64,1024]{1,0:T(8,128)(2,1)S(1)}, u32[]{:S(2)}, u32[]{:S(2)}) collective-permute-start(bf16[64,1024]{1,0:T(8,128)(2,1)S(1)} %concatenate.94), channel_id=1, source_target_pairs={{0,8},{1,9},{2,10},{3,11},{4,12},{5,13},{6,14},{7,15},{8,0},{9,1},... | collective-permute-start | bytes 393224 | tf_op jit(solution)/shard_map/ppermute | solution.py:29
  65.8 9.2 %copy-start.3 = (bf16[64,1024]{1,0:T(8,128)(2,1)}, bf16[64,1024]{1,0:T(8,128)(2,1)S(1)}, u32[]{:S(2)}) copy-start(bf16[64,1024]{1,0:T(8,128)(2,1)S(1)} %collective-permute-done.10) | copy-start | bytes 393220
  65.8 9.0 %copy-start.11 = (s32[3]{0:T(128)S(1)}, s32[3]{0:T(128)}, u32[]{:S(2)}) copy-start(s32[3]{0:T(128)} %get-tuple-element.20) | copy-start | bytes 40
  65.9 8.9 %collective-permute-start.11 = (bf16[128,1024]{1,0:T(8,128)(2,1)S(1)}, bf16[128,1024]{1,0:T(8,128)(2,1)S(1)}, u32[]{:S(2)}, u32[]{:S(2)}) collective-permute-start(bf16[128,1024]{1,0:T(8,128)(2,1)S(1)} %concatenate.95), channel_id=1, source_target_pairs={{0,2},{1,3},{2,0},{3,1},{4,6},{5,7},{6,4},{7,5},{8,10},{9,11},{10,... | collective-permute-start | bytes 786440 | tf_op jit(solution)/shard_map/ppermute | solution.py:29
  69.5 21.5 %collective-permute-start.3 = (bf16[3,128,1024]{2,1,0:T(8,128)(2,1)S(1)}, bf16[3,128,1024]{2,1,0:T(8,128)(2,1)S(1)}, u32[]{:S(2)}, u32[]{:S(2)}) collective-permute-start(bf16[3,128,1024]{2,1,0:T(8,128)(2,1)S(1)} %pad_maximum_fusion.own_ref), channel_id=1, source_target_pairs={{0,31},{1,2},{2,1},{3,4},{4,3},{5,6},{6,5},{7,8},{8,7},{9,10},{10,... | collective-permute-start | bytes 2359304 | tf_op jit(solution)/shard_map/ppermute | solution.py:34
  71.4 19.6 %collective-permute-start.2 = (bf16[3,128,1024]{2,1,0:T(8,128)(2,1)S(1)}, bf16[3,128,1024]{2,1,0:T(8,128)(2,1)S(1)}, u32[]{:S(2)}, u32[]{:S(2)}) collective-permute-start(bf16[3,128,1024]{2,1,0:T(8,128)(2,1)S(1)} %pad_maximum_fusion.own_ref), channel_id=1, source_target_pairs={{0,1},{1,0},{2,3},{3,2},{4,5},{5,4},{6,7},{7,6},{8,9},{9,8},{10,11... | collective-permute-start | bytes 2359304 | tf_op jit(solution)/shard_map/ppermute | solution.py:29
  74.8 3.4 %copy-start.5 = (bf16[128,1024]{1,0:T(8,128)(2,1)}, bf16[128,1024]{1,0:T(8,128)(2,1)S(1)}, u32[]{:S(2)}) copy-start(bf16[128,1024]{1,0:T(8,128)(2,1)S(1)} %collective-permute-done.11) | copy-start | bytes 786436
  75.0 3.9 %collective-permute-start.12 = (bf16[256,1024]{1,0:T(8,128)(2,1)S(1)}, bf16[256,1024]{1,0:T(8,128)(2,1)}, u32[]{:S(2)}, u32[]{:S(2)}) collective-permute-start(bf16[256,1024]{1,0:T(8,128)(2,1)S(1)} %concatenate.96), channel_id=1, source_target_pairs={{0,1},{1,0},{2,3},{3,2},{4,5},{5,4},{6,7},{7,6},{8,9},{9,8},{10,11... | collective-permute-start | bytes 1572872 | tf_op jit(solution)/shard_map/ppermute | solution.py:29
  77.8 13.2 %copy-start.1 = (bf16[1,1,128,512]{3,2,1,0:T(8,128)(2,1)S(1)}, bf16[1,1,128,512]{3,2,1,0:T(8,128)(2,1)}, u32[]{:S(2)}) copy-start(bf16[1,1,128,512]{3,2,1,0:T(8,128)(2,1)} %param.7) | copy-start | bytes 393220
  91.0 0.9 copy-start.2
  101.8 3.8 %collective-permute-start.17 = (bf16[256,1024]{1,0:T(8,128)(2,1)S(1)}, bf16[256,1024]{1,0:T(8,128)(2,1)S(1)}, u32[]{:S(2)}, u32[]{:S(2)}) collective-permute-start(bf16[256,1024]{1,0:T(8,128)(2,1)S(1)} %get-tuple-element.16), channel_id=1, source_target_pairs={{0,1},{1,0},{2,3},{3,2},{4,5},{5,4},{6,7},{7,6},{8,9},{9,8},{10,11... | collective-permute-start | bytes 1572872 | tf_op jit(solution)/shard_map/ppermute | solution.py:29
  105.8 11.4 %collective-permute-start.18 = (bf16[128,1024]{1,0:T(8,128)(2,1)S(1)}, bf16[128,1024]{1,0:T(8,128)(2,1)S(1)}, u32[]{:S(2)}, u32[]{:S(2)}) collective-permute-start(bf16[128,1024]{1,0:T(8,128)(2,1)S(1)} %slice.149), channel_id=1, source_target_pairs={{0,2},{1,3},{2,0},{3,1},{4,6},{5,7},{6,4},{7,5},{8,10},{9,11},{10,... | collective-permute-start | bytes 786440 | tf_op jit(solution)/shard_map/ppermute | solution.py:29
  117.3 8.7 %collective-permute-start.19 = (bf16[64,1024]{1,0:T(8,128)(2,1)S(1)}, bf16[64,1024]{1,0:T(8,128)(2,1)S(1)}, u32[]{:S(2)}, u32[]{:S(2)}) collective-permute-start(bf16[64,1024]{1,0:T(8,128)(2,1)S(1)} %slice.150), channel_id=1, source_target_pairs={{0,8},{1,9},{2,10},{3,11},{4,12},{5,13},{6,14},{7,15},{8,0},{9,1},... | collective-permute-start | bytes 393224 | tf_op jit(solution)/shard_map/ppermute | solution.py:29
  120.3 33.7 %collective-permute-start.13 = (bf16[3,128,1024]{2,1,0:T(8,128)(2,1)S(1)}, bf16[3,128,1024]{2,1,0:T(8,128)(2,1)S(1)}, u32[]{:S(2)}, u32[]{:S(2)}) collective-permute-start(bf16[3,128,1024]{2,1,0:T(8,128)(2,1)S(1)} %get-tuple-element.13), channel_id=1, source_target_pairs={{0,1},{1,0},{2,3},{3,2},{4,5},{5,4},{6,7},{7,6},{8,9},{9,8},{10,11... | collective-permute-start | bytes 2359304 | tf_op jit(solution)/shard_map/ppermute | solution.py:29
  122.3 31.8 %collective-permute-start.14 = (bf16[3,128,1024]{2,1,0:T(8,128)(2,1)S(1)}, bf16[3,128,1024]{2,1,0:T(8,128)(2,1)S(1)}, u32[]{:S(2)}, u32[]{:S(2)}) collective-permute-start(bf16[3,128,1024]{2,1,0:T(8,128)(2,1)S(1)} %get-tuple-element.14), channel_id=1, source_target_pairs={{0,31},{1,2},{2,1},{3,4},{4,3},{5,6},{6,5},{7,8},{8,7},{9,10},{10,... | collective-permute-start | bytes 2359304 | tf_op jit(solution)/shard_map/ppermute | solution.py:34
  126.1 6.9 %collective-permute-start.20 = (f32[32,1024]{1,0:T(8,128)S(1)}, f32[32,1024]{1,0:T(8,128)S(1)}, u32[]{:S(2)}, u32[]{:S(2)}) collective-permute-start(f32[32,1024]{1,0:T(8,128)S(1)} %slice.111), channel_id=1, source_target_pairs={{0,64},{32,96},{64,0},{96,32},{128,192},{160,224},{192,128},{224,1... | collective-permute-start | bytes 393224 | tf_op jit(solution)/shard_map/ppermute | solution.py:29
  133.0 12.4 %collective-permute-start.21 = (f32[16,1024]{1,0:T(8,128)S(1)}, f32[16,1024]{1,0:T(8,128)S(1)}, u32[]{:S(2)}, u32[]{:S(2)}) collective-permute-start(f32[16,1024]{1,0:T(8,128)S(1)} %slice.113), channel_id=1, source_target_pairs={{0,4},{1,5},{2,6},{3,7},{4,0},{5,1},{6,2},{7,3},{8,12},{9,13},{10,... | collective-permute-start | bytes 196616 | tf_op jit(solution)/shard_map/ppermute | solution.py:29
  145.4 10.5 %collective-permute-start.22 = (f32[8,1024]{1,0:T(8,128)S(1)}, f32[8,1024]{1,0:T(8,128)S(1)}, u32[]{:S(2)}, u32[]{:S(2)}) collective-permute-start(f32[8,1024]{1,0:T(8,128)S(1)} %slice.115), channel_id=1, source_target_pairs={{0,32},{32,0},{64,96},{96,64},{128,160},{160,128},{192,224},{224,1... | collective-permute-start | bytes 98312 | tf_op jit(solution)/shard_map/ppermute | solution.py:29
  155.9 8.8 %collective-permute-start.23 = (f32[4,1024]{1,0:T(4,128)S(1)}, f32[4,1024]{1,0:T(4,128)S(1)}, u32[]{:S(2)}, u32[]{:S(2)}) collective-permute-start(f32[4,1024]{1,0:T(4,128)S(1)} %slice.117), channel_id=1, source_target_pairs={{0,16},{1,17},{2,18},{3,19},{4,20},{5,21},{6,22},{7,23},{8,24},{9,... | collective-permute-start | bytes 49160 | tf_op jit(solution)/shard_map/ppermute | solution.py:29
  157.9 18.3 %collective-permute-start.15 = (bf16[128,1024]{1,0:T(8,128)(2,1)S(1)}, bf16[128,1024]{1,0:T(8,128)(2,1)S(1)}, u32[]{:S(2)}, u32[]{:S(2)}) collective-permute-start(bf16[128,1024]{1,0:T(8,128)(2,1)S(1)} %fusion.4), channel_id=1, source_target_pairs={{0,448},{32,96},{64,0},{96,160},{128,64},{160,224},{192,128},{224,... | collective-permute-start | bytes 786440 | tf_op jit(solution)/shard_map/ppermute | solution.py:39
  164.8 6.4 %collective-permute-start.24 = (f32[2,1024]{1,0:T(2,128)S(1)}, f32[2,1024]{1,0:T(2,128)S(1)}, u32[]{:S(2)}, u32[]{:S(2)}) collective-permute-start(f32[2,1024]{1,0:T(2,128)S(1)} %slice.119), channel_id=1, source_target_pairs={{0,128},{32,160},{64,192},{96,224},{128,0},{160,32},{192,64},{224,... | collective-permute-start | bytes 24584 | tf_op jit(solution)/shard_map/ppermute | solution.py:29
  171.2 9.4 %collective-permute-start.25 = (f32[1,1024]{1,0:T(1,128)S(1)}, f32[1,1024]{1,0:T(1,128)S(1)}, u32[]{:S(2)}, u32[]{:S(2)}) collective-permute-start(f32[1,1024]{1,0:T(1,128)S(1)} %slice.121), channel_id=1, source_target_pairs={{0,256},{32,288},{64,320},{96,352},{128,384},{160,416},{192,448},{... | collective-permute-start | bytes 12296 | tf_op jit(solution)/shard_map/ppermute | solution.py:29
  176.3 18.9 %collective-permute-start.16 = (bf16[128,1024]{1,0:T(8,128)(2,1)S(1)}, bf16[128,1024]{1,0:T(8,128)(2,1)S(1)}, u32[]{:S(2)}, u32[]{:S(2)}) collective-permute-start(bf16[128,1024]{1,0:T(8,128)(2,1)S(1)} %fusion.1), channel_id=1, source_target_pairs={{0,32},{32,0},{64,96},{96,64},{128,160},{160,128},{192,224},{224,1... | collective-permute-start | bytes 786440 | tf_op jit(solution)/shard_map/ppermute | solution.py:29

commit v2 on v1

--- a/solution.py
+++ b/solution.py
@@ -1,5 +1,3 @@
-import functools
-
 import jax
 import jax.numpy as jnp
 from jax import lax
@@ -12,19 +10,6 @@
 SCALE = HEAD_DIM ** (-0.5)
 NEGATIVE = -1e30
 
-GATHER_ORDER = (
-    ("row", 8),
-    ("row", 4),
-    ("col", 16),
-    ("row", 1),
-    ("col", 4),
-    ("row", 2),
-    ("col", 8),
-    ("col", 2),
-    ("col", 1),
-)
-
-
 def exchange(block, axis, bit):
     return lax.ppermute(block, axis, [(i, i ^ bit) for i in range(lax.axis_size(axis))])
 
@@ -39,52 +24,55 @@
     return lax.ppermute(block, "row", [(i, (i + (-way if i % 2 else way)) % size) for i in range(size)])
 
 
-def gather_steps():
-    return [(axis, bit) for axis, bit in GATHER_ORDER if bit < lax.axis_size(axis)]
+def same_core():
+    size = lax.axis_size("col")
+    return [list(range(core, size, 2)) for core in range(2)]
+
+
+def deal(block, axis, groups=None):
+    return lax.all_to_all(block, axis, 0, 0, axis_index_groups=groups, tiled=True)
 
 
 def gather_coarse(own):
     width = own.shape[-1]
-    block = own.reshape(1, 8, width // 8)
-    for axis, bit in gather_steps():
-        block = jnp.concatenate([block, exchange(block, axis, bit)], axis=0)
-        if block.ndim == 3 and block.shape[0] == 16:
-            block = block.reshape(16, width)
-    return block
-
-
-def scatter_coarse(lower, upper):
-    steps = gather_steps()[::-1]
-    for number, (axis, bit) in enumerate(steps):
-        lower = lower + exchange(upper, axis, bit).astype(jnp.float32)
-        if number + 1 < len(steps):
-            half = lower.shape[0] // 2
-            lower, upper = lower[:half], lower[half:]
-            if half >= 64:
-                upper = upper.astype(jnp.bfloat16)
-    return lower
+    lines = lax.axis_size("row")
+    members = lax.axis_size("col") // 2
+    block = jnp.broadcast_to(own.reshape(1, 8, width // 8), (lines, 8, width // 8))
+    block = deal(block, "row").reshape(1, lines, width)
+    block = deal(jnp.broadcast_to(block, (members, lines, width)), "col", same_core())
+    return block.reshape(members * lines, width)
+
+
+def scatter_coarse(kept, other):
+    width = kept.shape[-1]
+    lines = lax.axis_size("row")
+    members = lax.axis_size("col") // 2
+    block = (kept + exchange(other, "col", 1).astype(jnp.float32)).astype(jnp.bfloat16)
+    block = deal(block.reshape(members, lines, width), "col", same_core()).astype(jnp.float32).sum(axis=0)
+    block = deal(block.reshape(lines, 8, width // 8), "row").sum(axis=0)
+    return block.reshape(1, width)
 
 
 def attention_kernel(
-    counts, q_ref, g_ref, own_ref, near_ref, far_ref, coarse_ref,
-    dq_ref, own_out, near_out, far_out, low_out, high_out, p_ref, dp_ref,
+    counts, q_ref, g_ref, own_ref, near_ref, far_ref, kept_ref, other_ref,
+    dq_ref, own_out, near_out, far_out, kept_out, other_out, p_ref, dp_ref,
 ):
     rows, width = q_ref.shape
-    coarse_count = coarse_ref.shape[0]
-    half = coarse_count // 2
-    step = min(rows, half)
+    coarse_count = kept_ref.shape[0]
+    step = min(rows, coarse_count)
     tiles = []
     for column, (ref, out) in enumerate(((own_ref, own_out), (near_ref, near_out), (far_ref, far_out))):
         for line in range(3):
-            tiles.append((ref.at[line], out.at[line], 0, rows, counts[column * 3 + line]))
-    for start in range(0, coarse_count, step):
-        out = (low_out, start) if start < half else (high_out, start - half)
-        tiles.append((coarse_ref.at[start : start + step], out[0].at[out[1] : out[1] + step], 0, step, None))
+            tiles.append((ref.at[line], out.at[line], rows, counts[column * 3 + line]))
+    for ref, out in ((kept_ref, kept_out), (other_ref, other_out)):
+        for start in range(0, coarse_count, step):
+            span = slice(start, start + step)
+            tiles.append((ref.at[span], out.at[span], step, None))
     starts = []
     total = 0
     for tile in tiles:
         starts.append(total)
-        total += tile[3]
+        total += tile[2]
     contract_last = (((1,), (1,)), ((), ()))
     contract_first = (((0,), (0,)), ((), ()))
     f32 = jnp.float32
@@ -105,7 +93,7 @@
         query = stacked(q_ref[:, at_k] * jnp.asarray(SCALE, q_ref.dtype))
         upstream = stacked(g_ref[:, at_k])
         peak = jnp.full((1, 2 * rows), NEGATIVE, f32)
-        for (ref, _, _, size, count), start in zip(tiles, starts):
+        for (ref, _, size, count), start in zip(tiles, starts):
             scores = lax.dot_general(ref[:, at_k], query, contract_last, preferred_element_type=f32)
             if count is not None:
                 live = lax.broadcasted_iota(jnp.int32, scores.shape, 0) < count
@@ -113,13 +101,13 @@
             p_ref[start : start + size, :] = scores
             peak = jnp.maximum(peak, jnp.max(scores, axis=0, keepdims=True))
         norm = jnp.zeros((1, 2 * rows), f32)
-        for (_, _, _, size, _), start in zip(tiles, starts):
+        for (_, _, size, _), start in zip(tiles, starts):
             weights = jnp.exp(p_ref[start : start + size, :] - peak)
             p_ref[start : start + size, :] = weights
             norm = norm + jnp.sum(weights, axis=0, keepdims=True)
         inverse = query_live / norm
         delta = jnp.zeros((1, 2 * rows), f32)
-        for (ref, out, _, size, _), start in zip(tiles, starts):
+        for (ref, out, size, _), start in zip(tiles, starts):
             probs = p_ref[start : start + size, :] * inverse
             probs_low = probs.astype(jnp.bfloat16)
             p_ref[start : start + size, :] = probs
@@ -129,7 +117,7 @@
             value_terms = jnp.dot(probs_low, upstream, preferred_element_type=f32)
             out[:, at_v] = value_terms.astype(out.dtype)
         grad_query = jnp.zeros((LANES, 2 * rows), f32)
-        for (ref, out, _, size, _), start in zip(tiles, starts):
+        for (ref, out, size, _), start in zip(tiles, starts):
             span = slice(start, start + size)
             grad_low = (p_ref[span, :] * (dp_ref[span, :] - delta)).astype(jnp.bfloat16)
             key_terms = jnp.dot(grad_low, query, preferred_element_type=f32)
@@ -144,11 +132,11 @@
     lax.fori_loop(0, width // LANES, pair, 0)
 
 
-def attention(counts, query, upstream, own, near, far, coarse):
+def attention(counts, query, upstream, own, near, far, kept, other):
     rows, width = query.shape
     double = 2 * width
-    coarse_count = coarse.shape[0]
-    keys = 9 * rows + coarse_count
+    coarse_count = kept.shape[0]
+    keys = 9 * rows + 2 * coarse_count
     in_vmem = pl.BlockSpec(memory_space=pltpu.VMEM)
     work = 2 * rows * keys * width
     return pl.pallas_call(
@@ -158,10 +146,10 @@
             jax.ShapeDtypeStruct((3, rows, double), jnp.float32),
             jax.ShapeDtypeStruct((3, rows, double), jnp.bfloat16),
             jax.ShapeDtypeStruct((3, rows, double), jnp.bfloat16),
-            jax.ShapeDtypeStruct((coarse_count // 2, double), jnp.float32),
-            jax.ShapeDtypeStruct((coarse_count // 2, double), jnp.bfloat16),
-        ),
-        in_specs=[pl.BlockSpec(memory_space=pltpu.SMEM)] + [in_vmem] * 6,
+            jax.ShapeDtypeStruct((coarse_count, double), jnp.float32),
+            jax.ShapeDtypeStruct((coarse_count, double), jnp.bfloat16),
+        ),
+        in_specs=[pl.BlockSpec(memory_space=pltpu.SMEM)] + [in_vmem] * 7,
         out_specs=(in_vmem,) * 6,
         scratch_shapes=[
             pltpu.VMEM((keys, 2 * rows), jnp.float32),
@@ -171,7 +159,7 @@
         cost_estimate=pl.CostEstimate(
             flops=5 * work, bytes_accessed=12 * 2**20, transcendentals=rows * keys * width // HEAD_DIM
         ),
-    )(counts, query, upstream, own, near, far, coarse)
+    )(counts, query, upstream, own, near, far, kept, other)
 
 
 def neighbour_counts(tile_counts):
@@ -196,15 +184,16 @@
     counts = neighbour_counts(tile_counts)
     fine = jnp.concatenate([fine_keys[0, 0], fine_values[0, 0]], axis=-1)
     paired = exchange(fine, "row", 1)
-    coarse = gather_coarse(jnp.concatenate([coarse_keys, coarse_values], axis=-1))
+    kept = gather_coarse(jnp.concatenate([coarse_keys, coarse_values], axis=-1))
     far = skip_row(paired, 2)
     own_column = jnp.stack([fine, paired, far])
     near_column = exchange(own_column, "col", 1)
     far_column = to_far(own_column, "col")
-    grad_q, own_terms, near_terms, far_terms, coarse_low, coarse_high = attention(
-        counts, fine_queries[0, 0], grad_out[0, 0], own_column, near_column, far_column, coarse
-    )
-    coarse_sum = scatter_coarse(coarse_low, coarse_high)
+    other = exchange(kept, "col", 1)
+    grad_q, own_terms, near_terms, far_terms, kept_terms, other_terms = attention(
+        counts, fine_queries[0, 0], grad_out[0, 0], own_column, near_column, far_column, kept, other
+    )
+    coarse_sum = scatter_coarse(kept_terms, other_terms)
     line = (
         own_terms
         + exchange(near_terms, "col", 1).astype(jnp.float32)

time: 197 us -> 167 us (0.85)
  the two profiles are of different devices: /device:TPU:10 before, /device:TPU:1 now
where the time goes in v2:
time: 167 us
  starting transfers between devices  75.9 us (45%)
  waiting for transfers between devices  67.9 us (41%)
  Pallas kernels  9.95 us (6%)
  other arithmetic  6.61 us (4%)
  local copies, waits for them, and re-layouts  5.34 us (3%)
    all_to_all x4, starting transfers between devices, deal(): lax.all_to_all(block, axis, 0, 0, axis_index_groups=groups, tiled=True)  36 us
    ppermute x2, waiting for transfers between devices, to_far(): lax.ppermute(block, axis, [(i, (i + (1 if i % 2 else -1)) % size) for i i...  26.5 us
    ppermute x6, starting transfers between devices, exchange(): lax.ppermute(block, axis, [(i, i ^ bit) for i in range(lax.axis_size(axis...  23.1 us
    all_to_all x4, waiting for transfers between devices, deal(): lax.all_to_all(block, axis, 0, 0, axis_index_groups=groups, tiled=True)  22.3 us
    ppermute x6, waiting for transfers between devices, exchange(): lax.ppermute(block, axis, [(i, i ^ bit) for i in range(lax.axis_size(axis...  13.2 us
    ppermute x2, starting transfers between devices, to_far(): lax.ppermute(block, axis, [(i, (i + (1 if i % 2 else -1)) % size) for i i...  12.1 us
    pallas_call x1, Pallas kernels, attention(): pl.pallas_call(attention_kernel, out_shape=(jax.ShapeDtypeStruct((rows, w...  9.95 us
    ppermute x2, waiting for transfers between devices, skip_row(): lax.ppermute(block, 'row', [(i, (i + (-way if i % 2 else way)) % size) fo...  5.81 us
  transfers between devices with their start and end apart: 14, of which 7 were waited for; matrix products, arithmetic and copies ran while one was open for 5% of the time, Pallas kernels for 0%

profile of v2, /device:TPU:1, one launch (start us, length us, event | category | flops | bytes accessed | tf_op | source)
XLA Modules:
  0.0 166.5 jit_solution(9503097108392323577)
XLA Ops:
  0.6 0.0 copy-start
  0.6 0.7 maximum_reduce_fusion
  1.4 0.6 broadcast_in_dim.45
  2.0 16.2 %all-to-all-start = ((bf16[16,8,128]{2,1,0:T(8,128)(2,1)}), bf16[16,8,128]{2,1,0:T(8,128)(2,1)S(1)}, u32[]{:S(2)}, u32[]{:S(2)}) async-start(bf16[16,8,128]{2,1,0:T(8,128)(2,1)} %broadcast_in_dim.45), calls=%async_computation | async-start | bytes 65536 | tf_op jit(solution)/shard_map/all_to_all | solution.py:33
  18.2 1.0 fusion.9
  19.3 7.2 %collective-permute-start = (bf16[128,1024]{1,0:T(8,128)(2,1)S(1)}, bf16[128,1024]{1,0:T(8,128)(2,1)S(1)}, u32[]{:S(2)}, u32[]{:S(2)}) collective-permute-start(bf16[128,1024]{1,0:T(8,128)(2,1)S(1)} %get-tuple-element.24), channel_id=1, source_target_pairs={{0,32},{32,0},{64,96},{96,64},{128,160},{160,128},{192,224},{224,1... | collective-permute-start | bytes 786440 | tf_op jit(solution)/shard_map/ppermute | solution.py:14
  26.4 3.2 %all-to-all-done = bf16[16,8,128]{2,1,0:T(8,128)(2,1)S(1)} async-done(((bf16[16,8,128]{2,1,0:T(8,128)(2,1)}), bf16[16,8,128]{2,1,0:T(8,128)(2,1)S(1)}, u32[]{:S(2)}, u32[]{:S(2)}) %all-to-all-start) | async-done | bytes 32800 | tf_op jit(solution)/shard_map/all_to_all | solution.py:33
  29.6 0.9 broadcast_in_dim.47
  30.5 4.4 %all-to-all-start.1 = ((bf16[16,16,1024]{2,1,0:T(8,128)(2,1)}), bf16[16,16,1024]{2,1,0:T(8,128)(2,1)S(1)}, u32[]{:S(2)}, u32[]{:S(2)}) async-start(bf16[16,16,1024]{2,1,0:T(8,128)(2,1)} %broadcast_in_dim.47), calls=%async_computation.1 | async-start | bytes 1048576 | tf_op jit(solution)/shard_map/all_to_all | solution.py:33
  35.0 0.0 collective-permute-done
  35.0 2.2 %collective-permute-start.1 = (bf16[128,1024]{1,0:T(8,128)(2,1)S(1)}, bf16[128,1024]{1,0:T(8,128)(2,1)S(1)}, u32[]{:S(2)}, u32[]{:S(2)}) collective-permute-start(bf16[128,1024]{1,0:T(8,128)(2,1)S(1)} %collective-permute-done), channel_id=1, source_target_pairs={{0,64},{32,480},{64,128},{96,32},{128,192},{160,96},{192,256},{224... | collective-permute-start | bytes 786440 | tf_op jit(solution)/shard_map/ppermute | solution.py:24
  37.2 0.6 compare_and_fusion.1
  37.8 5.8 %collective-permute-done.1 = bf16[128,1024]{1,0:T(8,128)(2,1)S(1)} collective-permute-done((bf16[128,1024]{1,0:T(8,128)(2,1)S(1)}, bf16[128,1024]{1,0:T(8,128)(2,1)S(1)}, u32[]{:S(2)}, u32[]{:S(2)}) %collective-permute-start.1) | collective-permute-done | bytes 262176 | tf_op jit(solution)/shard_map/ppermute | solution.py:24
  43.6 0.0 copy-start.1
  43.6 0.1 pad_maximum_fusion.own_ref
  43.7 10.1 %collective-permute-start.3 = (bf16[3,128,1024]{2,1,0:T(8,128)(2,1)S(1)}, bf16[3,128,1024]{2,1,0:T(8,128)(2,1)S(1)}, u32[]{:S(2)}, u32[]{:S(2)}) collective-permute-start(bf16[3,128,1024]{2,1,0:T(8,128)(2,1)S(1)} %pad_maximum_fusion.own_ref), channel_id=1, source_target_pairs={{0,31},{1,2},{2,1},{3,4},{4,3},{5,6},{6,5},{7,8},{8,7},{9,10},{10,... | collective-permute-start | bytes 2359304 | tf_op jit(solution)/shard_map/ppermute | solution.py:19
  53.8 1.9 %collective-permute-start.2 = (bf16[3,128,1024]{2,1,0:T(8,128)(2,1)S(1)}, bf16[3,128,1024]{2,1,0:T(8,128)(2,1)S(1)}, u32[]{:S(2)}, u32[]{:S(2)}) collective-permute-start(bf16[3,128,1024]{2,1,0:T(8,128)(2,1)S(1)} %pad_maximum_fusion.own_ref), channel_id=1, source_target_pairs={{0,1},{1,0},{2,3},{3,2},{4,5},{5,4},{6,7},{7,6},{8,9},{9,8},{10,11... | collective-permute-start | bytes 2359304 | tf_op jit(solution)/shard_map/ppermute | solution.py:14
  55.8 0.6 compare_and_fusion
  56.4 0.5 fusion.6
  56.9 0.0 all-to-all-done.1
  56.9 2.4 %collective-permute-start.4 = (bf16[256,1024]{1,0:T(8,128)(2,1)S(1)}, bf16[256,1024]{1,0:T(8,128)(2,1)S(1)}, u32[]{:S(2)}, u32[]{:S(2)}) collective-permute-start(bf16[256,1024]{1,0:T(8,128)(2,1)S(1)} %bitcast.46), channel_id=1, source_target_pairs={{0,1},{1,0},{2,3},{3,2},{4,5},{5,4},{6,7},{7,6},{8,9},{9,8},{10,11... | collective-permute-start | bytes 1572872 | tf_op jit(solution)/shard_map/ppermute | solution.py:14
  59.3 0.7 broadcast_or_fusion
  60.0 0.1 reshape.183
  60.1 0.0 copy-done
  60.1 0.7 gather_fusion
  60.8 0.1 reshape.186
  60.9 0.7 and_select_fusion
  61.6 0.1 select_n.39
  61.7 0.1 pad_add_fusion.2.counts
  61.8 9.9 %collective-permute-done.3.far_ref = bf16[3,128,1024]{2,1,0:T(8,128)(2,1)S(1)} collective-permute-done((bf16[3,128,1024]{2,1,0:T(8,128)(2,1)S(1)}, bf16[3,128,1024]{2,1,0:T(8,128)(2,1)S(1)}, u32[]{:S(2)}, u32[]{:S(2)}) %collective-permute-start.3) | collective-permute-done | bytes 786464 | tf_op jit(solution)/shard_map/ppermute | solution.py:19
  71.8 0.0 collective-permute-done.2.near_ref
  71.8 0.0 collective-permute-done.4.other_ref
  71.8 0.0 copy-done.1
  71.8 0.0 copy-start.2
  71.8 0.9 copy-done.2
  72.7 9.9 %shard_map.110 = (bf16[128,512]{1,0:T(8,128)(2,1)}, f32[3,128,1024]{2,1,0:T(8,128)S(1)}, bf16[3,128,1024]{2,1,0:T(8,128)(2,1)S(1)}, bf16[3,128,1024]{2,1,0:T(8,1...) custom-call(s32[10]{0:T(128)S(1)} %pad_add_fusion.2.counts, bf16[128,512]{1,0:T(8,128)(2,1)S(1)} %bitcast.48, ...), custom_call_target="tpu_custom_call" | custom-call | flops 1090519040 | bytes 12582912 | tf_op jit(solution)/shard_map/pallas_call | solution.py:142
  82.6 2.3 %collective-permute-start.5 = (bf16[3,128,1024]{2,1,0:T(8,128)(2,1)S(1)}, bf16[3,128,1024]{2,1,0:T(8,128)(2,1)S(1)}, u32[]{:S(2)}, u32[]{:S(2)}) collective-permute-start(bf16[3,128,1024]{2,1,0:T(8,128)(2,1)S(1)} %get-tuple-element.13), channel_id=1, source_target_pairs={{0,1},{1,0},{2,3},{3,2},{4,5},{5,4},{6,7},{7,6},{8,9},{9,8},{10,11... | collective-permute-start | bytes 2359304 | tf_op jit(solution)/shard_map/ppermute | solution.py:14
  84.9 1.9 %collective-permute-start.6 = (bf16[3,128,1024]{2,1,0:T(8,128)(2,1)S(1)}, bf16[3,128,1024]{2,1,0:T(8,128)(2,1)S(1)}, u32[]{:S(2)}, u32[]{:S(2)}) collective-permute-start(bf16[3,128,1024]{2,1,0:T(8,128)(2,1)S(1)} %get-tuple-element.14), channel_id=1, source_target_pairs={{0,31},{1,2},{2,1},{3,4},{4,3},{5,6},{6,5},{7,8},{8,7},{9,10},{10,... | collective-permute-start | bytes 2359304 | tf_op jit(solution)/shard_map/ppermute | solution.py:19
  86.9 3.5 %collective-permute-start.9 = (bf16[256,1024]{1,0:T(8,128)(2,1)S(1)}, bf16[256,1024]{1,0:T(8,128)(2,1)S(1)}, u32[]{:S(2)}, u32[]{:S(2)}) collective-permute-start(bf16[256,1024]{1,0:T(8,128)(2,1)S(1)} %get-tuple-element.16), channel_id=1, source_target_pairs={{0,1},{1,0},{2,3},{3,2},{4,5},{5,4},{6,7},{7,6},{8,9},{9,8},{10,11... | collective-permute-start | bytes 1572872 | tf_op jit(solution)/shard_map/ppermute | solution.py:14
  90.3 0.0 collective-permute-done.5
  90.4 16.6 %collective-permute-done.6 = bf16[3,128,1024]{2,1,0:T(8,128)(2,1)S(1)} collective-permute-done((bf16[3,128,1024]{2,1,0:T(8,128)(2,1)S(1)}, bf16[3,128,1024]{2,1,0:T(8,128)(2,1)S(1)}, u32[]{:S(2)}, u32[]{:S(2)}) %collective-permute-start.6) | collective-permute-done | bytes 786464 | tf_op jit(solution)/shard_map/ppermute | solution.py:19
  107.0 0.3 convert_add_fusion
  107.3 2.5 %collective-permute-start.7 = (bf16[128,1024]{1,0:T(8,128)(2,1)S(1)}, bf16[128,1024]{1,0:T(8,128)(2,1)S(1)}, u32[]{:S(2)}, u32[]{:S(2)}) collective-permute-start(bf16[128,1024]{1,0:T(8,128)(2,1)S(1)} %fusion.4), channel_id=1, source_target_pairs={{0,448},{32,96},{64,0},{96,160},{128,64},{160,224},{192,128},{224,... | collective-permute-start | bytes 786440 | tf_op jit(solution)/shard_map/ppermute | solution.py:24
  109.9 0.0 collective-permute-done.9
  109.9 1.0 add_convert_fusion
  110.8 5.9 %all-to-all-start.2 = ((bf16[16,16,1024]{2,1,0:T(8,128)(2,1)}), bf16[16,16,1024]{2,1,0:T(8,128)(2,1)S(1)}, u32[]{:S(2)}, u32[]{:S(2)}) async-start(bf16[16,16,1024]{2,1,0:T(8,128)(2,1)} %bitcast.20), calls=%async_computation.2 | async-start | bytes 1048576 | tf_op jit(solution)/shard_map/all_to_all | solution.py:33
  116.7 0.0 collective-permute-done.7
  116.8 0.1 fusion.1
  116.8 5.8 %collective-permute-start.8 = (bf16[128,1024]{1,0:T(8,128)(2,1)S(1)}, bf16[128,1024]{1,0:T(8,128)(2,1)S(1)}, u32[]{:S(2)}, u32[]{:S(2)}) collective-permute-start(bf16[128,1024]{1,0:T(8,128)(2,1)S(1)} %fusion.1), channel_id=1, source_target_pairs={{0,32},{32,0},{64,96},{96,64},{128,160},{160,128},{192,224},{224,1... | collective-permute-start | bytes 786440 | tf_op jit(solution)/shard_map/ppermute | solution.py:14
  122.6 13.2 %collective-permute-done.8 = bf16[128,1024]{1,0:T(8,128)(2,1)S(1)} collective-permute-done((bf16[128,1024]{1,0:T(8,128)(2,1)S(1)}, bf16[128,1024]{1,0:T(8,128)(2,1)S(1)}, u32[]{:S(2)}, u32[]{:S(2)}) %collective-permute-start.8) | collective-permute-done | bytes 262176 | tf_op jit(solution)/shard_map/ppermute | solution.py:14
  135.8 0.1 fusion.3
  135.9 8.3 %all-to-all-done.2 = bf16[16,16,1024]{2,1,0:T(8,128)(2,1)S(1)} async-done(((bf16[16,16,1024]{2,1,0:T(8,128)(2,1)}), bf16[16,16,1024]{2,1,0:T(8,128)(2,1)S(1)}, u32[]{:S(2)}, u32[]{:S(2)}) %all-to-all-start.2) | async-done | bytes 524320 | tf_op jit(solution)/shard_map/all_to_all | solution.py:33
  144.2 0.1 convert_reduce_fusion
  144.3 0.6 copy.13
  144.9 9.5 %all-to-all-start.3 = ((f32[16,8,128]{2,1,0:T(8,128)}), f32[16,8,128]{2,1,0:T(8,128)S(1)}, u32[]{:S(2)}, u32[]{:S(2)}) async-start(f32[16,8,128]{2,1,0:T(8,128)} %bitcast.27), calls=%async_computation.3 | async-start | bytes 131072 | tf_op jit(solution)/shard_map/all_to_all | solution.py:33
  154.4 0.7 slice_bitcast_fusion.2
  155.1 10.8 %all-to-all-done.3 = f32[16,8,128]{2,1,0:T(8,128)S(1)} async-done(((f32[16,8,128]{2,1,0:T(8,128)}), f32[16,8,128]{2,1,0:T(8,128)S(1)}, u32[]{:S(2)}, u32[]{:S(2)}) %all-to-all-start.3) | async-done | bytes 65568 | tf_op jit(solution)/shard_map/all_to_all | solution.py:33
  165.9 0.6 fusion.10
  (3 shorter events, 0.1 us)
Async XLA Ops:
  0.6 59.5 %copy-start = (s32[16,32]{1,0:T(8,128)S(1)}, s32[16,32]{1,0:T(8,128)}, u32[]{:S(2)}) copy-start(s32[16,32]{1,0:T(8,128)} %param.13) | copy-start | bytes 6148
  2.0 27.6 %all-to-all-start = ((bf16[16,8,128]{2,1,0:T(8,128)(2,1)}), bf16[16,8,128]{2,1,0:T(8,128)(2,1)S(1)}, u32[]{:S(2)}, u32[]{:S(2)}) async-start(bf16[16,8,128]{2,1,0:T(8,128)(2,1)} %broadcast_in_dim.45), calls=%async_computation | async-start | bytes 65536 | tf_op jit(solution)/shard_map/all_to_all | solution.py:33
  19.3 15.7 %collective-permute-start = (bf16[128,1024]{1,0:T(8,128)(2,1)S(1)}, bf16[128,1024]{1,0:T(8,128)(2,1)S(1)}, u32[]{:S(2)}, u32[]{:S(2)}) collective-permute-start(bf16[128,1024]{1,0:T(8,128)(2,1)S(1)} %get-tuple-element.24), channel_id=1, source_target_pairs={{0,32},{32,0},{64,96},{96,64},{128,160},{160,128},{192,224},{224,1... | collective-permute-start | bytes 786440 | tf_op jit(solution)/shard_map/ppermute | solution.py:14
  30.5 26.4 %all-to-all-start.1 = ((bf16[16,16,1024]{2,1,0:T(8,128)(2,1)}), bf16[16,16,1024]{2,1,0:T(8,128)(2,1)S(1)}, u32[]{:S(2)}, u32[]{:S(2)}) async-start(bf16[16,16,1024]{2,1,0:T(8,128)(2,1)} %broadcast_in_dim.47), calls=%async_computation.1 | async-start | bytes 1048576 | tf_op jit(solution)/shard_map/all_to_all | solution.py:33
  35.0 8.6 %collective-permute-start.1 = (bf16[128,1024]{1,0:T(8,128)(2,1)S(1)}, bf16[128,1024]{1,0:T(8,128)(2,1)S(1)}, u32[]{:S(2)}, u32[]{:S(2)}) collective-permute-start(bf16[128,1024]{1,0:T(8,128)(2,1)S(1)} %collective-permute-done), channel_id=1, source_target_pairs={{0,64},{32,480},{64,128},{96,32},{128,192},{160,96},{192,256},{224... | collective-permute-start | bytes 786440 | tf_op jit(solution)/shard_map/ppermute | solution.py:24
  43.6 28.2 %copy-start.1 = (bf16[1,1,128,512]{3,2,1,0:T(8,128)(2,1)S(1)}, bf16[1,1,128,512]{3,2,1,0:T(8,128)(2,1)}, u32[]{:S(2)}) copy-start(bf16[1,1,128,512]{3,2,1,0:T(8,128)(2,1)} %param.7) | copy-start | bytes 393220
  43.7 28.1 %collective-permute-start.3 = (bf16[3,128,1024]{2,1,0:T(8,128)(2,1)S(1)}, bf16[3,128,1024]{2,1,0:T(8,128)(2,1)S(1)}, u32[]{:S(2)}, u32[]{:S(2)}) collective-permute-start(bf16[3,128,1024]{2,1,0:T(8,128)(2,1)S(1)} %pad_maximum_fusion.own_ref), channel_id=1, source_target_pairs={{0,31},{1,2},{2,1},{3,4},{4,3},{5,6},{6,5},{7,8},{8,7},{9,10},{10,... | collective-permute-start | bytes 2359304 | tf_op jit(solution)/shard_map/ppermute | solution.py:19
  53.8 17.9 %collective-permute-start.2 = (bf16[3,128,1024]{2,1,0:T(8,128)(2,1)S(1)}, bf16[3,128,1024]{2,1,0:T(8,128)(2,1)S(1)}, u32[]{:S(2)}, u32[]{:S(2)}) collective-permute-start(bf16[3,128,1024]{2,1,0:T(8,128)(2,1)S(1)} %pad_maximum_fusion.own_ref), channel_id=1, source_target_pairs={{0,1},{1,0},{2,3},{3,2},{4,5},{5,4},{6,7},{7,6},{8,9},{9,8},{10,11... | collective-permute-start | bytes 2359304 | tf_op jit(solution)/shard_map/ppermute | solution.py:14
  56.9 14.9 %collective-permute-start.4 = (bf16[256,1024]{1,0:T(8,128)(2,1)S(1)}, bf16[256,1024]{1,0:T(8,128)(2,1)S(1)}, u32[]{:S(2)}, u32[]{:S(2)}) collective-permute-start(bf16[256,1024]{1,0:T(8,128)(2,1)S(1)} %bitcast.46), channel_id=1, source_target_pairs={{0,1},{1,0},{2,3},{3,2},{4,5},{5,4},{6,7},{7,6},{8,9},{9,8},{10,11... | collective-permute-start | bytes 1572872 | tf_op jit(solution)/shard_map/ppermute | solution.py:14
  71.8 0.9 copy-start.2
  82.6 7.7 %collective-permute-start.5 = (bf16[3,128,1024]{2,1,0:T(8,128)(2,1)S(1)}, bf16[3,128,1024]{2,1,0:T(8,128)(2,1)S(1)}, u32[]{:S(2)}, u32[]{:S(2)}) collective-permute-start(bf16[3,128,1024]{2,1,0:T(8,128)(2,1)S(1)} %get-tuple-element.13), channel_id=1, source_target_pairs={{0,1},{1,0},{2,3},{3,2},{4,5},{5,4},{6,7},{7,6},{8,9},{9,8},{10,11... | collective-permute-start | bytes 2359304 | tf_op jit(solution)/shard_map/ppermute | solution.py:14
  84.9 22.0 %collective-permute-start.6 = (bf16[3,128,1024]{2,1,0:T(8,128)(2,1)S(1)}, bf16[3,128,1024]{2,1,0:T(8,128)(2,1)S(1)}, u32[]{:S(2)}, u32[]{:S(2)}) collective-permute-start(bf16[3,128,1024]{2,1,0:T(8,128)(2,1)S(1)} %get-tuple-element.14), channel_id=1, source_target_pairs={{0,31},{1,2},{2,1},{3,4},{4,3},{5,6},{6,5},{7,8},{8,7},{9,10},{10,... | collective-permute-start | bytes 2359304 | tf_op jit(solution)/shard_map/ppermute | solution.py:19
  86.9 23.0 %collective-permute-start.9 = (bf16[256,1024]{1,0:T(8,128)(2,1)S(1)}, bf16[256,1024]{1,0:T(8,128)(2,1)S(1)}, u32[]{:S(2)}, u32[]{:S(2)}) collective-permute-start(bf16[256,1024]{1,0:T(8,128)(2,1)S(1)} %get-tuple-element.16), channel_id=1, source_target_pairs={{0,1},{1,0},{2,3},{3,2},{4,5},{5,4},{6,7},{7,6},{8,9},{9,8},{10,11... | collective-permute-start | bytes 1572872 | tf_op jit(solution)/shard_map/ppermute | solution.py:14
  107.3 9.4 %collective-permute-start.7 = (bf16[128,1024]{1,0:T(8,128)(2,1)S(1)}, bf16[128,1024]{1,0:T(8,128)(2,1)S(1)}, u32[]{:S(2)}, u32[]{:S(2)}) collective-permute-start(bf16[128,1024]{1,0:T(8,128)(2,1)S(1)} %fusion.4), channel_id=1, source_target_pairs={{0,448},{32,96},{64,0},{96,160},{128,64},{160,224},{192,128},{224,... | collective-permute-start | bytes 786440 | tf_op jit(solution)/shard_map/ppermute | solution.py:24
  110.8 33.3 %all-to-all-start.2 = ((bf16[16,16,1024]{2,1,0:T(8,128)(2,1)}), bf16[16,16,1024]{2,1,0:T(8,128)(2,1)S(1)}, u32[]{:S(2)}, u32[]{:S(2)}) async-start(bf16[16,16,1024]{2,1,0:T(8,128)(2,1)} %bitcast.20), calls=%async_computation.2 | async-start | bytes 1048576 | tf_op jit(solution)/shard_map/all_to_all | solution.py:33
  116.8 19.0 %collective-permute-start.8 = (bf16[128,1024]{1,0:T(8,128)(2,1)S(1)}, bf16[128,1024]{1,0:T(8,128)(2,1)S(1)}, u32[]{:S(2)}, u32[]{:S(2)}) collective-permute-start(bf16[128,1024]{1,0:T(8,128)(2,1)S(1)} %fusion.1), channel_id=1, source_target_pairs={{0,32},{32,0},{64,96},{96,64},{128,160},{160,128},{192,224},{224,1... | collective-permute-start | bytes 786440 | tf_op jit(solution)/shard_map/ppermute | solution.py:14
  144.9 21.0 %all-to-all-start.3 = ((f32[16,8,128]{2,1,0:T(8,128)}), f32[16,8,128]{2,1,0:T(8,128)S(1)}, u32[]{:S(2)}, u32[]{:S(2)}) async-start(f32[16,8,128]{2,1,0:T(8,128)} %bitcast.27), calls=%async_computation.3 | async-start | bytes 131072 | tf_op jit(solution)/shard_map/all_to_all | solution.py:33

commit v3 on v2

--- a/solution.py
+++ b/solution.py
@@ -24,50 +24,68 @@
     return lax.ppermute(block, "row", [(i, (i + (-way if i % 2 else way)) % size) for i in range(size)])
 
 
-def same_core():
-    size = lax.axis_size("col")
-    return [list(range(core, size, 2)) for core in range(2)]
-
-
-def deal(block, axis, groups=None):
-    return lax.all_to_all(block, axis, 0, 0, axis_index_groups=groups, tiled=True)
-
-
-def gather_coarse(own):
+def place_groups():
+    lines, columns = lax.axis_size("row"), lax.axis_size("col")
+    half = columns // 2
+    first = [
+        [(z + y_hi) * columns + x_hi + x_lo + y_lo + core for x_hi in (0, half) for y_hi in range(2) for y_lo in range(0, 8, 2)]
+        for z in range(0, lines, 2)
+        for x_lo in range(0, half, 8)
+        for core in range(2)
+    ]
+    second = [
+        [(z + y_hi) * columns + x_hi + x_lo + y_lo + core for x_lo in range(0, half, 8) for z in range(0, lines, 2)]
+        for x_hi in (0, half)
+        for y_hi in range(2)
+        for y_lo in range(0, 8, 2)
+        for core in range(2)
+    ]
+    return first, second
+
+
+def deal(block, groups):
+    return lax.all_to_all(block, ("row", "col"), 0, 0, axis_index_groups=groups, tiled=True)
+
+
+def gather_first(own):
     width = own.shape[-1]
-    lines = lax.axis_size("row")
-    members = lax.axis_size("col") // 2
-    block = jnp.broadcast_to(own.reshape(1, 8, width // 8), (lines, 8, width // 8))
-    block = deal(block, "row").reshape(1, lines, width)
-    block = deal(jnp.broadcast_to(block, (members, lines, width)), "col", same_core())
-    return block.reshape(members * lines, width)
-
-
-def scatter_coarse(kept, other):
-    width = kept.shape[-1]
-    lines = lax.axis_size("row")
-    members = lax.axis_size("col") // 2
-    block = (kept + exchange(other, "col", 1).astype(jnp.float32)).astype(jnp.bfloat16)
-    block = deal(block.reshape(members, lines, width), "col", same_core()).astype(jnp.float32).sum(axis=0)
-    block = deal(block.reshape(lines, 8, width // 8), "row").sum(axis=0)
+    groups, _ = place_groups()
+    members = len(groups[0])
+    block = jnp.broadcast_to(own.reshape(1, 8, width // 8), (members, 8, width // 8))
+    return deal(block, groups).reshape(members, width)
+
+
+def gather_second(block):
+    held, width = block.shape
+    _, groups = place_groups()
+    members = len(groups[0])
+    return deal(jnp.broadcast_to(block, (members, held, width)), groups).reshape(members * held, width)
+
+
+def scatter_coarse(block):
+    width = block.shape[-1]
+    first, second = place_groups()
+    held = len(first[0])
+    block = deal(block.reshape(len(second[0]), held, width), second).astype(jnp.float32).sum(axis=0)
+    block = deal(block.reshape(held, 8, width // 8), first).sum(axis=0)
     return block.reshape(1, width)
 
 
 def attention_kernel(
-    counts, q_ref, g_ref, own_ref, near_ref, far_ref, kept_ref, other_ref,
-    dq_ref, own_out, near_out, far_out, kept_out, other_out, p_ref, dp_ref,
+    counts, q_ref, g_ref, own_ref, pair_ref, skip_ref, near_own_ref, near_ref, far_own_ref, far_ref, kept_ref, other_ref,
+    dq_ref, own_out, core_out, far_own_out, far_out, kept_out, p_ref, dp_ref,
 ):
     rows, width = q_ref.shape
     coarse_count = kept_ref.shape[0]
     step = min(rows, coarse_count)
-    tiles = []
-    for column, (ref, out) in enumerate(((own_ref, own_out), (near_ref, near_out), (far_ref, far_out))):
-        for line in range(3):
-            tiles.append((ref.at[line], out.at[line], rows, counts[column * 3 + line]))
-    for ref, out in ((kept_ref, kept_out), (other_ref, other_out)):
+    fine_in = (own_ref, pair_ref, skip_ref, near_own_ref, near_ref.at[0], near_ref.at[1], far_own_ref, far_ref.at[0], far_ref.at[1])
+    fine_out = [own_out.at[at] for at in range(3)]
+    fine_out += [core_out.at[at * rows : (at + 1) * rows] for at in range(3)]
+    fine_out += [far_own_out, far_out.at[0], far_out.at[1]]
+    tiles = [(fine_in[at], fine_out[at], rows, counts[at]) for at in range(9)]
+    for ref, out, ahead in ((kept_ref, kept_out, 0), (other_ref, core_out, 3 * rows)):
         for start in range(0, coarse_count, step):
-            span = slice(start, start + step)
-            tiles.append((ref.at[span], out.at[span], step, None))
+            tiles.append((ref.at[start : start + step], out.at[ahead + start : ahead + start + step], step, None))
     starts = []
     total = 0
     for tile in tiles:
@@ -132,24 +150,25 @@
     lax.fori_loop(0, width // LANES, pair, 0)
 
 
-def attention(counts, query, upstream, own, near, far, kept, other):
+def attention(counts, query, upstream, *blocks):
     rows, width = query.shape
     double = 2 * width
-    coarse_count = kept.shape[0]
+    coarse_count = blocks[-1].shape[0]
     keys = 9 * rows + 2 * coarse_count
     in_vmem = pl.BlockSpec(memory_space=pltpu.VMEM)
     work = 2 * rows * keys * width
+    held, sent = jnp.float32, jnp.bfloat16
     return pl.pallas_call(
         attention_kernel,
         out_shape=(
             jax.ShapeDtypeStruct((rows, width), jnp.bfloat16),
-            jax.ShapeDtypeStruct((3, rows, double), jnp.float32),
-            jax.ShapeDtypeStruct((3, rows, double), jnp.bfloat16),
-            jax.ShapeDtypeStruct((3, rows, double), jnp.bfloat16),
-            jax.ShapeDtypeStruct((coarse_count, double), jnp.float32),
-            jax.ShapeDtypeStruct((coarse_count, double), jnp.bfloat16),
-        ),
-        in_specs=[pl.BlockSpec(memory_space=pltpu.SMEM)] + [in_vmem] * 7,
+            jax.ShapeDtypeStruct((3, rows, double), held),
+            jax.ShapeDtypeStruct((3 * rows + coarse_count, double), sent),
+            jax.ShapeDtypeStruct((rows, double), sent),
+            jax.ShapeDtypeStruct((2, rows, double), sent),
+            jax.ShapeDtypeStruct((coarse_count, double), held),
+        ),
+        in_specs=[pl.BlockSpec(memory_space=pltpu.SMEM)] + [in_vmem] * (2 + len(blocks)),
         out_specs=(in_vmem,) * 6,
         scratch_shapes=[
             pltpu.VMEM((keys, 2 * rows), jnp.float32),
@@ -159,7 +178,7 @@
         cost_estimate=pl.CostEstimate(
             flops=5 * work, bytes_accessed=12 * 2**20, transcendentals=rows * keys * width // HEAD_DIM
         ),
-    )(counts, query, upstream, own, near, far, kept, other)
+    )(counts, query, upstream, *blocks)
 
 
 def neighbour_counts(tile_counts):
@@ -182,27 +201,36 @@
 ):
     rows, width = fine_queries.shape[2:]
     counts = neighbour_counts(tile_counts)
-    fine = jnp.concatenate([fine_keys[0, 0], fine_values[0, 0]], axis=-1)
-    paired = exchange(fine, "row", 1)
-    kept = gather_coarse(jnp.concatenate([coarse_keys, coarse_values], axis=-1))
-    far = skip_row(paired, 2)
-    own_column = jnp.stack([fine, paired, far])
-    near_column = exchange(own_column, "col", 1)
-    far_column = to_far(own_column, "col")
+    low, high = jnp.bfloat16, jnp.float32
+    own = jnp.concatenate([fine_keys[0, 0], fine_values[0, 0]], axis=-1)
+    token = jnp.concatenate([coarse_keys, coarse_values], axis=-1)
+    paired = exchange(own, "row", 1)
+    token, paired = lax.optimization_barrier((token, paired))
+    coarse = gather_first(token)
+    skipped = skip_row(paired, 2)
+    near_own, far_own = exchange(own, "col", 1), to_far(own, "col")
+    coarse, skipped, far_own = lax.optimization_barrier((coarse, skipped, far_own))
+    kept = gather_second(coarse)
+    lines = jnp.stack([paired, skipped])
+    near, far = exchange(lines, "col", 1), to_far(lines, "col")
+    kept, far = lax.optimization_barrier((kept, far))
     other = exchange(kept, "col", 1)
-    grad_q, own_terms, near_terms, far_terms, kept_terms, other_terms = attention(
-        counts, fine_queries[0, 0], grad_out[0, 0], own_column, near_column, far_column, kept, other
+    grad_q, own_terms, core_terms, far_own_terms, far_terms, kept_terms = attention(
+        counts, fine_queries[0, 0], grad_out[0, 0], own, paired, skipped, near_own, near, far_own, far, kept, other
     )
-    coarse_sum = scatter_coarse(kept_terms, other_terms)
-    line = (
-        own_terms
-        + exchange(near_terms, "col", 1).astype(jnp.float32)
-        + to_far(far_terms, "col").astype(jnp.float32)
-    )
-    low = jnp.bfloat16
-    forwarded = skip_row(line[2].astype(low), -2).astype(jnp.float32)
-    returned = exchange((line[1] + forwarded).astype(low), "row", 1).astype(jnp.float32)
-    total = (line[0] + returned).astype(low)
+    rows = own.shape[0]
+    far_back = to_far(far_terms, "col")
+    core_back = exchange(core_terms, "col", 1).astype(high)
+    half = (kept_terms + core_back[3 * rows :]).astype(low)
+    half, far_own_terms = lax.optimization_barrier((half, far_own_terms))
+    line = own_terms + core_back[: 3 * rows].reshape(own_terms.shape)
+    skipped_line = (line[2] + far_back[1].astype(high)).astype(low)
+    skipped_line, far_own_terms = lax.optimization_barrier((skipped_line, far_own_terms))
+    coarse_sum = scatter_coarse(half)
+    forwarded = skip_row(skipped_line, -2).astype(high)
+    paired_line = (line[1] + far_back[0].astype(high) + forwarded).astype(low)
+    returned = exchange(paired_line, "row", 1).astype(high)
+    total = (line[0] + to_far(far_own_terms, "col").astype(high) + returned).astype(low)
     return (
         grad_q[None, None],
         total[None, None, :, :width],

time: 167 us -> 159 us (0.952)
  waiting for transfers between devices: 67.9 us -> 39.9 us
  blocking collectives: 0 us -> 25.8 us
  starting transfers between devices: 75.9 us -> 68.5 us
    all_to_all x0 -> x1, blocking collectives: none -> 25.8 us  [deal(): lax.all_to_all(block, ('row', 'col'), 0, 0, axis_index_groups=groups, til...]
    all_to_all x4 -> x3, starting transfers between devices: 36 us -> 21 us  [deal(): lax.all_to_all(block, ('row', 'col'), 0, 0, axis_index_groups=groups, til...]
    all_to_all x4 -> x3, waiting for transfers between devices: 22.3 us -> 8.16 us  [deal(): lax.all_to_all(block, ('row', 'col'), 0, 0, axis_index_groups=groups, til...]
    ppermute x2 -> x4, waiting for transfers between devices: 26.5 us -> 15.6 us  [to_far(): lax.ppermute(block, axis, [(i, (i + (1 if i % 2 else -1)) % size) for i i...]
    ppermute x2, waiting for transfers between devices: 5.81 us -> 0.01 us  [skip_row(): lax.ppermute(block, 'row', [(i, (i + (-way if i % 2 else way)) % size) fo...]
    ppermute x2 -> x4, starting transfers between devices: 12.1 us -> 17.3 us  [to_far(): lax.ppermute(block, axis, [(i, (i + (1 if i % 2 else -1)) % size) for i i...]
    ppermute x6, waiting for transfers between devices: 13.2 us -> 16.2 us  [exchange(): lax.ppermute(block, axis, [(i, i ^ bit) for i in range(lax.axis_size(axis...]
  transfers between devices with their start and end apart: 14 -> 15, of which waited for: 7 -> 6; matrix products, arithmetic and copies ran while one was open for 5% -> 5% of each run, Pallas kernels for 0% -> 0%
where the time goes in v3:
time: 159 us; the launch traced here: 158 us
  starting transfers between devices  68.5 us (43%)
  waiting for transfers between devices  39.9 us (25%)
  blocking collectives  25.8 us (16%)
  Pallas kernels  9.94 us (6%)
  other arithmetic  7.71 us (5%)
  local copies, waits for them, and re-layouts  4.84 us (3%)
    all_to_all x1, blocking collectives, deal(): lax.all_to_all(block, ('row', 'col'), 0, 0, axis_index_groups=groups, til...  25.8 us
    ppermute x6, starting transfers between devices, exchange(): lax.ppermute(block, axis, [(i, i ^ bit) for i in range(lax.axis_size(axis...  24.2 us
    all_to_all x3, starting transfers between devices, deal(): lax.all_to_all(block, ('row', 'col'), 0, 0, axis_index_groups=groups, til...  21 us
    ppermute x4, starting transfers between devices, to_far(): lax.ppermute(block, axis, [(i, (i + (1 if i % 2 else -1)) % size) for i i...  17.3 us
    ppermute x6, waiting for transfers between devices, exchange(): lax.ppermute(block, axis, [(i, i ^ bit) for i in range(lax.axis_size(axis...  16.2 us
    ppermute x4, waiting for transfers between devices, to_far(): lax.ppermute(block, axis, [(i, (i + (1 if i % 2 else -1)) % size) for i i...  15.6 us
    pallas_call x1, Pallas kernels, attention(): pl.pallas_call(attention_kernel, out_shape=(jax.ShapeDtypeStruct((rows, w...  9.94 us
    all_to_all x3, waiting for transfers between devices, deal(): lax.all_to_all(block, ('row', 'col'), 0, 0, axis_index_groups=groups, til...  8.16 us
  transfers between devices with their start and end apart: 15, of which 6 were waited for; matrix products, arithmetic and copies ran while one was open for 5% of the time, Pallas kernels for 0%

profile of v3, /device:TPU:1, one launch (start us, length us, event | category | flops | bytes accessed | tf_op | source)
XLA Modules:
  0.0 157.7 jit_solution(2358004412806660938)
XLA Ops:
  0.6 0.0 copy-start
  0.6 1.0 pad_maximum_fusion.1.own_ref
  1.6 8.3 %collective-permute-start = (bf16[128,1024]{1,0:T(8,128)(2,1)S(1)}, bf16[128,1024]{1,0:T(8,128)(2,1)S(1)}, u32[]{:S(2)}, u32[]{:S(2)}) collective-permute-start(bf16[128,1024]{1,0:T(8,128)(2,1)S(1)} %pad_maximum_fusion.1.own_ref), channel_id=1, source_target_pairs={{0,32},{32,0},{64,96},{96,64},{128,160},{160,128},{192,224},{224,1... | collective-permute-start | bytes 786440 | tf_op jit(solution)/shard_map/ppermute | solution.py:14
  9.9 3.1 %collective-permute-start.2 = (bf16[128,1024]{1,0:T(8,128)(2,1)S(1)}, bf16[128,1024]{1,0:T(8,128)(2,1)S(1)}, u32[]{:S(2)}, u32[]{:S(2)}) collective-permute-start(bf16[128,1024]{1,0:T(8,128)(2,1)S(1)} %pad_maximum_fusion.1.own_ref), channel_id=1, source_target_pairs={{0,31},{1,2},{2,1},{3,4},{4,3},{5,6},{6,5},{7,8},{8,7},{9,10},{10,... | collective-permute-start | bytes 786440 | tf_op jit(solution)/shard_map/ppermute | solution.py:19
  13.1 0.7 pad_maximum_fusion.2
  13.8 6.8 %collective-permute-done.pair_ref = bf16[128,1024]{1,0:T(8,128)(2,1)S(1)} collective-permute-done((bf16[128,1024]{1,0:T(8,128)(2,1)S(1)}, bf16[128,1024]{1,0:T(8,128)(2,1)S(1)}, u32[]{:S(2)}, u32[]{:S(2)}) %collective-permute-start) | collective-permute-done | bytes 262176 | tf_op jit(solution)/shard_map/ppermute | solution.py:14
  20.6 1.9 %collective-permute-start.1 = (bf16[128,1024]{1,0:T(8,128)(2,1)S(1)}, bf16[128,1024]{1,0:T(8,128)(2,1)S(1)}, u32[]{:S(2)}, u32[]{:S(2)}) collective-permute-start(bf16[128,1024]{1,0:T(8,128)(2,1)S(1)} %collective-permute-done.pair_ref), channel_id=1, source_target_pairs={{0,64},{32,480},{64,128},{96,32},{128,192},{160,96},{192,256},{224... | collective-permute-start | bytes 786440 | tf_op jit(solution)/shard_map/ppermute | solution.py:24
  22.6 25.8 %all_to_all.20 = bf16[16,8,128]{2,1,0:T(8,128)(2,1)S(1)} all-to-all(bf16[16,8,128]{2,1,0:T(8,128)(2,1)S(1)} %broadcast_in_dim.41), channel_id=1, replica_groups={{0,2,4,6,32,34,36,38,16,18,20,22,48,50,52,54},{1,3,5,7,33,35,37,39,17,1..., dimensions={0} | all-to-all | bytes 65536 | tf_op jit(solution)/shard_map/all_to_all | solution.py:47
  48.4 0.0 collective-permute-done.2.far_own_ref
  48.4 0.0 collective-permute-done.1.skip_ref
  48.4 0.9 broadcast_in_dim.42
  49.3 3.6 %all-to-all-start.1 = ((bf16[16,16,1024]{2,1,0:T(8,128)(2,1)}), bf16[16,16,1024]{2,1,0:T(8,128)(2,1)S(1)}, u32[]{:S(2)}, u32[]{:S(2)}) async-start(bf16[16,16,1024]{2,1,0:T(8,128)(2,1)} %broadcast_in_dim.42), calls=%async_computation.1 | async-start | bytes 1048576 | tf_op jit(solution)/shard_map/all_to_all | solution.py:47
  52.8 0.0 copy-start.3
  52.9 0.8 pad_maximum_fusion
  53.7 8.0 %collective-permute-start.5 = (bf16[2,128,1024]{2,1,0:T(8,128)(2,1)}, bf16[2,128,1024]{2,1,0:T(8,128)(2,1)S(1)}, u32[]{:S(2)}, u32[]{:S(2)}) collective-permute-start(bf16[2,128,1024]{2,1,0:T(8,128)(2,1)} %pad_maximum_fusion), channel_id=1, source_target_pairs={{0,31},{1,2},{2,1},{3,4},{4,3},{5,6},{6,5},{7,8},{8,7},{9,10},{10,... | collective-permute-start | bytes 1572872 | tf_op jit(solution)/shard_map/ppermute | solution.py:19
  61.7 1.9 %collective-permute-start.3 = (bf16[128,1024]{1,0:T(8,128)(2,1)S(1)}, bf16[128,1024]{1,0:T(8,128)(2,1)S(1)}, u32[]{:S(2)}, u32[]{:S(2)}) collective-permute-start(bf16[128,1024]{1,0:T(8,128)(2,1)S(1)} %pad_maximum_fusion.1.own_ref), channel_id=1, source_target_pairs={{0,1},{1,0},{2,3},{3,2},{4,5},{5,4},{6,7},{7,6},{8,9},{9,8},{10,11... | collective-permute-start | bytes 786440 | tf_op jit(solution)/shard_map/ppermute | solution.py:14
  63.6 0.6 compare_and_fusion.1
  64.2 0.6 compare_and_fusion
  64.8 0.5 fusion.10
  65.3 2.4 %collective-permute-start.4 = (bf16[2,128,1024]{2,1,0:T(8,128)(2,1)}, bf16[2,128,1024]{2,1,0:T(8,128)(2,1)S(1)}, u32[]{:S(2)}, u32[]{:S(2)}) collective-permute-start(bf16[2,128,1024]{2,1,0:T(8,128)(2,1)} %pad_maximum_fusion), channel_id=1, source_target_pairs={{0,1},{1,0},{2,3},{3,2},{4,5},{5,4},{6,7},{7,6},{8,9},{9,8},{10,11... | collective-permute-start | bytes 1572872 | tf_op jit(solution)/shard_map/ppermute | solution.py:14
  67.7 5.9 %collective-permute-done.5.far_ref = bf16[2,128,1024]{2,1,0:T(8,128)(2,1)S(1)} collective-permute-done((bf16[2,128,1024]{2,1,0:T(8,128)(2,1)}, bf16[2,128,1024]{2,1,0:T(8,128)(2,1)S(1)}, u32[]{:S(2)}, u32[]{:S(2)}) %collective-permute-start.5) | collective-permute-done | bytes 524320 | tf_op jit(solution)/shard_map/ppermute | solution.py:19
  73.6 0.0 all-to-all-done.1
  73.6 3.9 %collective-permute-start.6 = (bf16[256,1024]{1,0:T(8,128)(2,1)S(1)}, bf16[256,1024]{1,0:T(8,128)(2,1)S(1)}, u32[]{:S(2)}, u32[]{:S(2)}) collective-permute-start(bf16[256,1024]{1,0:T(8,128)(2,1)S(1)} %bitcast.47), channel_id=1, source_target_pairs={{0,1},{1,0},{2,3},{3,2},{4,5},{5,4},{6,7},{7,6},{8,9},{9,8},{10,11... | collective-permute-start | bytes 1572872 | tf_op jit(solution)/shard_map/ppermute | solution.py:14
  77.5 0.7 broadcast_or_fusion
  78.3 0.1 reshape.193
  78.4 0.0 copy-done
  78.4 0.7 gather_fusion
  79.1 0.1 reshape.196
  79.1 0.7 and_select_fusion
  79.9 0.1 select_n.39
  80.0 0.1 pad_add_fusion.2.counts
  80.1 0.0 collective-permute-done.3.near_own_ref
  80.1 0.0 collective-permute-done.4.near_ref
  80.1 0.0 collective-permute-done.6.other_ref
  80.1 0.0 copy-done.3
  80.1 0.0 copy-start.4
  80.1 0.9 copy-done.4
  81.0 9.9 %shard_map.110 = (bf16[128,512]{1,0:T(8,128)(2,1)}, f32[3,128,1024]{2,1,0:T(8,128)S(1)}, bf16[640,1024]{1,0:T(8,128)(2,1)S(1)}, bf16[128,1024]{1,0:T(8,128)(2,1)...) custom-call(s32[10]{0:T(128)S(1)} %pad_add_fusion.2.counts, bf16[128,512]{1,0:T(8,128)(2,1)S(1)} %bitcast.51, ...), custom_call_target="tpu_custom_call" | custom-call | flops 1090519040 | bytes 12582912 | tf_op jit(solution)/shard_map/pallas_call | solution.py:161
  91.0 1.9 %collective-permute-start.7 = (bf16[640,1024]{1,0:T(8,128)(2,1)S(1)}, bf16[640,1024]{1,0:T(8,128)(2,1)S(1)}, u32[]{:S(2)}, u32[]{:S(2)}) collective-permute-start(bf16[640,1024]{1,0:T(8,128)(2,1)S(1)} %get-tuple-element.31), channel_id=1, source_target_pairs={{0,1},{1,0},{2,3},{3,2},{4,5},{5,4},{6,7},{7,6},{8,9},{9,8},{10,11... | collective-permute-start | bytes 3932168 | tf_op jit(solution)/shard_map/ppermute | solution.py:14
  92.9 2.8 %collective-permute-start.8 = (bf16[2,128,1024]{2,1,0:T(8,128)(2,1)S(1)}, bf16[2,128,1024]{2,1,0:T(8,128)(2,1)S(1)}, u32[]{:S(2)}, u32[]{:S(2)}) collective-permute-start(bf16[2,128,1024]{2,1,0:T(8,128)(2,1)S(1)} %get-tuple-element.32), channel_id=1, source_target_pairs={{0,31},{1,2},{2,1},{3,4},{4,3},{5,6},{6,5},{7,8},{8,7},{9,10},{10,... | collective-permute-start | bytes 1572872 | tf_op jit(solution)/shard_map/ppermute | solution.py:19
  95.6 0.2 collective-permute-done.7
  95.9 0.3 convert_element_type.38
  96.2 0.0 copy-done.1
  96.2 0.9 fusion
  97.1 0.2 slice.50
  97.3 0.3 add.69
  97.6 9.7 %collective-permute-done.8 = bf16[2,128,1024]{2,1,0:T(8,128)(2,1)S(1)} collective-permute-done((bf16[2,128,1024]{2,1,0:T(8,128)(2,1)S(1)}, bf16[2,128,1024]{2,1,0:T(8,128)(2,1)S(1)}, u32[]{:S(2)}, u32[]{:S(2)}) %collective-permute-start.8) | collective-permute-done | bytes 524320 | tf_op jit(solution)/shard_map/ppermute | solution.py:19
  107.3 0.1 fusion.8
  107.3 4.0 %collective-permute-start.10 = (bf16[128,1024]{1,0:T(8,128)(2,1)S(1)}, bf16[128,1024]{1,0:T(8,128)(2,1)S(1)}, u32[]{:S(2)}, u32[]{:S(2)}) collective-permute-start(bf16[128,1024]{1,0:T(8,128)(2,1)S(1)} %fusion.8), channel_id=1, source_target_pairs={{0,448},{32,96},{64,0},{96,160},{128,64},{160,224},{192,128},{224,... | collective-permute-start | bytes 786440 | tf_op jit(solution)/shard_map/ppermute | solution.py:24
  111.3 4.9 %all-to-all-start.2 = ((bf16[16,16,1024]{2,1,0:T(8,128)(2,1)}), bf16[16,16,1024]{2,1,0:T(8,128)(2,1)S(1)}, u32[]{:S(2)}, u32[]{:S(2)}) async-start(bf16[16,16,1024]{2,1,0:T(8,128)(2,1)} %bitcast.20), calls=%async_computation.2 | async-start | bytes 1048576 | tf_op jit(solution)/shard_map/all_to_all | solution.py:47
  116.3 3.5 %collective-permute-start.9 = (bf16[128,1024]{1,0:T(8,128)(2,1)S(1)}, bf16[128,1024]{1,0:T(8,128)(2,1)S(1)}, u32[]{:S(2)}, u32[]{:S(2)}) collective-permute-start(bf16[128,1024]{1,0:T(8,128)(2,1)S(1)} %copy-done.2), channel_id=1, source_target_pairs={{0,31},{1,2},{2,1},{3,4},{4,3},{5,6},{6,5},{7,8},{8,7},{9,10},{10,... | collective-permute-start | bytes 786440 | tf_op jit(solution)/shard_map/ppermute | solution.py:19
  119.7 0.0 collective-permute-done.10
  119.7 0.1 fusion.3
  119.8 5.8 %collective-permute-start.11 = (bf16[128,1024]{1,0:T(8,128)(2,1)S(1)}, bf16[128,1024]{1,0:T(8,128)(2,1)S(1)}, u32[]{:S(2)}, u32[]{:S(2)}) collective-permute-start(bf16[128,1024]{1,0:T(8,128)(2,1)S(1)} %fusion.3), channel_id=1, source_target_pairs={{0,32},{32,0},{64,96},{96,64},{128,160},{160,128},{192,224},{224,1... | collective-permute-start | bytes 786440 | tf_op jit(solution)/shard_map/ppermute | solution.py:14
  125.7 0.0 collective-permute-done.9
  125.7 9.1 %collective-permute-done.11 = bf16[128,1024]{1,0:T(8,128)(2,1)S(1)} collective-permute-done((bf16[128,1024]{1,0:T(8,128)(2,1)S(1)}, bf16[128,1024]{1,0:T(8,128)(2,1)S(1)}, u32[]{:S(2)}, u32[]{:S(2)}) %collective-permute-start.11) | collective-permute-done | bytes 262176 | tf_op jit(solution)/shard_map/ppermute | solution.py:14
  134.8 0.1 fusion.7
  134.9 0.0 all-to-all-done.2
  134.9 0.1 convert_reduce_fusion
  135.0 0.6 copy.13
  135.6 12.6 %all-to-all-start.3 = ((f32[16,8,128]{2,1,0:T(8,128)}), f32[16,8,128]{2,1,0:T(8,128)S(1)}, u32[]{:S(2)}, u32[]{:S(2)}) async-start(f32[16,8,128]{2,1,0:T(8,128)} %bitcast.27), calls=%async_computation.3 | async-start | bytes 131072 | tf_op jit(solution)/shard_map/all_to_all | solution.py:47
  148.2 0.7 slice_bitcast_fusion.1
  148.9 8.2 %all-to-all-done.3 = f32[16,8,128]{2,1,0:T(8,128)S(1)} async-done(((f32[16,8,128]{2,1,0:T(8,128)}), f32[16,8,128]{2,1,0:T(8,128)S(1)}, u32[]{:S(2)}, u32[]{:S(2)}) %all-to-all-start.3) | async-done | bytes 65568 | tf_op jit(solution)/shard_map/all_to_all | solution.py:47
  157.1 0.6 fusion.13
  (7 shorter events, 0.1 us)
Async XLA Ops:
  0.6 77.7 %copy-start = (s32[16,32]{1,0:T(8,128)S(1)}, s32[16,32]{1,0:T(8,128)}, u32[]{:S(2)}) copy-start(s32[16,32]{1,0:T(8,128)} %param.13) | copy-start | bytes 6148
  1.6 19.0 %collective-permute-start = (bf16[128,1024]{1,0:T(8,128)(2,1)S(1)}, bf16[128,1024]{1,0:T(8,128)(2,1)S(1)}, u32[]{:S(2)}, u32[]{:S(2)}) collective-permute-start(bf16[128,1024]{1,0:T(8,128)(2,1)S(1)} %pad_maximum_fusion.1.own_ref), channel_id=1, source_target_pairs={{0,32},{32,0},{64,96},{96,64},{128,160},{160,128},{192,224},{224,1... | collective-permute-start | bytes 786440 | tf_op jit(solution)/shard_map/ppermute | solution.py:14
  9.9 38.5 %collective-permute-start.2 = (bf16[128,1024]{1,0:T(8,128)(2,1)S(1)}, bf16[128,1024]{1,0:T(8,128)(2,1)S(1)}, u32[]{:S(2)}, u32[]{:S(2)}) collective-permute-start(bf16[128,1024]{1,0:T(8,128)(2,1)S(1)} %pad_maximum_fusion.1.own_ref), channel_id=1, source_target_pairs={{0,31},{1,2},{2,1},{3,4},{4,3},{5,6},{6,5},{7,8},{8,7},{9,10},{10,... | collective-permute-start | bytes 786440 | tf_op jit(solution)/shard_map/ppermute | solution.py:19
  20.6 27.8 %collective-permute-start.1 = (bf16[128,1024]{1,0:T(8,128)(2,1)S(1)}, bf16[128,1024]{1,0:T(8,128)(2,1)S(1)}, u32[]{:S(2)}, u32[]{:S(2)}) collective-permute-start(bf16[128,1024]{1,0:T(8,128)(2,1)S(1)} %collective-permute-done.pair_ref), channel_id=1, source_target_pairs={{0,64},{32,480},{64,128},{96,32},{128,192},{160,96},{192,256},{224... | collective-permute-start | bytes 786440 | tf_op jit(solution)/shard_map/ppermute | solution.py:24
  49.3 24.4 %all-to-all-start.1 = ((bf16[16,16,1024]{2,1,0:T(8,128)(2,1)}), bf16[16,16,1024]{2,1,0:T(8,128)(2,1)S(1)}, u32[]{:S(2)}, u32[]{:S(2)}) async-start(bf16[16,16,1024]{2,1,0:T(8,128)(2,1)} %broadcast_in_dim.42), calls=%async_computation.1 | async-start | bytes 1048576 | tf_op jit(solution)/shard_map/all_to_all | solution.py:47
  52.8 27.3 %copy-start.3 = (bf16[1,1,128,512]{3,2,1,0:T(8,128)(2,1)S(1)}, bf16[1,1,128,512]{3,2,1,0:T(8,128)(2,1)}, u32[]{:S(2)}) copy-start(bf16[1,1,128,512]{3,2,1,0:T(8,128)(2,1)} %param.7) | copy-start | bytes 393220
  53.7 19.9 %collective-permute-start.5 = (bf16[2,128,1024]{2,1,0:T(8,128)(2,1)}, bf16[2,128,1024]{2,1,0:T(8,128)(2,1)S(1)}, u32[]{:S(2)}, u32[]{:S(2)}) collective-permute-start(bf16[2,128,1024]{2,1,0:T(8,128)(2,1)} %pad_maximum_fusion), channel_id=1, source_target_pairs={{0,31},{1,2},{2,1},{3,4},{4,3},{5,6},{6,5},{7,8},{8,7},{9,10},{10,... | collective-permute-start | bytes 1572872 | tf_op jit(solution)/shard_map/ppermute | solution.py:19
  61.7 18.4 %collective-permute-start.3 = (bf16[128,1024]{1,0:T(8,128)(2,1)S(1)}, bf16[128,1024]{1,0:T(8,128)(2,1)S(1)}, u32[]{:S(2)}, u32[]{:S(2)}) collective-permute-start(bf16[128,1024]{1,0:T(8,128)(2,1)S(1)} %pad_maximum_fusion.1.own_ref), channel_id=1, source_target_pairs={{0,1},{1,0},{2,3},{3,2},{4,5},{5,4},{6,7},{7,6},{8,9},{9,8},{10,11... | collective-permute-start | bytes 786440 | tf_op jit(solution)/shard_map/ppermute | solution.py:14
  65.3 14.8 %collective-permute-start.4 = (bf16[2,128,1024]{2,1,0:T(8,128)(2,1)}, bf16[2,128,1024]{2,1,0:T(8,128)(2,1)S(1)}, u32[]{:S(2)}, u32[]{:S(2)}) collective-permute-start(bf16[2,128,1024]{2,1,0:T(8,128)(2,1)} %pad_maximum_fusion), channel_id=1, source_target_pairs={{0,1},{1,0},{2,3},{3,2},{4,5},{5,4},{6,7},{7,6},{8,9},{9,8},{10,11... | collective-permute-start | bytes 1572872 | tf_op jit(solution)/shard_map/ppermute | solution.py:14
  73.6 6.5 %collective-permute-start.6 = (bf16[256,1024]{1,0:T(8,128)(2,1)S(1)}, bf16[256,1024]{1,0:T(8,128)(2,1)S(1)}, u32[]{:S(2)}, u32[]{:S(2)}) collective-permute-start(bf16[256,1024]{1,0:T(8,128)(2,1)S(1)} %bitcast.47), channel_id=1, source_target_pairs={{0,1},{1,0},{2,3},{3,2},{4,5},{5,4},{6,7},{7,6},{8,9},{9,8},{10,11... | collective-permute-start | bytes 1572872 | tf_op jit(solution)/shard_map/ppermute | solution.py:14
  80.1 0.9 copy-start.4
  91.0 5.2 %copy-start.1 = (bf16[128,1024]{1,0:T(8,128)(2,1)}, bf16[128,1024]{1,0:T(8,128)(2,1)S(1)}, u32[]{:S(2)}) copy-start(bf16[128,1024]{1,0:T(8,128)(2,1)S(1)} %get-tuple-element.36) | copy-start | bytes 786436
  91.0 4.9 %collective-permute-start.7 = (bf16[640,1024]{1,0:T(8,128)(2,1)S(1)}, bf16[640,1024]{1,0:T(8,128)(2,1)S(1)}, u32[]{:S(2)}, u32[]{:S(2)}) collective-permute-start(bf16[640,1024]{1,0:T(8,128)(2,1)S(1)} %get-tuple-element.31), channel_id=1, source_target_pairs={{0,1},{1,0},{2,3},{3,2},{4,5},{5,4},{6,7},{7,6},{8,9},{9,8},{10,11... | collective-permute-start | bytes 3932168 | tf_op jit(solution)/shard_map/ppermute | solution.py:14
  92.9 14.4 %collective-permute-start.8 = (bf16[2,128,1024]{2,1,0:T(8,128)(2,1)S(1)}, bf16[2,128,1024]{2,1,0:T(8,128)(2,1)S(1)}, u32[]{:S(2)}, u32[]{:S(2)}) collective-permute-start(bf16[2,128,1024]{2,1,0:T(8,128)(2,1)S(1)} %get-tuple-element.32), channel_id=1, source_target_pairs={{0,31},{1,2},{2,1},{3,4},{4,3},{5,6},{6,5},{7,8},{8,7},{9,10},{10,... | collective-permute-start | bytes 1572872 | tf_op jit(solution)/shard_map/ppermute | solution.py:19
  97.6 18.7 %copy-start.2 = (bf16[128,1024]{1,0:T(8,128)(2,1)S(1)}, bf16[128,1024]{1,0:T(8,128)(2,1)}, u32[]{:S(2)}) copy-start(bf16[128,1024]{1,0:T(8,128)(2,1)} %copy-done.1) | copy-start | bytes 786436
  107.3 12.4 %collective-permute-start.10 = (bf16[128,1024]{1,0:T(8,128)(2,1)S(1)}, bf16[128,1024]{1,0:T(8,128)(2,1)S(1)}, u32[]{:S(2)}, u32[]{:S(2)}) collective-permute-start(bf16[128,1024]{1,0:T(8,128)(2,1)S(1)} %fusion.8), channel_id=1, source_target_pairs={{0,448},{32,96},{64,0},{96,160},{128,64},{160,224},{192,128},{224,... | collective-permute-start | bytes 786440 | tf_op jit(solution)/shard_map/ppermute | solution.py:24
  111.3 23.6 %all-to-all-start.2 = ((bf16[16,16,1024]{2,1,0:T(8,128)(2,1)}), bf16[16,16,1024]{2,1,0:T(8,128)(2,1)S(1)}, u32[]{:S(2)}, u32[]{:S(2)}) async-start(bf16[16,16,1024]{2,1,0:T(8,128)(2,1)} %bitcast.20), calls=%async_computation.2 | async-start | bytes 1048576 | tf_op jit(solution)/shard_map/all_to_all | solution.py:47
  116.3 9.4 %collective-permute-start.9 = (bf16[128,1024]{1,0:T(8,128)(2,1)S(1)}, bf16[128,1024]{1,0:T(8,128)(2,1)S(1)}, u32[]{:S(2)}, u32[]{:S(2)}) collective-permute-start(bf16[128,1024]{1,0:T(8,128)(2,1)S(1)} %copy-done.2), channel_id=1, source_target_pairs={{0,31},{1,2},{2,1},{3,4},{4,3},{5,6},{6,5},{7,8},{8,7},{9,10},{10,... | collective-permute-start | bytes 786440 | tf_op jit(solution)/shard_map/ppermute | solution.py:19
  119.8 15.0 %collective-permute-start.11 = (bf16[128,1024]{1,0:T(8,128)(2,1)S(1)}, bf16[128,1024]{1,0:T(8,128)(2,1)S(1)}, u32[]{:S(2)}, u32[]{:S(2)}) collective-permute-start(bf16[128,1024]{1,0:T(8,128)(2,1)S(1)} %fusion.3), channel_id=1, source_target_pairs={{0,32},{32,0},{64,96},{96,64},{128,160},{160,128},{192,224},{224,1... | collective-permute-start | bytes 786440 | tf_op jit(solution)/shard_map/ppermute | solution.py:14
  135.6 21.4 %all-to-all-start.3 = ((f32[16,8,128]{2,1,0:T(8,128)}), f32[16,8,128]{2,1,0:T(8,128)S(1)}, u32[]{:S(2)}, u32[]{:S(2)}) async-start(f32[16,8,128]{2,1,0:T(8,128)} %bitcast.27), calls=%async_computation.3 | async-start | bytes 131072 | tf_op jit(solution)/shard_map/all_to_all | solution.py:47

commit v4 on v3

--- a/solution.py
+++ b/solution.py
@@ -62,13 +62,16 @@
     return deal(jnp.broadcast_to(block, (members, held, width)), groups).reshape(members * held, width)
 
 
-def scatter_coarse(block):
+def scatter_second(block):
     width = block.shape[-1]
     first, second = place_groups()
-    held = len(first[0])
-    block = deal(block.reshape(len(second[0]), held, width), second).astype(jnp.float32).sum(axis=0)
-    block = deal(block.reshape(held, 8, width // 8), first).sum(axis=0)
-    return block.reshape(1, width)
+    return deal(block.reshape(len(second[0]), len(first[0]), width), second).astype(jnp.float32).sum(axis=0)
+
+
+def scatter_first(block):
+    held, width = block.shape
+    first, _ = place_groups()
+    return deal(block.reshape(held, 8, width // 8), first).sum(axis=0).reshape(1, width)
 
 
 def attention_kernel(
@@ -205,12 +208,12 @@
     own = jnp.concatenate([fine_keys[0, 0], fine_values[0, 0]], axis=-1)
     token = jnp.concatenate([coarse_keys, coarse_values], axis=-1)
     paired = exchange(own, "row", 1)
-    token, paired = lax.optimization_barrier((token, paired))
     coarse = gather_first(token)
+    coarse, paired, again = lax.optimization_barrier((coarse, paired, own))
     skipped = skip_row(paired, 2)
-    near_own, far_own = exchange(own, "col", 1), to_far(own, "col")
-    coarse, skipped, far_own = lax.optimization_barrier((coarse, skipped, far_own))
+    near_own, far_own = exchange(again, "col", 1), to_far(again, "col")
     kept = gather_second(coarse)
+    skipped, far_own = lax.optimization_barrier((skipped, far_own))
     lines = jnp.stack([paired, skipped])
     near, far = exchange(lines, "col", 1), to_far(lines, "col")
     kept, far = lax.optimization_barrier((kept, far))
@@ -222,11 +225,11 @@
     far_back = to_far(far_terms, "col")
     core_back = exchange(core_terms, "col", 1).astype(high)
     half = (kept_terms + core_back[3 * rows :]).astype(low)
-    half, far_own_terms = lax.optimization_barrier((half, far_own_terms))
     line = own_terms + core_back[: 3 * rows].reshape(own_terms.shape)
     skipped_line = (line[2] + far_back[1].astype(high)).astype(low)
-    skipped_line, far_own_terms = lax.optimization_barrier((skipped_line, far_own_terms))
-    coarse_sum = scatter_coarse(half)
+    coarse_sum = scatter_second(half)
+    coarse_sum, skipped_line, far_own_terms = lax.optimization_barrier((coarse_sum, skipped_line, far_own_terms))
+    coarse_sum = scatter_first(coarse_sum)
     forwarded = skip_row(skipped_line, -2).astype(high)
     paired_line = (line[1] + far_back[0].astype(high) + forwarded).astype(low)
     returned = exchange(paired_line, "row", 1).astype(high)

time: 159 us -> 170 us (1.069)
  blocking collectives: 25.8 us -> 14.7 us
  local copies, waits for them, and re-layouts: 4.84 us -> 11.2 us
  waiting for transfers between devices: 39.9 us -> 46.1 us
  starting transfers between devices: 68.5 us -> 74.2 us
  other arithmetic: 7.71 us -> 10.4 us
    ppermute x2, waiting for transfers between devices: 0.01 us -> 11.7 us  [skip_row(): lax.ppermute(block, 'row', [(i, (i + (-way if i % 2 else way)) % size) fo...]
    all_to_all x1, blocking collectives: 25.8 us -> 14.7 us  [deal(): lax.all_to_all(block, ('row', 'col'), 0, 0, axis_index_groups=groups, til...]
    all_to_all x3, waiting for transfers between devices: 8.16 us -> 0.01 us  [deal(): lax.all_to_all(block, ('row', 'col'), 0, 0, axis_index_groups=groups, til...]
    unnamed x12 -> x32, local copies, waits for them, and re-layouts: 1.56 us -> 7.91 us
    ppermute x6, starting transfers between devices: 24.2 us -> 29.6 us  [exchange(): lax.ppermute(block, axis, [(i, i ^ bit) for i in range(lax.axis_size(axis...]
    ppermute x4, waiting for transfers between devices: 15.6 us -> 18.4 us  [to_far(): lax.ppermute(block, axis, [(i, (i + (1 if i % 2 else -1)) % size) for i i...]
    ppermute x2, starting transfers between devices: 5.89 us -> 8.18 us  [skip_row(): lax.ppermute(block, 'row', [(i, (i + (-way if i % 2 else way)) % size) fo...]
    ppermute x4, starting transfers between devices: 17.3 us -> 15.1 us  [to_far(): lax.ppermute(block, axis, [(i, (i + (1 if i % 2 else -1)) % size) for i i...]
  transfers between devices with their start and end apart: 15 -> 15, of which waited for: 6 -> 7; matrix products, arithmetic and copies ran while one was open for 5% -> 5% of each run, Pallas kernels for 0% -> 0%
where the time goes in v4:
time: 170 us; the launch traced here: 168 us
  starting transfers between devices  74.2 us (44%)
  waiting for transfers between devices  46.1 us (27%)
  blocking collectives  14.7 us (9%)
  local copies, waits for them, and re-layouts  11.2 us (7%)
  other arithmetic  10.4 us (6%)
  Pallas kernels  9.95 us (6%)
    ppermute x6, starting transfers between devices, exchange(): lax.ppermute(block, axis, [(i, i ^ bit) for i in range(lax.axis_size(axis...  29.6 us
    all_to_all x3, starting transfers between devices, deal(): lax.all_to_all(block, ('row', 'col'), 0, 0, axis_index_groups=groups, til...  21.4 us
    ppermute x4, waiting for transfers between devices, to_far(): lax.ppermute(block, axis, [(i, (i + (1 if i % 2 else -1)) % size) for i i...  18.4 us
    ppermute x6, waiting for transfers between devices, exchange(): lax.ppermute(block, axis, [(i, i ^ bit) for i in range(lax.axis_size(axis...  16 us
    ppermute x4, starting transfers between devices, to_far(): lax.ppermute(block, axis, [(i, (i + (1 if i % 2 else -1)) % size) for i i...  15.1 us
    all_to_all x1, blocking collectives, deal(): lax.all_to_all(block, ('row', 'col'), 0, 0, axis_index_groups=groups, til...  14.7 us
    ppermute x2, waiting for transfers between devices, skip_row(): lax.ppermute(block, 'row', [(i, (i + (-way if i % 2 else way)) % size) fo...  11.7 us
    pallas_call x1, Pallas kernels, attention(): pl.pallas_call(attention_kernel, out_shape=(jax.ShapeDtypeStruct((rows, w...  9.95 us
  transfers between devices with their start and end apart: 15, of which 7 were waited for; matrix products, arithmetic and copies ran while one was open for 5% of the time, Pallas kernels for 0%

profile of v4, /device:TPU:1, one launch (start us, length us, event | category | flops | bytes accessed | tf_op | source)
XLA Modules:
  0.0 167.5 jit_solution(10743684813341074253)
XLA Ops:
  0.6 0.0 copy-start
  0.6 1.0 pad_maximum_fusion.1.own_ref
  1.6 8.3 %collective-permute-start = (bf16[128,1024]{1,0:T(8,128)(2,1)S(1)}, bf16[128,1024]{1,0:T(8,128)(2,1)S(1)}, u32[]{:S(2)}, u32[]{:S(2)}) collective-permute-start(bf16[128,1024]{1,0:T(8,128)(2,1)S(1)} %pad_maximum_fusion.1.own_ref), channel_id=1, source_target_pairs={{0,32},{32,0},{64,96},{96,64},{128,160},{160,128},{192,224},{224,1... | collective-permute-start | bytes 786440 | tf_op jit(solution)/shard_map/ppermute | solution.py:14
  9.9 0.7 maximum_reduce_fusion
  10.7 14.7 %all_to_all.20 = bf16[16,8,128]{2,1,0:T(8,128)(2,1)S(1)} all-to-all(bf16[16,8,128]{2,1,0:T(8,128)(2,1)S(1)} %broadcast_in_dim.41), channel_id=1, replica_groups={{0,2,4,6,32,34,36,38,16,18,20,22,48,50,52,54},{1,3,5,7,33,35,37,39,17,1..., dimensions={0} | all-to-all | bytes 65536 | tf_op jit(solution)/shard_map/all_to_all | solution.py:47
  25.4 0.0 collective-permute-done.pair_ref
  25.4 0.9 broadcast_in_dim.42
  26.2 10.5 %all-to-all-start.1 = ((bf16[16,16,1024]{2,1,0:T(8,128)(2,1)}), bf16[16,16,1024]{2,1,0:T(8,128)(2,1)S(1)}, u32[]{:S(2)}, u32[]{:S(2)}) async-start(bf16[16,16,1024]{2,1,0:T(8,128)(2,1)} %broadcast_in_dim.42), calls=%async_computation.1 | async-start | bytes 1048576 | tf_op jit(solution)/shard_map/all_to_all | solution.py:47
  36.7 3.8 %collective-permute-start.2 = (bf16[128,1024]{1,0:T(8,128)(2,1)S(1)}, bf16[128,1024]{1,0:T(8,128)(2,1)S(1)}, u32[]{:S(2)}, u32[]{:S(2)}) collective-permute-start(bf16[128,1024]{1,0:T(8,128)(2,1)S(1)} %pad_maximum_fusion.1.own_ref), channel_id=1, source_target_pairs={{0,31},{1,2},{2,1},{3,4},{4,3},{5,6},{6,5},{7,8},{8,7},{9,10},{10,... | collective-permute-start | bytes 786440 | tf_op jit(solution)/shard_map/ppermute | solution.py:19
  40.5 3.5 %collective-permute-start.1 = (bf16[128,1024]{1,0:T(8,128)(2,1)S(1)}, bf16[128,1024]{1,0:T(8,128)(2,1)S(1)}, u32[]{:S(2)}, u32[]{:S(2)}) collective-permute-start(bf16[128,1024]{1,0:T(8,128)(2,1)S(1)} %collective-permute-done.pair_ref), channel_id=1, source_target_pairs={{0,64},{32,480},{64,128},{96,32},{128,192},{160,96},{192,256},{224... | collective-permute-start | bytes 786440 | tf_op jit(solution)/shard_map/ppermute | solution.py:24
  44.0 0.8 collective-permute-done.2.far_own_ref
  44.8 11.7 %collective-permute-done.1.skip_ref = bf16[128,1024]{1,0:T(8,128)(2,1)S(1)} collective-permute-done((bf16[128,1024]{1,0:T(8,128)(2,1)S(1)}, bf16[128,1024]{1,0:T(8,128)(2,1)S(1)}, u32[]{:S(2)}, u32[]{:S(2)}) %collective-permute-start.1) | collective-permute-done | bytes 262176 | tf_op jit(solution)/shard_map/ppermute | solution.py:24
  56.5 0.9 pad_maximum_fusion
  57.4 3.8 %collective-permute-start.5 = (bf16[2,128,1024]{2,1,0:T(8,128)(2,1)}, bf16[2,128,1024]{2,1,0:T(8,128)(2,1)S(1)}, u32[]{:S(2)}, u32[]{:S(2)}) collective-permute-start(bf16[2,128,1024]{2,1,0:T(8,128)(2,1)} %pad_maximum_fusion), channel_id=1, source_target_pairs={{0,31},{1,2},{2,1},{3,4},{4,3},{5,6},{6,5},{7,8},{8,7},{9,10},{10,... | collective-permute-start | bytes 1572872 | tf_op jit(solution)/shard_map/ppermute | solution.py:19
  61.3 0.1 compare_and_fusion.1
  61.3 0.1 compare_and_fusion
  61.4 3.4 %collective-permute-start.4 = (bf16[2,128,1024]{2,1,0:T(8,128)(2,1)}, bf16[2,128,1024]{2,1,0:T(8,128)(2,1)S(1)}, u32[]{:S(2)}, u32[]{:S(2)}) collective-permute-start(bf16[2,128,1024]{2,1,0:T(8,128)(2,1)} %pad_maximum_fusion), channel_id=1, source_target_pairs={{0,1},{1,0},{2,3},{3,2},{4,5},{5,4},{6,7},{7,6},{8,9},{9,8},{10,11... | collective-permute-start | bytes 1572872 | tf_op jit(solution)/shard_map/ppermute | solution.py:14
  64.9 6.6 %collective-permute-done.5.far_ref = bf16[2,128,1024]{2,1,0:T(8,128)(2,1)S(1)} collective-permute-done((bf16[2,128,1024]{2,1,0:T(8,128)(2,1)}, bf16[2,128,1024]{2,1,0:T(8,128)(2,1)S(1)}, u32[]{:S(2)}, u32[]{:S(2)}) %collective-permute-start.5) | collective-permute-done | bytes 524320 | tf_op jit(solution)/shard_map/ppermute | solution.py:19
  71.5 0.0 all-to-all-done.1
  71.5 7.8 %collective-permute-start.6 = (bf16[256,1024]{1,0:T(8,128)(2,1)S(1)}, bf16[256,1024]{1,0:T(8,128)(2,1)S(1)}, u32[]{:S(2)}, u32[]{:S(2)}) collective-permute-start(bf16[256,1024]{1,0:T(8,128)(2,1)S(1)} %bitcast.47), channel_id=1, source_target_pairs={{0,1},{1,0},{2,3},{3,2},{4,5},{5,4},{6,7},{7,6},{8,9},{9,8},{10,11... | collective-permute-start | bytes 1572872 | tf_op jit(solution)/shard_map/ppermute | solution.py:14
  79.3 0.1 broadcast_or_fusion
  79.4 0.1 reshape.193
  79.5 0.7 gather_fusion
  80.2 0.1 reshape.196
  80.3 1.9 %collective-permute-start.3 = (bf16[128,1024]{1,0:T(8,128)(2,1)S(1)}, bf16[128,1024]{1,0:T(8,128)(2,1)S(1)}, u32[]{:S(2)}, u32[]{:S(2)}) collective-permute-start(bf16[128,1024]{1,0:T(8,128)(2,1)S(1)} %pad_maximum_fusion.1.own_ref), channel_id=1, source_target_pairs={{0,1},{1,0},{2,3},{3,2},{4,5},{5,4},{6,7},{7,6},{8,9},{9,8},{10,11... | collective-permute-start | bytes 786440 | tf_op jit(solution)/shard_map/ppermute | solution.py:14
  82.2 0.1 and_select_fusion
  82.2 0.1 select_n.39
  82.3 0.1 pad_add_fusion.2.counts
  82.4 1.2 collective-permute-done.3.near_own_ref
  83.7 0.7 copy-done.11
  84.4 0.0 collective-permute-done.4.near_ref
  84.4 0.8 copy-done.1
  85.2 0.0 collective-permute-done.6.other_ref
  85.2 0.8 copy-done.3
  86.0 1.0 copy-done.2
  87.1 1.0 copy-done.4
  88.1 0.9 copy-done.8
  89.1 0.9 copy-done.12
  90.0 0.9 copy-done.14
  90.9 9.9 %shard_map.110 = (bf16[128,512]{1,0:T(8,128)(2,1)}, f32[3,128,1024]{2,1,0:T(8,128)S(1)}, bf16[640,1024]{1,0:T(8,128)(2,1)S(1)}, bf16[128,1024]{1,0:T(8,128)(2,1)...) custom-call(s32[10]{0:T(128)S(1)} %pad_add_fusion.2.counts, bf16[128,512]{1,0:T(8,128)(2,1)S(1)} %bitcast.51, ...), custom_call_target="tpu_custom_call" | custom-call | flops 1090519040 | bytes 12582912 | tf_op jit(solution)/shard_map/pallas_call | solution.py:164
  100.9 2.0 %collective-permute-start.7 = (bf16[640,1024]{1,0:T(8,128)(2,1)S(1)}, bf16[640,1024]{1,0:T(8,128)(2,1)S(1)}, u32[]{:S(2)}, u32[]{:S(2)}) collective-permute-start(bf16[640,1024]{1,0:T(8,128)(2,1)S(1)} %get-tuple-element.30), channel_id=1, source_target_pairs={{0,1},{1,0},{2,3},{3,2},{4,5},{5,4},{6,7},{7,6},{8,9},{9,8},{10,11... | collective-permute-start | bytes 3932168 | tf_op jit(solution)/shard_map/ppermute | solution.py:14
  102.9 2.9 %collective-permute-done.7 = bf16[640,1024]{1,0:T(8,128)(2,1)S(1)} collective-permute-done((bf16[640,1024]{1,0:T(8,128)(2,1)S(1)}, bf16[640,1024]{1,0:T(8,128)(2,1)S(1)}, u32[]{:S(2)}, u32[]{:S(2)}) %collective-permute-start.7) | collective-permute-done | bytes 1310752 | tf_op jit(solution)/shard_map/ppermute | solution.py:14
  105.8 0.3 convert_element_type.38
  106.2 0.9 fusion
  107.1 4.4 %all-to-all-start.2 = ((bf16[16,16,1024]{2,1,0:T(8,128)(2,1)}), bf16[16,16,1024]{2,1,0:T(8,128)(2,1)}, u32[]{:S(2)}, u32[]{:S(2)}) async-start(bf16[16,16,1024]{2,1,0:T(8,128)(2,1)} %bitcast.54), calls=%async_computation.2 | async-start | bytes 1048576 | tf_op jit(solution)/shard_map/all_to_all | solution.py:47
  111.5 1.9 %collective-permute-start.8 = (bf16[2,128,1024]{2,1,0:T(8,128)(2,1)S(1)}, bf16[2,128,1024]{2,1,0:T(8,128)(2,1)}, u32[]{:S(2)}, u32[]{:S(2)}) collective-permute-start(bf16[2,128,1024]{2,1,0:T(8,128)(2,1)S(1)} %copy-done.6), channel_id=1, source_target_pairs={{0,31},{1,2},{2,1},{3,4},{4,3},{5,6},{6,5},{7,8},{8,7},{9,10},{10,... | collective-permute-start | bytes 1572872 | tf_op jit(solution)/shard_map/ppermute | solution.py:19
  113.5 0.2 slice.50
  113.6 1.5 add.69
  115.1 11.0 %collective-permute-done.8 = bf16[2,128,1024]{2,1,0:T(8,128)(2,1)} collective-permute-done((bf16[2,128,1024]{2,1,0:T(8,128)(2,1)S(1)}, bf16[2,128,1024]{2,1,0:T(8,128)(2,1)}, u32[]{:S(2)}, u32[]{:S(2)}) %collective-permute-start.8) | collective-permute-done | bytes 524320 | tf_op jit(solution)/shard_map/ppermute | solution.py:19
  126.1 1.2 fusion.8
  127.3 0.0 all-to-all-done.2
  127.3 1.1 convert_reduce_fusion
  128.4 4.6 %collective-permute-start.10 = (bf16[128,1024]{1,0:T(8,128)(2,1)S(1)}, bf16[128,1024]{1,0:T(8,128)(2,1)S(1)}, u32[]{:S(2)}, u32[]{:S(2)}) collective-permute-start(bf16[128,1024]{1,0:T(8,128)(2,1)S(1)} %fusion.8), channel_id=1, source_target_pairs={{0,448},{32,96},{64,0},{96,160},{128,64},{160,224},{192,128},{224,... | collective-permute-start | bytes 786440 | tf_op jit(solution)/shard_map/ppermute | solution.py:24
  133.0 0.6 copy.13
  133.7 6.5 %all-to-all-start.3 = ((f32[16,8,128]{2,1,0:T(8,128)}), f32[16,8,128]{2,1,0:T(8,128)S(1)}, u32[]{:S(2)}, u32[]{:S(2)}) async-start(f32[16,8,128]{2,1,0:T(8,128)} %bitcast.27), calls=%async_computation.3 | async-start | bytes 131072 | tf_op jit(solution)/shard_map/all_to_all | solution.py:47
  140.2 5.5 %collective-permute-start.9 = (bf16[128,1024]{1,0:T(8,128)(2,1)S(1)}, bf16[128,1024]{1,0:T(8,128)(2,1)S(1)}, u32[]{:S(2)}, u32[]{:S(2)}) collective-permute-start(bf16[128,1024]{1,0:T(8,128)(2,1)S(1)} %copy-done.10), channel_id=1, source_target_pairs={{0,31},{1,2},{2,1},{3,4},{4,3},{5,6},{6,5},{7,8},{8,7},{9,10},{10,... | collective-permute-start | bytes 786440 | tf_op jit(solution)/shard_map/ppermute | solution.py:19
  145.8 0.0 collective-permute-done.10
  145.8 1.2 fusion.3
  147.0 6.1 %collective-permute-start.11 = (bf16[128,1024]{1,0:T(8,128)(2,1)S(1)}, bf16[128,1024]{1,0:T(8,128)(2,1)S(1)}, u32[]{:S(2)}, u32[]{:S(2)}) collective-permute-start(bf16[128,1024]{1,0:T(8,128)(2,1)S(1)} %fusion.3), channel_id=1, source_target_pairs={{0,32},{32,0},{64,96},{96,64},{128,160},{160,128},{192,224},{224,1... | collective-permute-start | bytes 786440 | tf_op jit(solution)/shard_map/ppermute | solution.py:14
  153.1 0.0 all-to-all-done.3
  153.1 0.6 fusion.13
  153.7 11.9 %collective-permute-done.11 = bf16[128,1024]{1,0:T(8,128)(2,1)S(1)} collective-permute-done((bf16[128,1024]{1,0:T(8,128)(2,1)S(1)}, bf16[128,1024]{1,0:T(8,128)(2,1)S(1)}, u32[]{:S(2)}, u32[]{:S(2)}) %collective-permute-start.11) | collective-permute-done | bytes 262176 | tf_op jit(solution)/shard_map/ppermute | solution.py:14
  165.6 1.2 fusion.7
  166.8 0.7 slice_bitcast_fusion.1
  (26 shorter events, 0.1 us)
Async XLA Ops:
  0.6 78.8 %copy-start = (s32[16,32]{1,0:T(8,128)S(1)}, s32[16,32]{1,0:T(8,128)}, u32[]{:S(2)}) copy-start(s32[16,32]{1,0:T(8,128)} %param.13) | copy-start | bytes 6148
  1.6 23.7 %collective-permute-start = (bf16[128,1024]{1,0:T(8,128)(2,1)S(1)}, bf16[128,1024]{1,0:T(8,128)(2,1)S(1)}, u32[]{:S(2)}, u32[]{:S(2)}) collective-permute-start(bf16[128,1024]{1,0:T(8,128)(2,1)S(1)} %pad_maximum_fusion.1.own_ref), channel_id=1, source_target_pairs={{0,32},{32,0},{64,96},{96,64},{128,160},{160,128},{192,224},{224,1... | collective-permute-start | bytes 786440 | tf_op jit(solution)/shard_map/ppermute | solution.py:14
  26.2 45.3 %all-to-all-start.1 = ((bf16[16,16,1024]{2,1,0:T(8,128)(2,1)}), bf16[16,16,1024]{2,1,0:T(8,128)(2,1)S(1)}, u32[]{:S(2)}, u32[]{:S(2)}) async-start(bf16[16,16,1024]{2,1,0:T(8,128)(2,1)} %broadcast_in_dim.42), calls=%async_computation.1 | async-start | bytes 1048576 | tf_op jit(solution)/shard_map/all_to_all | solution.py:47
  36.7 8.1 %collective-permute-start.2 = (bf16[128,1024]{1,0:T(8,128)(2,1)S(1)}, bf16[128,1024]{1,0:T(8,128)(2,1)S(1)}, u32[]{:S(2)}, u32[]{:S(2)}) collective-permute-start(bf16[128,1024]{1,0:T(8,128)(2,1)S(1)} %pad_maximum_fusion.1.own_ref), channel_id=1, source_target_pairs={{0,31},{1,2},{2,1},{3,4},{4,3},{5,6},{6,5},{7,8},{8,7},{9,10},{10,... | collective-permute-start | bytes 786440 | tf_op jit(solution)/shard_map/ppermute | solution.py:19
  40.5 16.0 %collective-permute-start.1 = (bf16[128,1024]{1,0:T(8,128)(2,1)S(1)}, bf16[128,1024]{1,0:T(8,128)(2,1)S(1)}, u32[]{:S(2)}, u32[]{:S(2)}) collective-permute-start(bf16[128,1024]{1,0:T(8,128)(2,1)S(1)} %collective-permute-done.pair_ref), channel_id=1, source_target_pairs={{0,64},{32,480},{64,128},{96,32},{128,192},{160,96},{192,256},{224... | collective-permute-start | bytes 786440 | tf_op jit(solution)/shard_map/ppermute | solution.py:24
  44.8 16.6 %copy-start.7 = (bf16[128,1024]{1,0:T(8,128)(2,1)}, bf16[128,1024]{1,0:T(8,128)(2,1)S(1)}, u32[]{:S(2)}) copy-start(bf16[128,1024]{1,0:T(8,128)(2,1)S(1)} %collective-permute-done.2.far_own_ref) | copy-start | bytes 786436
  56.5 29.5 %copy-start.13 = (bf16[1,1,128,512]{3,2,1,0:T(8,128)(2,1)S(1)}, bf16[1,1,128,512]{3,2,1,0:T(8,128)(2,1)}, u32[]{:S(2)}) copy-start(bf16[1,1,128,512]{3,2,1,0:T(8,128)(2,1)} %param.7) | copy-start | bytes 393220
  57.4 14.1 %collective-permute-start.5 = (bf16[2,128,1024]{2,1,0:T(8,128)(2,1)}, bf16[2,128,1024]{2,1,0:T(8,128)(2,1)S(1)}, u32[]{:S(2)}, u32[]{:S(2)}) collective-permute-start(bf16[2,128,1024]{2,1,0:T(8,128)(2,1)} %pad_maximum_fusion), channel_id=1, source_target_pairs={{0,31},{1,2},{2,1},{3,4},{4,3},{5,6},{6,5},{7,8},{8,7},{9,10},{10,... | collective-permute-start | bytes 1572872 | tf_op jit(solution)/shard_map/ppermute | solution.py:19
  61.4 23.0 %collective-permute-start.4 = (bf16[2,128,1024]{2,1,0:T(8,128)(2,1)}, bf16[2,128,1024]{2,1,0:T(8,128)(2,1)S(1)}, u32[]{:S(2)}, u32[]{:S(2)}) collective-permute-start(bf16[2,128,1024]{2,1,0:T(8,128)(2,1)} %pad_maximum_fusion), channel_id=1, source_target_pairs={{0,1},{1,0},{2,3},{3,2},{4,5},{5,4},{6,7},{7,6},{8,9},{9,8},{10,11... | collective-permute-start | bytes 1572872 | tf_op jit(solution)/shard_map/ppermute | solution.py:14
  71.5 13.7 %collective-permute-start.6 = (bf16[256,1024]{1,0:T(8,128)(2,1)S(1)}, bf16[256,1024]{1,0:T(8,128)(2,1)S(1)}, u32[]{:S(2)}, u32[]{:S(2)}) collective-permute-start(bf16[256,1024]{1,0:T(8,128)(2,1)S(1)} %bitcast.47), channel_id=1, source_target_pairs={{0,1},{1,0},{2,3},{3,2},{4,5},{5,4},{6,7},{7,6},{8,9},{9,8},{10,11... | collective-permute-start | bytes 1572872 | tf_op jit(solution)/shard_map/ppermute | solution.py:14
  80.3 3.4 %collective-permute-start.3 = (bf16[128,1024]{1,0:T(8,128)(2,1)S(1)}, bf16[128,1024]{1,0:T(8,128)(2,1)S(1)}, u32[]{:S(2)}, u32[]{:S(2)}) collective-permute-start(bf16[128,1024]{1,0:T(8,128)(2,1)S(1)} %pad_maximum_fusion.1.own_ref), channel_id=1, source_target_pairs={{0,1},{1,0},{2,3},{3,2},{4,5},{5,4},{6,7},{7,6},{8,9},{9,8},{10,11... | collective-permute-start | bytes 786440 | tf_op jit(solution)/shard_map/ppermute | solution.py:14
  83.7 0.7 copy-start.11
  84.4 0.8 copy-start.1
  85.2 0.8 copy-start.3
  86.0 1.0 copy-start.2
  87.1 1.0 copy-start.4
  88.1 0.9 copy-start.8
  89.1 0.9 copy-start.12
  90.0 0.9 copy-start.14
  100.9 5.3 %copy-start.5 = (bf16[2,128,1024]{2,1,0:T(8,128)(2,1)}, bf16[2,128,1024]{2,1,0:T(8,128)(2,1)S(1)}, u32[]{:S(2)}) copy-start(bf16[2,128,1024]{2,1,0:T(8,128)(2,1)S(1)} %get-tuple-element.32) | copy-start | bytes 1572868
  100.9 5.3 %copy-start.9 = (bf16[128,1024]{1,0:T(8,128)(2,1)}, bf16[128,1024]{1,0:T(8,128)(2,1)S(1)}, u32[]{:S(2)}) copy-start(bf16[128,1024]{1,0:T(8,128)(2,1)S(1)} %get-tuple-element.34) | copy-start | bytes 786436
  100.9 4.9 %collective-permute-start.7 = (bf16[640,1024]{1,0:T(8,128)(2,1)S(1)}, bf16[640,1024]{1,0:T(8,128)(2,1)S(1)}, u32[]{:S(2)}, u32[]{:S(2)}) collective-permute-start(bf16[640,1024]{1,0:T(8,128)(2,1)S(1)} %get-tuple-element.30), channel_id=1, source_target_pairs={{0,1},{1,0},{2,3},{3,2},{4,5},{5,4},{6,7},{7,6},{8,9},{9,8},{10,11... | collective-permute-start | bytes 3932168 | tf_op jit(solution)/shard_map/ppermute | solution.py:14
  106.1 5.4 %copy-start.6 = (bf16[2,128,1024]{2,1,0:T(8,128)(2,1)S(1)}, bf16[2,128,1024]{2,1,0:T(8,128)(2,1)}, u32[]{:S(2)}) copy-start(bf16[2,128,1024]{2,1,0:T(8,128)(2,1)} %copy-done.5) | copy-start | bytes 1572868
  107.1 20.2 %all-to-all-start.2 = ((bf16[16,16,1024]{2,1,0:T(8,128)(2,1)}), bf16[16,16,1024]{2,1,0:T(8,128)(2,1)}, u32[]{:S(2)}, u32[]{:S(2)}) async-start(bf16[16,16,1024]{2,1,0:T(8,128)(2,1)} %bitcast.54), calls=%async_computation.2 | async-start | bytes 1048576 | tf_op jit(solution)/shard_map/all_to_all | solution.py:47
  111.5 14.6 %collective-permute-start.8 = (bf16[2,128,1024]{2,1,0:T(8,128)(2,1)S(1)}, bf16[2,128,1024]{2,1,0:T(8,128)(2,1)}, u32[]{:S(2)}, u32[]{:S(2)}) collective-permute-start(bf16[2,128,1024]{2,1,0:T(8,128)(2,1)S(1)} %copy-done.6), channel_id=1, source_target_pairs={{0,31},{1,2},{2,1},{3,4},{4,3},{5,6},{6,5},{7,8},{8,7},{9,10},{10,... | collective-permute-start | bytes 1572872 | tf_op jit(solution)/shard_map/ppermute | solution.py:19
  115.1 25.1 %copy-start.10 = (bf16[128,1024]{1,0:T(8,128)(2,1)S(1)}, bf16[128,1024]{1,0:T(8,128)(2,1)}, u32[]{:S(2)}) copy-start(bf16[128,1024]{1,0:T(8,128)(2,1)} %copy-done.9) | copy-start | bytes 786436
  128.4 17.4 %collective-permute-start.10 = (bf16[128,1024]{1,0:T(8,128)(2,1)S(1)}, bf16[128,1024]{1,0:T(8,128)(2,1)S(1)}, u32[]{:S(2)}, u32[]{:S(2)}) collective-permute-start(bf16[128,1024]{1,0:T(8,128)(2,1)S(1)} %fusion.8), channel_id=1, source_target_pairs={{0,448},{32,96},{64,0},{96,160},{128,64},{160,224},{192,128},{224,... | collective-permute-start | bytes 786440 | tf_op jit(solution)/shard_map/ppermute | solution.py:24
  133.7 19.4 %all-to-all-start.3 = ((f32[16,8,128]{2,1,0:T(8,128)}), f32[16,8,128]{2,1,0:T(8,128)S(1)}, u32[]{:S(2)}, u32[]{:S(2)}) async-start(f32[16,8,128]{2,1,0:T(8,128)} %bitcast.27), calls=%async_computation.3 | async-start | bytes 131072 | tf_op jit(solution)/shard_map/all_to_all | solution.py:47
  140.2 13.5 %collective-permute-start.9 = (bf16[128,1024]{1,0:T(8,128)(2,1)S(1)}, bf16[128,1024]{1,0:T(8,128)(2,1)S(1)}, u32[]{:S(2)}, u32[]{:S(2)}) collective-permute-start(bf16[128,1024]{1,0:T(8,128)(2,1)S(1)} %copy-done.10), channel_id=1, source_target_pairs={{0,31},{1,2},{2,1},{3,4},{4,3},{5,6},{6,5},{7,8},{8,7},{9,10},{10,... | collective-permute-start | bytes 786440 | tf_op jit(solution)/shard_map/ppermute | solution.py:19
  147.0 18.7 %collective-permute-start.11 = (bf16[128,1024]{1,0:T(8,128)(2,1)S(1)}, bf16[128,1024]{1,0:T(8,128)(2,1)S(1)}, u32[]{:S(2)}, u32[]{:S(2)}) collective-permute-start(bf16[128,1024]{1,0:T(8,128)(2,1)S(1)} %fusion.3), channel_id=1, source_target_pairs={{0,32},{32,0},{64,96},{96,64},{128,160},{160,128},{192,224},{224,1... | collective-permute-start | bytes 786440 | tf_op jit(solution)/shard_map/ppermute | solution.py:14

commit v5 on v4

--- a/solution.py
+++ b/solution.py
@@ -177,7 +177,7 @@
             pltpu.VMEM((keys, 2 * rows), jnp.float32),
             pltpu.VMEM((keys, 2 * rows), jnp.float32),
         ],
-        compiler_params=pltpu.CompilerParams(vmem_limit_bytes=40 * 2**20),
+        compiler_params=pltpu.CompilerParams(vmem_limit_bytes=50 * 2**20),
         cost_estimate=pl.CostEstimate(
             flops=5 * work, bytes_accessed=12 * 2**20, transcendentals=rows * keys * width // HEAD_DIM
         ),
@@ -212,8 +212,8 @@
     coarse, paired, again = lax.optimization_barrier((coarse, paired, own))
     skipped = skip_row(paired, 2)
     near_own, far_own = exchange(again, "col", 1), to_far(again, "col")
+    coarse, skipped, far_own = lax.optimization_barrier((coarse, skipped, far_own))
     kept = gather_second(coarse)
-    skipped, far_own = lax.optimization_barrier((skipped, far_own))
     lines = jnp.stack([paired, skipped])
     near, far = exchange(lines, "col", 1), to_far(lines, "col")
     kept, far = lax.optimization_barrier((kept, far))
@@ -228,9 +228,10 @@
     line = own_terms + core_back[: 3 * rows].reshape(own_terms.shape)
     skipped_line = (line[2] + far_back[1].astype(high)).astype(low)
     coarse_sum = scatter_second(half)
-    coarse_sum, skipped_line, far_own_terms = lax.optimization_barrier((coarse_sum, skipped_line, far_own_terms))
+    skipped_line, far_own_terms = lax.optimization_barrier((skipped_line, far_own_terms))
+    forwarded = skip_row(skipped_line, -2).astype(high)
+    coarse_sum, forwarded = lax.optimization_barrier((coarse_sum, forwarded))
     coarse_sum = scatter_first(coarse_sum)
-    forwarded = skip_row(skipped_line, -2).astype(high)
     paired_line = (line[1] + far_back[0].astype(high) + forwarded).astype(low)
     returned = exchange(paired_line, "row", 1).astype(high)
     total = (line[0] + to_far(far_own_terms, "col").astype(high) + returned).astype(low)

time: 170 us -> 155 us (0.912)
  the two profiles are of different devices: /device:TPU:1 before, /device:TPU:23 now
where the time goes in v5:
time: 155 us; the launch traced here: 154 us
  starting transfers between devices  71.1 us (46%)
  waiting for transfers between devices  41.3 us (27%)
  blocking collectives  14.2 us (9%)
  Pallas kernels  11.3 us (7%)
  other arithmetic  7.88 us (5%)
  local copies, waits for them, and re-layouts  7.74 us (5%)
    all_to_all x3, starting transfers between devices, deal(): lax.all_to_all(block, ('row', 'col'), 0, 0, axis_index_groups=groups, til...  25.1 us
    ppermute x6, starting transfers between devices, exchange(): lax.ppermute(block, axis, [(i, i ^ bit) for i in range(lax.axis_size(axis...  19.4 us
    ppermute x4, starting transfers between devices, to_far(): lax.ppermute(block, axis, [(i, (i + (1 if i % 2 else -1)) % size) for i i...  18.3 us
    ppermute x2, waiting for transfers between devices, skip_row(): lax.ppermute(block, 'row', [(i, (i + (-way if i % 2 else way)) % size) fo...  15.6 us
    ppermute x6, waiting for transfers between devices, exchange(): lax.ppermute(block, axis, [(i, i ^ bit) for i in range(lax.axis_size(axis...  14.7 us
    all_to_all x1, blocking collectives, deal(): lax.all_to_all(block, ('row', 'col'), 0, 0, axis_index_groups=groups, til...  14.2 us
    pallas_call x1, Pallas kernels, attention(): pl.pallas_call(attention_kernel, out_shape=(jax.ShapeDtypeStruct((rows, w...  11.3 us
    ppermute x4, waiting for transfers between devices, to_far(): lax.ppermute(block, axis, [(i, (i + (1 if i % 2 else -1)) % size) for i i...  10.9 us
  transfers between devices with their start and end apart: 15, of which 6 were waited for; matrix products, arithmetic and copies ran while one was open for 6% of the time, Pallas kernels for 0%

profile of v5, /device:TPU:23, one launch (start us, length us, event | category | flops | bytes accessed | tf_op | source)
XLA Modules:
  0.0 154.3 jit_solution(5092860662662838376)
XLA Ops:
  0.6 0.0 copy-start
  0.6 1.0 pad_maximum_fusion.1.own_ref
  1.6 5.7 %collective-permute-start = (bf16[128,1024]{1,0:T(8,128)(2,1)S(1)}, bf16[128,1024]{1,0:T(8,128)(2,1)S(1)}, u32[]{:S(2)}, u32[]{:S(2)}) collective-permute-start(bf16[128,1024]{1,0:T(8,128)(2,1)S(1)} %pad_maximum_fusion.1.own_ref), channel_id=1, source_target_pairs={{0,32},{32,0},{64,96},{96,64},{128,160},{160,128},{192,224},{224,1... | collective-permute-start | bytes 786440 | tf_op jit(solution)/shard_map/ppermute | solution.py:14
  7.3 0.7 maximum_reduce_fusion
  8.0 14.2 %all_to_all.20 = bf16[16,8,128]{2,1,0:T(8,128)(2,1)S(1)} all-to-all(bf16[16,8,128]{2,1,0:T(8,128)(2,1)S(1)} %broadcast_in_dim.41), channel_id=1, replica_groups={{0,2,4,6,32,34,36,38,16,18,20,22,48,50,52,54},{1,3,5,7,33,35,37,39,17,1..., dimensions={0} | all-to-all | bytes 65536 | tf_op jit(solution)/shard_map/all_to_all | solution.py:47
  22.2 0.0 collective-permute-done.pair_ref
  22.3 4.3 %collective-permute-start.2 = (bf16[128,1024]{1,0:T(8,128)(2,1)S(1)}, bf16[128,1024]{1,0:T(8,128)(2,1)S(1)}, u32[]{:S(2)}, u32[]{:S(2)}) collective-permute-start(bf16[128,1024]{1,0:T(8,128)(2,1)S(1)} %pad_maximum_fusion.1.own_ref), channel_id=1, source_target_pairs={{0,31},{1,2},{2,1},{3,4},{4,3},{5,6},{6,5},{7,8},{8,7},{9,10},{10,... | collective-permute-start | bytes 786440 | tf_op jit(solution)/shard_map/ppermute | solution.py:19
  26.6 4.0 %collective-permute-start.1 = (bf16[128,1024]{1,0:T(8,128)(2,1)S(1)}, bf16[128,1024]{1,0:T(8,128)(2,1)S(1)}, u32[]{:S(2)}, u32[]{:S(2)}) collective-permute-start(bf16[128,1024]{1,0:T(8,128)(2,1)S(1)} %collective-permute-done.pair_ref), channel_id=1, source_target_pairs={{0,64},{32,480},{64,128},{96,32},{128,192},{160,96},{192,256},{224... | collective-permute-start | bytes 786440 | tf_op jit(solution)/shard_map/ppermute | solution.py:24
  30.6 0.9 collective-permute-done.2.far_own_ref
  31.5 11.3 %collective-permute-done.1.skip_ref = bf16[128,1024]{1,0:T(8,128)(2,1)S(1)} collective-permute-done((bf16[128,1024]{1,0:T(8,128)(2,1)S(1)}, bf16[128,1024]{1,0:T(8,128)(2,1)S(1)}, u32[]{:S(2)}, u32[]{:S(2)}) %collective-permute-start.1) | collective-permute-done | bytes 262176 | tf_op jit(solution)/shard_map/ppermute | solution.py:24
  42.8 0.9 broadcast_in_dim.42
  43.7 5.4 %all-to-all-start.1 = ((bf16[16,16,1024]{2,1,0:T(8,128)(2,1)}), bf16[16,16,1024]{2,1,0:T(8,128)(2,1)S(1)}, u32[]{:S(2)}, u32[]{:S(2)}) async-start(bf16[16,16,1024]{2,1,0:T(8,128)(2,1)} %broadcast_in_dim.42), calls=%async_computation.1 | async-start | bytes 1048576 | tf_op jit(solution)/shard_map/all_to_all | solution.py:47
  49.1 0.9 pad_maximum_fusion
  49.9 2.7 %collective-permute-start.5 = (bf16[2,128,1024]{2,1,0:T(8,128)(2,1)}, bf16[2,128,1024]{2,1,0:T(8,128)(2,1)S(1)}, u32[]{:S(2)}, u32[]{:S(2)}) collective-permute-start(bf16[2,128,1024]{2,1,0:T(8,128)(2,1)} %pad_maximum_fusion), channel_id=1, source_target_pairs={{0,31},{1,2},{2,1},{3,4},{4,3},{5,6},{6,5},{7,8},{8,7},{9,10},{10,... | collective-permute-start | bytes 1572872 | tf_op jit(solution)/shard_map/ppermute | solution.py:19
  52.6 0.1 compare_and_fusion.1
  52.7 0.1 compare_and_fusion
  52.8 2.0 %collective-permute-start.4 = (bf16[2,128,1024]{2,1,0:T(8,128)(2,1)}, bf16[2,128,1024]{2,1,0:T(8,128)(2,1)S(1)}, u32[]{:S(2)}, u32[]{:S(2)}) collective-permute-start(bf16[2,128,1024]{2,1,0:T(8,128)(2,1)} %pad_maximum_fusion), channel_id=1, source_target_pairs={{0,1},{1,0},{2,3},{3,2},{4,5},{5,4},{6,7},{7,6},{8,9},{9,8},{10,11... | collective-permute-start | bytes 1572872 | tf_op jit(solution)/shard_map/ppermute | solution.py:14
  54.8 10.0 %collective-permute-done.5.far_ref = bf16[2,128,1024]{2,1,0:T(8,128)(2,1)S(1)} collective-permute-done((bf16[2,128,1024]{2,1,0:T(8,128)(2,1)}, bf16[2,128,1024]{2,1,0:T(8,128)(2,1)S(1)}, u32[]{:S(2)}, u32[]{:S(2)}) %collective-permute-start.5) | collective-permute-done | bytes 524320 | tf_op jit(solution)/shard_map/ppermute | solution.py:19
  64.8 0.0 all-to-all-done.1
  64.8 2.1 %collective-permute-start.6 = (bf16[256,1024]{1,0:T(8,128)(2,1)S(1)}, bf16[256,1024]{1,0:T(8,128)(2,1)}, u32[]{:S(2)}, u32[]{:S(2)}) collective-permute-start(bf16[256,1024]{1,0:T(8,128)(2,1)S(1)} %bitcast.47), channel_id=1, source_target_pairs={{0,1},{1,0},{2,3},{3,2},{4,5},{5,4},{6,7},{7,6},{8,9},{9,8},{10,11... | collective-permute-start | bytes 1572872 | tf_op jit(solution)/shard_map/ppermute | solution.py:14
  66.8 0.1 broadcast_or_fusion
  66.9 0.1 reshape.193
  67.0 0.0 copy-done
  67.0 0.7 gather_fusion
  67.7 0.1 reshape.196
  67.8 2.2 %collective-permute-start.3 = (bf16[128,1024]{1,0:T(8,128)(2,1)S(1)}, bf16[128,1024]{1,0:T(8,128)(2,1)S(1)}, u32[]{:S(2)}, u32[]{:S(2)}) collective-permute-start(bf16[128,1024]{1,0:T(8,128)(2,1)S(1)} %pad_maximum_fusion.1.own_ref), channel_id=1, source_target_pairs={{0,1},{1,0},{2,3},{3,2},{4,5},{5,4},{6,7},{7,6},{8,9},{9,8},{10,11... | collective-permute-start | bytes 786440 | tf_op jit(solution)/shard_map/ppermute | solution.py:14
  70.1 0.1 and_select_fusion
  70.1 0.1 select_n.39
  70.2 0.1 pad_add_fusion.2.counts
  70.3 0.9 collective-permute-done.3.near_own_ref
  71.2 0.7 copy-done.1
  71.9 0.0 collective-permute-done.4.near_ref
  71.9 0.0 collective-permute-done.6.other_ref
  71.9 0.0 copy-done.3
  71.9 0.9 copy-done.2
  72.9 0.9 copy-done.4
  73.8 11.3 %shard_map.110 = (bf16[128,512]{1,0:T(8,128)(2,1)}, f32[3,128,1024]{2,1,0:T(8,128)}, bf16[640,1024]{1,0:T(8,128)(2,1)}, bf16[128,1024]{1,0:T(8,128)(2,1)S(1)}, b...) custom-call(s32[10]{0:T(128)S(1)} %pad_add_fusion.2.counts, bf16[128,512]{1,0:T(8,128)(2,1)S(1)} %bitcast.51, ...), custom_call_target="tpu_custom_call" | custom-call | flops 1090519040 | bytes 12582912 | tf_op jit(solution)/shard_map/pallas_call | solution.py:164
  85.1 2.3 %collective-permute-start.7 = (bf16[640,1024]{1,0:T(8,128)(2,1)}, bf16[640,1024]{1,0:T(8,128)(2,1)S(1)}, u32[]{:S(2)}, u32[]{:S(2)}) collective-permute-start(bf16[640,1024]{1,0:T(8,128)(2,1)} %get-tuple-element.33), channel_id=1, source_target_pairs={{0,1},{1,0},{2,3},{3,2},{4,5},{5,4},{6,7},{7,6},{8,9},{9,8},{10,11... | collective-permute-start | bytes 3932168 | tf_op jit(solution)/shard_map/ppermute | solution.py:14
  87.3 0.0 copy-start.6
  87.3 5.4 %collective-permute-start.8 = (bf16[2,128,1024]{2,1,0:T(8,128)(2,1)S(1)}, bf16[2,128,1024]{2,1,0:T(8,128)(2,1)}, u32[]{:S(2)}, u32[]{:S(2)}) collective-permute-start(bf16[2,128,1024]{2,1,0:T(8,128)(2,1)S(1)} %get-tuple-element.34), channel_id=1, source_target_pairs={{0,31},{1,2},{2,1},{3,4},{4,3},{5,6},{6,5},{7,8},{8,7},{9,10},{10,... | collective-permute-start | bytes 1572872 | tf_op jit(solution)/shard_map/ppermute | solution.py:19
  92.7 0.0 collective-permute-done.7
  92.7 0.3 convert_element_type.38
  93.0 0.9 fusion
  94.0 8.0 %all-to-all-start.2 = ((bf16[16,16,1024]{2,1,0:T(8,128)(2,1)}), bf16[16,16,1024]{2,1,0:T(8,128)(2,1)}, u32[]{:S(2)}, u32[]{:S(2)}) async-start(bf16[16,16,1024]{2,1,0:T(8,128)(2,1)} %bitcast.18), calls=%async_computation.2 | async-start | bytes 1048576 | tf_op jit(solution)/shard_map/all_to_all | solution.py:47
  102.0 0.2 slice.50
  102.2 1.2 copy-done.5
  103.4 0.3 add.69
  103.7 0.0 collective-permute-done.8
  103.7 1.0 fusion.8
  104.7 4.3 %collective-permute-start.10 = (bf16[128,1024]{1,0:T(8,128)(2,1)S(1)}, bf16[128,1024]{1,0:T(8,128)(2,1)S(1)}, u32[]{:S(2)}, u32[]{:S(2)}) collective-permute-start(bf16[128,1024]{1,0:T(8,128)(2,1)S(1)} %fusion.8), channel_id=1, source_target_pairs={{0,448},{32,96},{64,0},{96,160},{128,64},{160,224},{192,128},{224,... | collective-permute-start | bytes 786440 | tf_op jit(solution)/shard_map/ppermute | solution.py:24
  109.0 6.0 %collective-permute-start.9 = (bf16[128,1024]{1,0:T(8,128)(2,1)S(1)}, bf16[128,1024]{1,0:T(8,128)(2,1)S(1)}, u32[]{:S(2)}, u32[]{:S(2)}) collective-permute-start(bf16[128,1024]{1,0:T(8,128)(2,1)S(1)} %get-tuple-element.36), channel_id=1, source_target_pairs={{0,31},{1,2},{2,1},{3,4},{4,3},{5,6},{6,5},{7,8},{8,7},{9,10},{10,... | collective-permute-start | bytes 786440 | tf_op jit(solution)/shard_map/ppermute | solution.py:19
  115.0 4.3 %collective-permute-done.10 = bf16[128,1024]{1,0:T(8,128)(2,1)S(1)} collective-permute-done((bf16[128,1024]{1,0:T(8,128)(2,1)S(1)}, bf16[128,1024]{1,0:T(8,128)(2,1)S(1)}, u32[]{:S(2)}, u32[]{:S(2)}) %collective-permute-start.10) | collective-permute-done | bytes 262176 | tf_op jit(solution)/shard_map/ppermute | solution.py:24
  119.3 0.0 all-to-all-done.2
  119.4 1.1 convert_reduce_fusion
  120.5 0.6 copy.13
  121.1 11.7 %all-to-all-start.3 = ((f32[16,8,128]{2,1,0:T(8,128)}), f32[16,8,128]{2,1,0:T(8,128)S(1)}, u32[]{:S(2)}, u32[]{:S(2)}) async-start(f32[16,8,128]{2,1,0:T(8,128)} %bitcast.27), calls=%async_computation.3 | async-start | bytes 131072 | tf_op jit(solution)/shard_map/all_to_all | solution.py:47
  132.8 1.1 fusion.3
  133.9 5.2 %collective-permute-start.11 = (bf16[128,1024]{1,0:T(8,128)(2,1)S(1)}, bf16[128,1024]{1,0:T(8,128)(2,1)S(1)}, u32[]{:S(2)}, u32[]{:S(2)}) collective-permute-start(bf16[128,1024]{1,0:T(8,128)(2,1)S(1)} %fusion.3), channel_id=1, source_target_pairs={{0,32},{32,0},{64,96},{96,64},{128,160},{160,128},{192,224},{224,1... | collective-permute-start | bytes 786440 | tf_op jit(solution)/shard_map/ppermute | solution.py:14
  139.1 0.0 all-to-all-done.3
  139.1 0.6 fusion.13
  139.7 0.0 collective-permute-done.9
  139.7 13.8 %collective-permute-done.11 = bf16[128,1024]{1,0:T(8,128)(2,1)S(1)} collective-permute-done((bf16[128,1024]{1,0:T(8,128)(2,1)S(1)}, bf16[128,1024]{1,0:T(8,128)(2,1)S(1)}, u32[]{:S(2)}, u32[]{:S(2)}) %collective-permute-start.11) | collective-permute-done | bytes 262176 | tf_op jit(solution)/shard_map/ppermute | solution.py:14
  153.5 0.1 fusion.7
  153.6 0.7 slice_bitcast_fusion.1
  (11 shorter events, 0.1 us)
Async XLA Ops:
  0.6 66.4 %copy-start = (s32[16,32]{1,0:T(8,128)S(1)}, s32[16,32]{1,0:T(8,128)}, u32[]{:S(2)}) copy-start(s32[16,32]{1,0:T(8,128)} %param.13) | copy-start | bytes 6148
  1.6 20.6 %collective-permute-start = (bf16[128,1024]{1,0:T(8,128)(2,1)S(1)}, bf16[128,1024]{1,0:T(8,128)(2,1)S(1)}, u32[]{:S(2)}, u32[]{:S(2)}) collective-permute-start(bf16[128,1024]{1,0:T(8,128)(2,1)S(1)} %pad_maximum_fusion.1.own_ref), channel_id=1, source_target_pairs={{0,32},{32,0},{64,96},{96,64},{128,160},{160,128},{192,224},{224,1... | collective-permute-start | bytes 786440 | tf_op jit(solution)/shard_map/ppermute | solution.py:14
  22.3 9.2 %collective-permute-start.2 = (bf16[128,1024]{1,0:T(8,128)(2,1)S(1)}, bf16[128,1024]{1,0:T(8,128)(2,1)S(1)}, u32[]{:S(2)}, u32[]{:S(2)}) collective-permute-start(bf16[128,1024]{1,0:T(8,128)(2,1)S(1)} %pad_maximum_fusion.1.own_ref), channel_id=1, source_target_pairs={{0,31},{1,2},{2,1},{3,4},{4,3},{5,6},{6,5},{7,8},{8,7},{9,10},{10,... | collective-permute-start | bytes 786440 | tf_op jit(solution)/shard_map/ppermute | solution.py:19
  26.6 16.2 %collective-permute-start.1 = (bf16[128,1024]{1,0:T(8,128)(2,1)S(1)}, bf16[128,1024]{1,0:T(8,128)(2,1)S(1)}, u32[]{:S(2)}, u32[]{:S(2)}) collective-permute-start(bf16[128,1024]{1,0:T(8,128)(2,1)S(1)} %collective-permute-done.pair_ref), channel_id=1, source_target_pairs={{0,64},{32,480},{64,128},{96,32},{128,192},{160,96},{192,256},{224... | collective-permute-start | bytes 786440 | tf_op jit(solution)/shard_map/ppermute | solution.py:24
  43.7 21.1 %all-to-all-start.1 = ((bf16[16,16,1024]{2,1,0:T(8,128)(2,1)}), bf16[16,16,1024]{2,1,0:T(8,128)(2,1)S(1)}, u32[]{:S(2)}, u32[]{:S(2)}) async-start(bf16[16,16,1024]{2,1,0:T(8,128)(2,1)} %broadcast_in_dim.42), calls=%async_computation.1 | async-start | bytes 1048576 | tf_op jit(solution)/shard_map/all_to_all | solution.py:47
  49.1 22.9 %copy-start.3 = (bf16[1,1,128,512]{3,2,1,0:T(8,128)(2,1)S(1)}, bf16[1,1,128,512]{3,2,1,0:T(8,128)(2,1)}, u32[]{:S(2)}) copy-start(bf16[1,1,128,512]{3,2,1,0:T(8,128)(2,1)} %param.7) | copy-start | bytes 393220
  49.9 14.9 %collective-permute-start.5 = (bf16[2,128,1024]{2,1,0:T(8,128)(2,1)}, bf16[2,128,1024]{2,1,0:T(8,128)(2,1)S(1)}, u32[]{:S(2)}, u32[]{:S(2)}) collective-permute-start(bf16[2,128,1024]{2,1,0:T(8,128)(2,1)} %pad_maximum_fusion), channel_id=1, source_target_pairs={{0,31},{1,2},{2,1},{3,4},{4,3},{5,6},{6,5},{7,8},{8,7},{9,10},{10,... | collective-permute-start | bytes 1572872 | tf_op jit(solution)/shard_map/ppermute | solution.py:19
  52.8 19.1 %collective-permute-start.4 = (bf16[2,128,1024]{2,1,0:T(8,128)(2,1)}, bf16[2,128,1024]{2,1,0:T(8,128)(2,1)S(1)}, u32[]{:S(2)}, u32[]{:S(2)}) collective-permute-start(bf16[2,128,1024]{2,1,0:T(8,128)(2,1)} %pad_maximum_fusion), channel_id=1, source_target_pairs={{0,1},{1,0},{2,3},{3,2},{4,5},{5,4},{6,7},{7,6},{8,9},{9,8},{10,11... | collective-permute-start | bytes 1572872 | tf_op jit(solution)/shard_map/ppermute | solution.py:14
  64.8 7.1 %collective-permute-start.6 = (bf16[256,1024]{1,0:T(8,128)(2,1)S(1)}, bf16[256,1024]{1,0:T(8,128)(2,1)}, u32[]{:S(2)}, u32[]{:S(2)}) collective-permute-start(bf16[256,1024]{1,0:T(8,128)(2,1)S(1)} %bitcast.47), channel_id=1, source_target_pairs={{0,1},{1,0},{2,3},{3,2},{4,5},{5,4},{6,7},{7,6},{8,9},{9,8},{10,11... | collective-permute-start | bytes 1572872 | tf_op jit(solution)/shard_map/ppermute | solution.py:14
  67.8 3.4 %collective-permute-start.3 = (bf16[128,1024]{1,0:T(8,128)(2,1)S(1)}, bf16[128,1024]{1,0:T(8,128)(2,1)S(1)}, u32[]{:S(2)}, u32[]{:S(2)}) collective-permute-start(bf16[128,1024]{1,0:T(8,128)(2,1)S(1)} %pad_maximum_fusion.1.own_ref), channel_id=1, source_target_pairs={{0,1},{1,0},{2,3},{3,2},{4,5},{5,4},{6,7},{7,6},{8,9},{9,8},{10,11... | collective-permute-start | bytes 786440 | tf_op jit(solution)/shard_map/ppermute | solution.py:14
  71.2 0.7 copy-start.1
  71.9 1.0 copy-start.2
  72.9 0.9 copy-start.4
  85.1 7.6 %collective-permute-start.7 = (bf16[640,1024]{1,0:T(8,128)(2,1)}, bf16[640,1024]{1,0:T(8,128)(2,1)S(1)}, u32[]{:S(2)}, u32[]{:S(2)}) collective-permute-start(bf16[640,1024]{1,0:T(8,128)(2,1)} %get-tuple-element.33), channel_id=1, source_target_pairs={{0,1},{1,0},{2,3},{3,2},{4,5},{5,4},{6,7},{7,6},{8,9},{9,8},{10,11... | collective-permute-start | bytes 3932168 | tf_op jit(solution)/shard_map/ppermute | solution.py:14
  87.3 5.7 %copy-start.6 = (f32[256,1024]{1,0:T(8,128)S(1)}, f32[256,1024]{1,0:T(8,128)}, u32[]{:S(2)}) copy-start(f32[256,1024]{1,0:T(8,128)} %get-tuple-element.37) | copy-start | bytes 3145732
  87.3 16.3 %collective-permute-start.8 = (bf16[2,128,1024]{2,1,0:T(8,128)(2,1)S(1)}, bf16[2,128,1024]{2,1,0:T(8,128)(2,1)}, u32[]{:S(2)}, u32[]{:S(2)}) collective-permute-start(bf16[2,128,1024]{2,1,0:T(8,128)(2,1)S(1)} %get-tuple-element.34), channel_id=1, source_target_pairs={{0,31},{1,2},{2,1},{3,4},{4,3},{5,6},{6,5},{7,8},{8,7},{9,10},{10,... | collective-permute-start | bytes 1572872 | tf_op jit(solution)/shard_map/ppermute | solution.py:19
  94.0 25.4 %all-to-all-start.2 = ((bf16[16,16,1024]{2,1,0:T(8,128)(2,1)}), bf16[16,16,1024]{2,1,0:T(8,128)(2,1)}, u32[]{:S(2)}, u32[]{:S(2)}) async-start(bf16[16,16,1024]{2,1,0:T(8,128)(2,1)} %bitcast.18), calls=%async_computation.2 | async-start | bytes 1048576 | tf_op jit(solution)/shard_map/all_to_all | solution.py:47
  102.0 1.4 copy-start.5
  104.7 14.6 %collective-permute-start.10 = (bf16[128,1024]{1,0:T(8,128)(2,1)S(1)}, bf16[128,1024]{1,0:T(8,128)(2,1)S(1)}, u32[]{:S(2)}, u32[]{:S(2)}) collective-permute-start(bf16[128,1024]{1,0:T(8,128)(2,1)S(1)} %fusion.8), channel_id=1, source_target_pairs={{0,448},{32,96},{64,0},{96,160},{128,64},{160,224},{192,128},{224,... | collective-permute-start | bytes 786440 | tf_op jit(solution)/shard_map/ppermute | solution.py:24
  109.0 30.7 %collective-permute-start.9 = (bf16[128,1024]{1,0:T(8,128)(2,1)S(1)}, bf16[128,1024]{1,0:T(8,128)(2,1)S(1)}, u32[]{:S(2)}, u32[]{:S(2)}) collective-permute-start(bf16[128,1024]{1,0:T(8,128)(2,1)S(1)} %get-tuple-element.36), channel_id=1, source_target_pairs={{0,31},{1,2},{2,1},{3,4},{4,3},{5,6},{6,5},{7,8},{8,7},{9,10},{10,... | collective-permute-start | bytes 786440 | tf_op jit(solution)/shard_map/ppermute | solution.py:19
  121.1 18.0 %all-to-all-start.3 = ((f32[16,8,128]{2,1,0:T(8,128)}), f32[16,8,128]{2,1,0:T(8,128)S(1)}, u32[]{:S(2)}, u32[]{:S(2)}) async-start(f32[16,8,128]{2,1,0:T(8,128)} %bitcast.27), calls=%async_computation.3 | async-start | bytes 131072 | tf_op jit(solution)/shard_map/all_to_all | solution.py:47
  133.9 19.6 %collective-permute-start.11 = (bf16[128,1024]{1,0:T(8,128)(2,1)S(1)}, bf16[128,1024]{1,0:T(8,128)(2,1)S(1)}, u32[]{:S(2)}, u32[]{:S(2)}) collective-permute-start(bf16[128,1024]{1,0:T(8,128)(2,1)S(1)} %fusion.3), channel_id=1, source_target_pairs={{0,32},{32,0},{64,96},{96,64},{128,160},{160,128},{192,224},{224,1... | collective-permute-start | bytes 786440 | tf_op jit(solution)/shard_map/ppermute | solution.py:14

commit v6 on v4

--- a/solution.py
+++ b/solution.py
@@ -75,16 +75,16 @@
 
 
 def attention_kernel(
-    counts, q_ref, g_ref, own_ref, pair_ref, skip_ref, near_own_ref, near_ref, far_own_ref, far_ref, kept_ref, other_ref,
-    dq_ref, own_out, core_out, far_own_out, far_out, kept_out, p_ref, dp_ref,
+    counts, q_ref, g_ref, own_ref, near_ref, far_ref, kept_ref, other_ref,
+    dq_ref, own_out, core_out, far_out, kept_out, p_ref, dp_ref,
 ):
     rows, width = q_ref.shape
     coarse_count = kept_ref.shape[0]
     step = min(rows, coarse_count)
-    fine_in = (own_ref, pair_ref, skip_ref, near_own_ref, near_ref.at[0], near_ref.at[1], far_own_ref, far_ref.at[0], far_ref.at[1])
+    fine_in = [ref.at[at] for ref in (own_ref, near_ref, far_ref) for at in range(3)]
     fine_out = [own_out.at[at] for at in range(3)]
     fine_out += [core_out.at[at * rows : (at + 1) * rows] for at in range(3)]
-    fine_out += [far_own_out, far_out.at[0], far_out.at[1]]
+    fine_out += [far_out.at[at] for at in range(3)]
     tiles = [(fine_in[at], fine_out[at], rows, counts[at]) for at in range(9)]
     for ref, out, ahead in ((kept_ref, kept_out, 0), (other_ref, core_out, 3 * rows)):
         for start in range(0, coarse_count, step):
@@ -167,17 +167,16 @@
             jax.ShapeDtypeStruct((rows, width), jnp.bfloat16),
             jax.ShapeDtypeStruct((3, rows, double), held),
             jax.ShapeDtypeStruct((3 * rows + coarse_count, double), sent),
-            jax.ShapeDtypeStruct((rows, double), sent),
-            jax.ShapeDtypeStruct((2, rows, double), sent),
+            jax.ShapeDtypeStruct((3, rows, double), sent),
             jax.ShapeDtypeStruct((coarse_count, double), held),
         ),
         in_specs=[pl.BlockSpec(memory_space=pltpu.SMEM)] + [in_vmem] * (2 + len(blocks)),
-        out_specs=(in_vmem,) * 6,
+        out_specs=(in_vmem,) * 5,
         scratch_shapes=[
             pltpu.VMEM((keys, 2 * rows), jnp.float32),
             pltpu.VMEM((keys, 2 * rows), jnp.float32),
         ],
-        compiler_params=pltpu.CompilerParams(vmem_limit_bytes=40 * 2**20),
+        compiler_params=pltpu.CompilerParams(vmem_limit_bytes=48 * 2**20),
         cost_estimate=pl.CostEstimate(
             flops=5 * work, bytes_accessed=12 * 2**20, transcendentals=rows * keys * width // HEAD_DIM
         ),
@@ -209,31 +208,27 @@
     token = jnp.concatenate([coarse_keys, coarse_values], axis=-1)
     paired = exchange(own, "row", 1)
     coarse = gather_first(token)
-    coarse, paired, again = lax.optimization_barrier((coarse, paired, own))
-    skipped = skip_row(paired, 2)
-    near_own, far_own = exchange(again, "col", 1), to_far(again, "col")
+    coarse, paired = lax.optimization_barrier((coarse, paired))
+    column = jnp.stack([own, paired, skip_row(paired, 2)])
+    near, far = exchange(column, "col", 1), to_far(column, "col")
+    coarse, near = lax.optimization_barrier((coarse, near))
     kept = gather_second(coarse)
-    skipped, far_own = lax.optimization_barrier((skipped, far_own))
-    lines = jnp.stack([paired, skipped])
-    near, far = exchange(lines, "col", 1), to_far(lines, "col")
-    kept, far = lax.optimization_barrier((kept, far))
     other = exchange(kept, "col", 1)
-    grad_q, own_terms, core_terms, far_own_terms, far_terms, kept_terms = attention(
-        counts, fine_queries[0, 0], grad_out[0, 0], own, paired, skipped, near_own, near, far_own, far, kept, other
+    grad_q, own_terms, core_terms, far_terms, kept_terms = attention(
+        counts, fine_queries[0, 0], grad_out[0, 0], column, near, far, kept, other
     )
     rows = own.shape[0]
     far_back = to_far(far_terms, "col")
     core_back = exchange(core_terms, "col", 1).astype(high)
     half = (kept_terms + core_back[3 * rows :]).astype(low)
     line = own_terms + core_back[: 3 * rows].reshape(own_terms.shape)
-    skipped_line = (line[2] + far_back[1].astype(high)).astype(low)
     coarse_sum = scatter_second(half)
-    coarse_sum, skipped_line, far_own_terms = lax.optimization_barrier((coarse_sum, skipped_line, far_own_terms))
+    line = line + far_back.astype(high)
+    coarse_sum, line = lax.optimization_barrier((coarse_sum, line))
+    forwarded = skip_row(line[2].astype(low), -2).astype(high)
     coarse_sum = scatter_first(coarse_sum)
-    forwarded = skip_row(skipped_line, -2).astype(high)
-    paired_line = (line[1] + far_back[0].astype(high) + forwarded).astype(low)
-    returned = exchange(paired_line, "row", 1).astype(high)
-    total = (line[0] + to_far(far_own_terms, "col").astype(high) + returned).astype(low)
+    returned = exchange((line[1] + forwarded).astype(low), "row", 1).astype(high)
+    total = (line[0] + returned).astype(low)
     return (
         grad_q[None, None],
         total[None, None, :, :width],

time: 170 us -> 149 us (0.88)
  the two profiles are of different devices: /device:TPU:1 before, /device:TPU:22 now
where the time goes in v6:
time: 149 us; the launch traced here: 148 us
  starting transfers between devices  56.8 us (38%)
  waiting for transfers between devices  53.3 us (36%)
  blocking collectives  14.5 us (10%)
  Pallas kernels  10.7 us (7%)
  other arithmetic  7.04 us (5%)
  local copies, waits for them, and re-layouts  4.88 us (3%)
    all_to_all x3, starting transfers between devices, deal(): lax.all_to_all(block, ('row', 'col'), 0, 0, axis_index_groups=groups, til...  25.1 us
    all_to_all x3, waiting for transfers between devices, deal(): lax.all_to_all(block, ('row', 'col'), 0, 0, axis_index_groups=groups, til...  19.2 us
    ppermute x5, starting transfers between devices, exchange(): lax.ppermute(block, axis, [(i, i ^ bit) for i in range(lax.axis_size(axis...  17.2 us
    ppermute x5, waiting for transfers between devices, exchange(): lax.ppermute(block, axis, [(i, i ^ bit) for i in range(lax.axis_size(axis...  14.5 us
    all_to_all x1, blocking collectives, deal(): lax.all_to_all(block, ('row', 'col'), 0, 0, axis_index_groups=groups, til...  14.5 us
    ppermute x2, waiting for transfers between devices, skip_row(): lax.ppermute(block, 'row', [(i, (i + (-way if i % 2 else way)) % size) fo...  12.4 us
    pallas_call x1, Pallas kernels, attention(): pl.pallas_call(attention_kernel, out_shape=(jax.ShapeDtypeStruct((rows, w...  10.7 us
    ppermute x2, starting transfers between devices, skip_row(): lax.ppermute(block, 'row', [(i, (i + (-way if i % 2 else way)) % size) fo...  9.81 us
  transfers between devices with their start and end apart: 12, of which 9 were waited for; matrix products, arithmetic and copies ran while one was open for 6% of the time, Pallas kernels for 0%

profile of v6, /device:TPU:22, one launch (start us, length us, event | category | flops | bytes accessed | tf_op | source)
XLA Modules:
  0.0 148.1 jit_solution(11934226327390327530)
XLA Ops:
  0.6 0.0 copy-start
  0.6 1.0 fusion.8
  1.7 5.9 %collective-permute-start = (bf16[128,1024]{1,0:T(8,128)(2,1)S(1)}, bf16[128,1024]{1,0:T(8,128)(2,1)S(1)}, u32[]{:S(2)}, u32[]{:S(2)}) collective-permute-start(bf16[128,1024]{1,0:T(8,128)(2,1)S(1)} %get-tuple-element.34), channel_id=1, source_target_pairs={{0,32},{32,0},{64,96},{96,64},{128,160},{160,128},{192,224},{224,1... | collective-permute-start | bytes 786440 | tf_op jit(solution)/shard_map/ppermute | solution.py:14
  7.6 0.7 maximum_reduce_fusion
  8.4 14.5 %all_to_all.20 = bf16[16,8,128]{2,1,0:T(8,128)(2,1)S(1)} all-to-all(bf16[16,8,128]{2,1,0:T(8,128)(2,1)S(1)} %broadcast_in_dim.41), channel_id=1, replica_groups={{0,2,4,6,32,34,36,38,16,18,20,22,48,50,52,54},{1,3,5,7,33,35,37,39,17,1..., dimensions={0} | all-to-all | bytes 65536 | tf_op jit(solution)/shard_map/all_to_all | solution.py:47
  22.8 0.0 collective-permute-done
  22.8 4.3 %collective-permute-start.1 = (bf16[128,1024]{1,0:T(8,128)(2,1)S(1)}, bf16[128,1024]{1,0:T(8,128)(2,1)S(1)}, u32[]{:S(2)}, u32[]{:S(2)}) collective-permute-start(bf16[128,1024]{1,0:T(8,128)(2,1)S(1)} %collective-permute-done), channel_id=1, source_target_pairs={{0,64},{32,480},{64,128},{96,32},{128,192},{160,96},{192,256},{224... | collective-permute-start | bytes 786440 | tf_op jit(solution)/shard_map/ppermute | solution.py:24
  27.1 12.4 %collective-permute-done.1 = bf16[128,1024]{1,0:T(8,128)(2,1)S(1)} collective-permute-done((bf16[128,1024]{1,0:T(8,128)(2,1)S(1)}, bf16[128,1024]{1,0:T(8,128)(2,1)S(1)}, u32[]{:S(2)}, u32[]{:S(2)}) %collective-permute-start.1) | collective-permute-done | bytes 262176 | tf_op jit(solution)/shard_map/ppermute | solution.py:24
  39.5 0.1 pad_maximum_fusion.own_ref
  39.6 1.9 %collective-permute-start.2 = (bf16[3,128,1024]{2,1,0:T(8,128)(2,1)S(1)}, bf16[3,128,1024]{2,1,0:T(8,128)(2,1)S(1)}, u32[]{:S(2)}, u32[]{:S(2)}) collective-permute-start(bf16[3,128,1024]{2,1,0:T(8,128)(2,1)S(1)} %pad_maximum_fusion.own_ref), channel_id=1, source_target_pairs={{0,1},{1,0},{2,3},{3,2},{4,5},{5,4},{6,7},{7,6},{8,9},{9,8},{10,11... | collective-permute-start | bytes 2359304 | tf_op jit(solution)/shard_map/ppermute | solution.py:14
  41.6 2.3 %collective-permute-done.2.near_ref = bf16[3,128,1024]{2,1,0:T(8,128)(2,1)S(1)} collective-permute-done((bf16[3,128,1024]{2,1,0:T(8,128)(2,1)S(1)}, bf16[3,128,1024]{2,1,0:T(8,128)(2,1)S(1)}, u32[]{:S(2)}, u32[]{:S(2)}) %collective-permute-start.2) | collective-permute-done | bytes 786464 | tf_op jit(solution)/shard_map/ppermute | solution.py:14
  43.8 0.8 broadcast_in_dim.42
  44.7 0.0 copy-start.1
  44.7 5.8 %all-to-all-start.1 = ((bf16[16,16,1024]{2,1,0:T(8,128)(2,1)}), bf16[16,16,1024]{2,1,0:T(8,128)(2,1)S(1)}, u32[]{:S(2)}, u32[]{:S(2)}) async-start(bf16[16,16,1024]{2,1,0:T(8,128)(2,1)} %broadcast_in_dim.42), calls=%async_computation.1 | async-start | bytes 1048576 | tf_op jit(solution)/shard_map/all_to_all | solution.py:47
  50.5 0.6 compare_and_fusion.1
  51.0 1.9 %collective-permute-start.3 = (bf16[3,128,1024]{2,1,0:T(8,128)(2,1)S(1)}, bf16[3,128,1024]{2,1,0:T(8,128)(2,1)S(1)}, u32[]{:S(2)}, u32[]{:S(2)}) collective-permute-start(bf16[3,128,1024]{2,1,0:T(8,128)(2,1)S(1)} %pad_maximum_fusion.own_ref), channel_id=1, source_target_pairs={{0,31},{1,2},{2,1},{3,4},{4,3},{5,6},{6,5},{7,8},{8,7},{9,10},{10,... | collective-permute-start | bytes 2359304 | tf_op jit(solution)/shard_map/ppermute | solution.py:19
  53.0 0.6 compare_and_fusion
  53.6 0.5 fusion.5
  54.1 11.3 %all-to-all-done.1 = bf16[16,16,1024]{2,1,0:T(8,128)(2,1)S(1)} async-done(((bf16[16,16,1024]{2,1,0:T(8,128)(2,1)}), bf16[16,16,1024]{2,1,0:T(8,128)(2,1)S(1)}, u32[]{:S(2)}, u32[]{:S(2)}) %all-to-all-start.1) | async-done | bytes 524320 | tf_op jit(solution)/shard_map/all_to_all | solution.py:47
  65.4 1.9 %collective-permute-start.4 = (bf16[256,1024]{1,0:T(8,128)(2,1)S(1)}, bf16[256,1024]{1,0:T(8,128)(2,1)S(1)}, u32[]{:S(2)}, u32[]{:S(2)}) collective-permute-start(bf16[256,1024]{1,0:T(8,128)(2,1)S(1)} %bitcast.43), channel_id=1, source_target_pairs={{0,1},{1,0},{2,3},{3,2},{4,5},{5,4},{6,7},{7,6},{8,9},{9,8},{10,11... | collective-permute-start | bytes 1572872 | tf_op jit(solution)/shard_map/ppermute | solution.py:14
  67.3 0.7 broadcast_or_fusion
  68.0 0.1 reshape.189
  68.1 0.0 copy-done
  68.1 0.7 gather_fusion
  68.8 0.1 reshape.192
  68.9 0.7 and_select_fusion
  69.6 0.1 select_n.39
  69.7 0.1 pad_add_fusion.2.counts
  69.8 1.9 %collective-permute-done.3.far_ref = bf16[3,128,1024]{2,1,0:T(8,128)(2,1)S(1)} collective-permute-done((bf16[3,128,1024]{2,1,0:T(8,128)(2,1)S(1)}, bf16[3,128,1024]{2,1,0:T(8,128)(2,1)S(1)}, u32[]{:S(2)}, u32[]{:S(2)}) %collective-permute-start.3) | collective-permute-done | bytes 786464 | tf_op jit(solution)/shard_map/ppermute | solution.py:19
  71.7 0.0 collective-permute-done.4.other_ref
  71.7 0.0 copy-done.1
  71.7 0.0 copy-start.2
  71.7 0.9 copy-done.2
  72.6 10.7 %shard_map.110 = (bf16[128,512]{1,0:T(8,128)(2,1)}, f32[3,128,1024]{2,1,0:T(8,128)}, bf16[640,1024]{1,0:T(8,128)(2,1)}, bf16[3,128,1024]{2,1,0:T(8,128)(2,1)}, f32[256,1024]{1,0:T(8,128)S(1)}) custom-call(s32[10]{0:T(128)S(1)} %pad_add_fusion.2.counts, bf16[128,512]{1,0:T(8,128)(2,1)S(1)} %bitcast.45, bf16[128,512]{1,0:T(8,128)(2,1)S(1)} %bitcast.46, ...), custom_call_target="tpu_custom_call" | custom-call | flops 1090519040 | bytes 12582912 | tf_op jit(solution)/shard_map/pallas_call | solution.py:164
  83.4 1.9 %collective-permute-start.5 = (bf16[640,1024]{1,0:T(8,128)(2,1)}, bf16[640,1024]{1,0:T(8,128)(2,1)S(1)}, u32[]{:S(2)}, u32[]{:S(2)}) collective-permute-start(bf16[640,1024]{1,0:T(8,128)(2,1)} %get-tuple-element.22), channel_id=1, source_target_pairs={{0,1},{1,0},{2,3},{3,2},{4,5},{5,4},{6,7},{7,6},{8,9},{9,8},{10,11... | collective-permute-start | bytes 3932168 | tf_op jit(solution)/shard_map/ppermute | solution.py:14
  85.3 2.9 %collective-permute-start.6 = (bf16[3,128,1024]{2,1,0:T(8,128)(2,1)}, bf16[3,128,1024]{2,1,0:T(8,128)(2,1)S(1)}, u32[]{:S(2)}, u32[]{:S(2)}) collective-permute-start(bf16[3,128,1024]{2,1,0:T(8,128)(2,1)} %get-tuple-element.24), channel_id=1, source_target_pairs={{0,31},{1,2},{2,1},{3,4},{4,3},{5,6},{6,5},{7,8},{8,7},{9,10},{10,... | collective-permute-start | bytes 2359304 | tf_op jit(solution)/shard_map/ppermute | solution.py:19
  88.2 0.3 collective-permute-done.5
  88.5 0.3 convert_element_type.28
  88.8 1.0 fusion
  89.8 8.0 %all-to-all-start.2 = ((bf16[16,16,1024]{2,1,0:T(8,128)(2,1)}), bf16[16,16,1024]{2,1,0:T(8,128)(2,1)S(1)}, u32[]{:S(2)}, u32[]{:S(2)}) async-start(bf16[16,16,1024]{2,1,0:T(8,128)(2,1)} %bitcast.15), calls=%async_computation.2 | async-start | bytes 1048576 | tf_op jit(solution)/shard_map/all_to_all | solution.py:47
  97.7 0.0 copy-start.3
  97.7 0.2 slice.44
  97.9 5.3 %collective-permute-done.6 = bf16[3,128,1024]{2,1,0:T(8,128)(2,1)S(1)} collective-permute-done((bf16[3,128,1024]{2,1,0:T(8,128)(2,1)}, bf16[3,128,1024]{2,1,0:T(8,128)(2,1)S(1)}, u32[]{:S(2)}, u32[]{:S(2)}) %collective-permute-start.6) | collective-permute-done | bytes 786464 | tf_op jit(solution)/shard_map/ppermute | solution.py:19
  103.2 0.0 copy-done.3
  103.2 0.4 convert_add_fusion
  103.7 7.5 %all-to-all-done.2 = bf16[16,16,1024]{2,1,0:T(8,128)(2,1)S(1)} async-done(((bf16[16,16,1024]{2,1,0:T(8,128)(2,1)}), bf16[16,16,1024]{2,1,0:T(8,128)(2,1)S(1)}, u32[]{:S(2)}, u32[]{:S(2)}) %all-to-all-start.2) | async-done | bytes 524320 | tf_op jit(solution)/shard_map/all_to_all | solution.py:47
  111.2 0.1 convert_reduce_fusion
  111.3 5.5 %collective-permute-start.7 = (bf16[128,1024]{1,0:T(8,128)(2,1)S(1)}, bf16[128,1024]{1,0:T(8,128)(2,1)S(1)}, u32[]{:S(2)}, u32[]{:S(2)}) collective-permute-start(bf16[128,1024]{1,0:T(8,128)(2,1)S(1)} %fusion.3), channel_id=1, source_target_pairs={{0,448},{32,96},{64,0},{96,160},{128,64},{160,224},{192,128},{224,... | collective-permute-start | bytes 786440 | tf_op jit(solution)/shard_map/ppermute | solution.py:24
  116.8 0.6 copy.13
  117.5 11.3 %all-to-all-start.3 = ((f32[16,8,128]{2,1,0:T(8,128)}), f32[16,8,128]{2,1,0:T(8,128)S(1)}, u32[]{:S(2)}, u32[]{:S(2)}) async-start(f32[16,8,128]{2,1,0:T(8,128)} %bitcast.28), calls=%async_computation.3 | async-start | bytes 131072 | tf_op jit(solution)/shard_map/all_to_all | solution.py:47
  128.8 0.0 collective-permute-done.7
  128.8 0.1 fusion.1
  128.8 5.5 %collective-permute-start.8 = (bf16[128,1024]{1,0:T(8,128)(2,1)S(1)}, bf16[128,1024]{1,0:T(8,128)(2,1)S(1)}, u32[]{:S(2)}, u32[]{:S(2)}) collective-permute-start(bf16[128,1024]{1,0:T(8,128)(2,1)S(1)} %fusion.1), channel_id=1, source_target_pairs={{0,32},{32,0},{64,96},{96,64},{128,160},{160,128},{192,224},{224,1... | collective-permute-start | bytes 786440 | tf_op jit(solution)/shard_map/ppermute | solution.py:14
  134.3 0.4 all-to-all-done.3
  134.8 0.6 fusion.9
  135.3 12.0 %collective-permute-done.8 = bf16[128,1024]{1,0:T(8,128)(2,1)S(1)} collective-permute-done((bf16[128,1024]{1,0:T(8,128)(2,1)S(1)}, bf16[128,1024]{1,0:T(8,128)(2,1)S(1)}, u32[]{:S(2)}, u32[]{:S(2)}) %collective-permute-start.8) | collective-permute-done | bytes 262176 | tf_op jit(solution)/shard_map/ppermute | solution.py:14
  147.3 0.1 fusion.2
  147.4 0.7 slice_bitcast_fusion
  (4 shorter events, 0.1 us)
Async XLA Ops:
  0.6 67.5 %copy-start = (s32[16,32]{1,0:T(8,128)S(1)}, s32[16,32]{1,0:T(8,128)}, u32[]{:S(2)}) copy-start(s32[16,32]{1,0:T(8,128)} %param.13) | copy-start | bytes 6148
  1.7 21.1 %collective-permute-start = (bf16[128,1024]{1,0:T(8,128)(2,1)S(1)}, bf16[128,1024]{1,0:T(8,128)(2,1)S(1)}, u32[]{:S(2)}, u32[]{:S(2)}) collective-permute-start(bf16[128,1024]{1,0:T(8,128)(2,1)S(1)} %get-tuple-element.34), channel_id=1, source_target_pairs={{0,32},{32,0},{64,96},{96,64},{128,160},{160,128},{192,224},{224,1... | collective-permute-start | bytes 786440 | tf_op jit(solution)/shard_map/ppermute | solution.py:14
  22.8 16.7 %collective-permute-start.1 = (bf16[128,1024]{1,0:T(8,128)(2,1)S(1)}, bf16[128,1024]{1,0:T(8,128)(2,1)S(1)}, u32[]{:S(2)}, u32[]{:S(2)}) collective-permute-start(bf16[128,1024]{1,0:T(8,128)(2,1)S(1)} %collective-permute-done), channel_id=1, source_target_pairs={{0,64},{32,480},{64,128},{96,32},{128,192},{160,96},{192,256},{224... | collective-permute-start | bytes 786440 | tf_op jit(solution)/shard_map/ppermute | solution.py:24
  39.6 4.2 %collective-permute-start.2 = (bf16[3,128,1024]{2,1,0:T(8,128)(2,1)S(1)}, bf16[3,128,1024]{2,1,0:T(8,128)(2,1)S(1)}, u32[]{:S(2)}, u32[]{:S(2)}) collective-permute-start(bf16[3,128,1024]{2,1,0:T(8,128)(2,1)S(1)} %pad_maximum_fusion.own_ref), channel_id=1, source_target_pairs={{0,1},{1,0},{2,3},{3,2},{4,5},{5,4},{6,7},{7,6},{8,9},{9,8},{10,11... | collective-permute-start | bytes 2359304 | tf_op jit(solution)/shard_map/ppermute | solution.py:14
  44.7 27.1 %copy-start.1 = (bf16[1,1,128,512]{3,2,1,0:T(8,128)(2,1)S(1)}, bf16[1,1,128,512]{3,2,1,0:T(8,128)(2,1)}, u32[]{:S(2)}) copy-start(bf16[1,1,128,512]{3,2,1,0:T(8,128)(2,1)} %param.7) | copy-start | bytes 393220
  44.7 20.7 %all-to-all-start.1 = ((bf16[16,16,1024]{2,1,0:T(8,128)(2,1)}), bf16[16,16,1024]{2,1,0:T(8,128)(2,1)S(1)}, u32[]{:S(2)}, u32[]{:S(2)}) async-start(bf16[16,16,1024]{2,1,0:T(8,128)(2,1)} %broadcast_in_dim.42), calls=%async_computation.1 | async-start | bytes 1048576 | tf_op jit(solution)/shard_map/all_to_all | solution.py:47
  51.0 20.7 %collective-permute-start.3 = (bf16[3,128,1024]{2,1,0:T(8,128)(2,1)S(1)}, bf16[3,128,1024]{2,1,0:T(8,128)(2,1)S(1)}, u32[]{:S(2)}, u32[]{:S(2)}) collective-permute-start(bf16[3,128,1024]{2,1,0:T(8,128)(2,1)S(1)} %pad_maximum_fusion.own_ref), channel_id=1, source_target_pairs={{0,31},{1,2},{2,1},{3,4},{4,3},{5,6},{6,5},{7,8},{8,7},{9,10},{10,... | collective-permute-start | bytes 2359304 | tf_op jit(solution)/shard_map/ppermute | solution.py:19
  65.4 6.3 %collective-permute-start.4 = (bf16[256,1024]{1,0:T(8,128)(2,1)S(1)}, bf16[256,1024]{1,0:T(8,128)(2,1)S(1)}, u32[]{:S(2)}, u32[]{:S(2)}) collective-permute-start(bf16[256,1024]{1,0:T(8,128)(2,1)S(1)} %bitcast.43), channel_id=1, source_target_pairs={{0,1},{1,0},{2,3},{3,2},{4,5},{5,4},{6,7},{7,6},{8,9},{9,8},{10,11... | collective-permute-start | bytes 1572872 | tf_op jit(solution)/shard_map/ppermute | solution.py:14
  71.7 0.9 copy-start.2
  83.4 5.1 %collective-permute-start.5 = (bf16[640,1024]{1,0:T(8,128)(2,1)}, bf16[640,1024]{1,0:T(8,128)(2,1)S(1)}, u32[]{:S(2)}, u32[]{:S(2)}) collective-permute-start(bf16[640,1024]{1,0:T(8,128)(2,1)} %get-tuple-element.22), channel_id=1, source_target_pairs={{0,1},{1,0},{2,3},{3,2},{4,5},{5,4},{6,7},{7,6},{8,9},{9,8},{10,11... | collective-permute-start | bytes 3932168 | tf_op jit(solution)/shard_map/ppermute | solution.py:14
  85.3 17.9 %collective-permute-start.6 = (bf16[3,128,1024]{2,1,0:T(8,128)(2,1)}, bf16[3,128,1024]{2,1,0:T(8,128)(2,1)S(1)}, u32[]{:S(2)}, u32[]{:S(2)}) collective-permute-start(bf16[3,128,1024]{2,1,0:T(8,128)(2,1)} %get-tuple-element.24), channel_id=1, source_target_pairs={{0,31},{1,2},{2,1},{3,4},{4,3},{5,6},{6,5},{7,8},{8,7},{9,10},{10,... | collective-permute-start | bytes 2359304 | tf_op jit(solution)/shard_map/ppermute | solution.py:19
  89.8 21.4 %all-to-all-start.2 = ((bf16[16,16,1024]{2,1,0:T(8,128)(2,1)}), bf16[16,16,1024]{2,1,0:T(8,128)(2,1)S(1)}, u32[]{:S(2)}, u32[]{:S(2)}) async-start(bf16[16,16,1024]{2,1,0:T(8,128)(2,1)} %bitcast.15), calls=%async_computation.2 | async-start | bytes 1048576 | tf_op jit(solution)/shard_map/all_to_all | solution.py:47
  97.7 5.5 %copy-start.3 = (f32[3,128,1024]{2,1,0:T(8,128)S(1)}, f32[3,128,1024]{2,1,0:T(8,128)}, u32[]{:S(2)}) copy-start(f32[3,128,1024]{2,1,0:T(8,128)} %get-tuple-element.23) | copy-start | bytes 4718596
  111.3 17.5 %collective-permute-start.7 = (bf16[128,1024]{1,0:T(8,128)(2,1)S(1)}, bf16[128,1024]{1,0:T(8,128)(2,1)S(1)}, u32[]{:S(2)}, u32[]{:S(2)}) collective-permute-start(bf16[128,1024]{1,0:T(8,128)(2,1)S(1)} %fusion.3), channel_id=1, source_target_pairs={{0,448},{32,96},{64,0},{96,160},{128,64},{160,224},{192,128},{224,... | collective-permute-start | bytes 786440 | tf_op jit(solution)/shard_map/ppermute | solution.py:24
  117.5 17.3 %all-to-all-start.3 = ((f32[16,8,128]{2,1,0:T(8,128)}), f32[16,8,128]{2,1,0:T(8,128)S(1)}, u32[]{:S(2)}, u32[]{:S(2)}) async-start(f32[16,8,128]{2,1,0:T(8,128)} %bitcast.28), calls=%async_computation.3 | async-start | bytes 131072 | tf_op jit(solution)/shard_map/all_to_all | solution.py:47
  128.8 18.5 %collective-permute-start.8 = (bf16[128,1024]{1,0:T(8,128)(2,1)S(1)}, bf16[128,1024]{1,0:T(8,128)(2,1)S(1)}, u32[]{:S(2)}, u32[]{:S(2)}) collective-permute-start(bf16[128,1024]{1,0:T(8,128)(2,1)S(1)} %fusion.1), channel_id=1, source_target_pairs={{0,32},{32,0},{64,96},{96,64},{128,160},{160,128},{192,224},{224,1... | collective-permute-start | bytes 786440 | tf_op jit(solution)/shard_map/ppermute | solution.py:14

commit v7 on v6

--- a/solution.py
+++ b/solution.py
@@ -47,19 +47,21 @@
     return lax.all_to_all(block, ("row", "col"), 0, 0, axis_index_groups=groups, tiled=True)
 
 
-def gather_first(own):
-    width = own.shape[-1]
-    groups, _ = place_groups()
-    members = len(groups[0])
-    block = jnp.broadcast_to(own.reshape(1, 8, width // 8), (members, 8, width // 8))
-    return deal(block, groups).reshape(members, width)
-
-
-def gather_second(block):
-    held, width = block.shape
-    _, groups = place_groups()
-    members = len(groups[0])
-    return deal(jnp.broadcast_to(block, (members, held, width)), groups).reshape(members * held, width)
+def gather_line(own):
+    lines = lax.axis_size("row")
+    tile = (8, own.shape[-1] // 8)
+    return lax.all_to_all(jnp.broadcast_to(own.reshape(1, *tile), (lines, *tile)), "row", 0, 0, tiled=True)
+
+
+def gather_rest(block):
+    lines, *tile = block.shape
+    columns = lax.axis_size("col")
+    members = columns // 2
+    same_core = [list(range(core, columns, 2)) for core in range(2)]
+    block = jnp.broadcast_to(block[None], (members, lines, *tile))
+    block = lax.all_to_all(block, "col", 0, 0, axis_index_groups=same_core, tiled=True)
+    block = block.reshape(2, columns // 16, 4, lines // 2, 2, *tile).transpose(1, 3, 0, 4, 2, 5, 6)
+    return block.reshape(members * lines, tile[0] * tile[1])
 
 
 def scatter_second(block):
@@ -207,12 +209,11 @@
     own = jnp.concatenate([fine_keys[0, 0], fine_values[0, 0]], axis=-1)
     token = jnp.concatenate([coarse_keys, coarse_values], axis=-1)
     paired = exchange(own, "row", 1)
-    coarse = gather_first(token)
+    coarse = gather_line(token)
     coarse, paired = lax.optimization_barrier((coarse, paired))
+    kept = gather_rest(coarse)
     column = jnp.stack([own, paired, skip_row(paired, 2)])
     near, far = exchange(column, "col", 1), to_far(column, "col")
-    coarse, near = lax.optimization_barrier((coarse, near))
-    kept = gather_second(coarse)
     other = exchange(kept, "col", 1)
     grad_q, own_terms, core_terms, far_terms, kept_terms = attention(
         counts, fine_queries[0, 0], grad_out[0, 0], column, near, far, kept, other

time: 149 us -> 144 us (0.966)
  the two profiles are of different devices: /device:TPU:22 before, /device:TPU:14 now
where the time goes in v7:
time: 144 us; the launch traced here: 143 us
  starting transfers between devices  56.7 us (39%)
  waiting for transfers between devices  39.8 us (28%)
  blocking collectives  23.2 us (16%)
  Pallas kernels  10.7 us (7%)
  other arithmetic  6.48 us (4%)
  local copies, waits for them, and re-layouts  5.16 us (4%)
    all_to_all x1, blocking collectives, gather_line(): lax.all_to_all(jnp.broadcast_to(own.reshape(1, *tile), (lines, *tile)), '...  23.2 us
    ppermute x2, waiting for transfers between devices, to_far(): lax.ppermute(block, axis, [(i, (i + (1 if i % 2 else -1)) % size) for i i...  23 us
    ppermute x5, starting transfers between devices, exchange(): lax.ppermute(block, axis, [(i, i ^ bit) for i in range(lax.axis_size(axis...  21.2 us
    all_to_all x2, starting transfers between devices, deal(): lax.all_to_all(block, ('row', 'col'), 0, 0, axis_index_groups=groups, til...  13.5 us
    pallas_call x1, Pallas kernels, attention(): pl.pallas_call(attention_kernel, out_shape=(jax.ShapeDtypeStruct((rows, w...  10.7 us
    ppermute x5, waiting for transfers between devices, exchange(): lax.ppermute(block, axis, [(i, i ^ bit) for i in range(lax.axis_size(axis...  10.6 us
    all_to_all x1, starting transfers between devices, gather_rest(): lax.all_to_all(block, 'col', 0, 0, axis_index_groups=same_core, tiled=True)  7.72 us
    ppermute x2, starting transfers between devices, skip_row(): lax.ppermute(block, 'row', [(i, (i + (-way if i % 2 else way)) % size) fo...  7.46 us
  transfers between devices with their start and end apart: 12, of which 5 were waited for; matrix products, arithmetic and copies ran while one was open for 6% of the time, Pallas kernels for 0%

profile of v7, /device:TPU:14, one launch (start us, length us, event | category | flops | bytes accessed | tf_op | source)
XLA Modules:
  0.0 143.0 jit_solution(12824300026494789823)
XLA Ops:
  0.6 0.0 copy-start
  0.6 1.0 fusion.8
  1.7 6.8 %collective-permute-start = (bf16[128,1024]{1,0:T(8,128)(2,1)S(1)}, bf16[128,1024]{1,0:T(8,128)(2,1)S(1)}, u32[]{:S(2)}, u32[]{:S(2)}) collective-permute-start(bf16[128,1024]{1,0:T(8,128)(2,1)S(1)} %get-tuple-element.30), channel_id=1, source_target_pairs={{0,32},{32,0},{64,96},{96,64},{128,160},{160,128},{192,224},{224,1... | collective-permute-start | bytes 786440 | tf_op jit(solution)/shard_map/ppermute | solution.py:14
  8.5 0.7 maximum_reduce_fusion
  9.3 23.2 %all_to_all.20 = bf16[16,8,128]{2,1,0:T(8,128)(2,1)S(1)} all-to-all(bf16[16,8,128]{2,1,0:T(8,128)(2,1)S(1)} %broadcast_in_dim.44), channel_id=1, replica_groups=mesh['row'=16,'col'=32] {'row'}, dimensions={0} | all-to-all | bytes 65536 | tf_op jit(solution)/shard_map/all_to_all | solution.py:53
  32.5 0.0 collective-permute-done
  32.5 0.9 broadcast_in_dim.45
  33.4 7.7 %all-to-all-start.1 = ((bf16[16,16,8,128]{3,2,1,0:T(8,128)(2,1)}), bf16[16,16,8,128]{3,2,1,0:T(8,128)(2,1)S(1)}, u32[]{:S(2)}, u32[]{:S(2)}) async-start(bf16[16,16,8,128]{3,2,1,0:T(8,128)(2,1)} %broadcast_in_dim.45), calls=%async_computation.1 | async-start | bytes 1048576 | tf_op jit(solution)/shard_map/all_to_all | solution.py:62
  41.1 3.1 %collective-permute-start.1 = (bf16[128,1024]{1,0:T(8,128)(2,1)S(1)}, bf16[128,1024]{1,0:T(8,128)(2,1)S(1)}, u32[]{:S(2)}, u32[]{:S(2)}) collective-permute-start(bf16[128,1024]{1,0:T(8,128)(2,1)S(1)} %collective-permute-done), channel_id=1, source_target_pairs={{0,64},{32,480},{64,128},{96,32},{128,192},{160,96},{192,256},{224... | collective-permute-start | bytes 786440 | tf_op jit(solution)/shard_map/ppermute | solution.py:24
  44.2 0.6 compare_and_fusion.1
  44.8 5.7 %collective-permute-done.1 = bf16[128,1024]{1,0:T(8,128)(2,1)S(1)} collective-permute-done((bf16[128,1024]{1,0:T(8,128)(2,1)S(1)}, bf16[128,1024]{1,0:T(8,128)(2,1)S(1)}, u32[]{:S(2)}, u32[]{:S(2)}) %collective-permute-start.1) | collective-permute-done | bytes 262176 | tf_op jit(solution)/shard_map/ppermute | solution.py:24
  50.6 0.1 pad_maximum_fusion.own_ref
  50.6 1.9 %collective-permute-start.3 = (bf16[3,128,1024]{2,1,0:T(8,128)(2,1)S(1)}, bf16[3,128,1024]{2,1,0:T(8,128)(2,1)S(1)}, u32[]{:S(2)}, u32[]{:S(2)}) collective-permute-start(bf16[3,128,1024]{2,1,0:T(8,128)(2,1)S(1)} %pad_maximum_fusion.own_ref), channel_id=1, source_target_pairs={{0,31},{1,2},{2,1},{3,4},{4,3},{5,6},{6,5},{7,8},{8,7},{9,10},{10,... | collective-permute-start | bytes 2359304 | tf_op jit(solution)/shard_map/ppermute | solution.py:19
  52.6 3.5 %collective-permute-start.2 = (bf16[3,128,1024]{2,1,0:T(8,128)(2,1)S(1)}, bf16[3,128,1024]{2,1,0:T(8,128)(2,1)S(1)}, u32[]{:S(2)}, u32[]{:S(2)}) collective-permute-start(bf16[3,128,1024]{2,1,0:T(8,128)(2,1)S(1)} %pad_maximum_fusion.own_ref), channel_id=1, source_target_pairs={{0,1},{1,0},{2,3},{3,2},{4,5},{5,4},{6,7},{7,6},{8,9},{9,8},{10,11... | collective-permute-start | bytes 2359304 | tf_op jit(solution)/shard_map/ppermute | solution.py:14
  56.1 0.6 compare_and_fusion
  56.6 0.5 fusion.5
  57.2 0.0 all-to-all-done.1
  57.2 0.0 copy-start.4
  57.2 0.1 copy.13
  57.3 0.0 copy-start.1
  57.3 0.1 copy.17
  57.4 1.9 %collective-permute-start.4 = (bf16[256,1024]{1,0:T(8,128)(2,1)S(1)}, bf16[256,1024]{1,0:T(8,128)(2,1)S(1)}, u32[]{:S(2)}, u32[]{:S(2)}) collective-permute-start(bf16[256,1024]{1,0:T(8,128)(2,1)S(1)} %bitcast.46), channel_id=1, source_target_pairs={{0,1},{1,0},{2,3},{3,2},{4,5},{5,4},{6,7},{7,6},{8,9},{9,8},{10,11... | collective-permute-start | bytes 1572872 | tf_op jit(solution)/shard_map/ppermute | solution.py:14
  59.4 0.0 copy-done.4
  59.4 0.1 broadcast_or_fusion
  59.4 0.1 reshape.190
  59.5 0.0 copy-done
  59.5 0.7 gather_fusion
  60.2 0.1 reshape.193
  60.3 0.7 and_select_fusion
  61.1 0.1 select_n.39
  61.1 0.1 pad_add_fusion.2.counts
  61.3 10.2 %collective-permute-done.3.far_ref = bf16[3,128,1024]{2,1,0:T(8,128)(2,1)S(1)} collective-permute-done((bf16[3,128,1024]{2,1,0:T(8,128)(2,1)S(1)}, bf16[3,128,1024]{2,1,0:T(8,128)(2,1)S(1)}, u32[]{:S(2)}, u32[]{:S(2)}) %collective-permute-start.3) | collective-permute-done | bytes 786464 | tf_op jit(solution)/shard_map/ppermute | solution.py:19
  71.5 0.0 collective-permute-done.2.near_ref
  71.5 0.0 collective-permute-done.4.other_ref
  71.5 0.0 copy-done.1
  71.5 0.0 copy-start.2
  71.5 0.9 copy-done.2
  72.4 10.7 %shard_map.110 = (bf16[128,512]{1,0:T(8,128)(2,1)}, f32[3,128,1024]{2,1,0:T(8,128)}, bf16[640,1024]{1,0:T(8,128)(2,1)}, bf16[3,128,1024]{2,1,0:T(8,128)(2,1)}, f32[256,1024]{1,0:T(8,128)S(1)}) custom-call(s32[10]{0:T(128)S(1)} %pad_add_fusion.2.counts, bf16[128,512]{1,0:T(8,128)(2,1)S(1)} %bitcast.48, bf16[128,512]{1,0:T(8,128)(2,1)S(1)} %bitcast.49, ...), custom_call_target="tpu_custom_call" | custom-call | flops 1090519040 | bytes 12582912 | tf_op jit(solution)/shard_map/pallas_call | solution.py:166
  83.2 2.6 %collective-permute-start.5 = (bf16[640,1024]{1,0:T(8,128)(2,1)}, bf16[640,1024]{1,0:T(8,128)(2,1)S(1)}, u32[]{:S(2)}, u32[]{:S(2)}) collective-permute-start(bf16[640,1024]{1,0:T(8,128)(2,1)} %get-tuple-element.18), channel_id=1, source_target_pairs={{0,1},{1,0},{2,3},{3,2},{4,5},{5,4},{6,7},{7,6},{8,9},{9,8},{10,11... | collective-permute-start | bytes 3932168 | tf_op jit(solution)/shard_map/ppermute | solution.py:14
  85.8 4.9 %collective-permute-start.6 = (bf16[3,128,1024]{2,1,0:T(8,128)(2,1)}, bf16[3,128,1024]{2,1,0:T(8,128)(2,1)S(1)}, u32[]{:S(2)}, u32[]{:S(2)}) collective-permute-start(bf16[3,128,1024]{2,1,0:T(8,128)(2,1)} %get-tuple-element.20), channel_id=1, source_target_pairs={{0,31},{1,2},{2,1},{3,4},{4,3},{5,6},{6,5},{7,8},{8,7},{9,10},{10,... | collective-permute-start | bytes 2359304 | tf_op jit(solution)/shard_map/ppermute | solution.py:19
  90.7 0.0 collective-permute-done.5
  90.7 0.3 convert_element_type.28
  91.0 1.0 fusion
  92.0 4.0 %all-to-all-start.2 = ((bf16[16,16,1024]{2,1,0:T(8,128)(2,1)}), bf16[16,16,1024]{2,1,0:T(8,128)(2,1)S(1)}, u32[]{:S(2)}, u32[]{:S(2)}) async-start(bf16[16,16,1024]{2,1,0:T(8,128)(2,1)} %bitcast.16), calls=%async_computation.2 | async-start | bytes 1048576 | tf_op jit(solution)/shard_map/all_to_all | solution.py:47
  96.0 0.0 copy-start.3
  96.0 0.2 slice.44
  96.2 12.7 %collective-permute-done.6 = bf16[3,128,1024]{2,1,0:T(8,128)(2,1)S(1)} collective-permute-done((bf16[3,128,1024]{2,1,0:T(8,128)(2,1)}, bf16[3,128,1024]{2,1,0:T(8,128)(2,1)S(1)}, u32[]{:S(2)}, u32[]{:S(2)}) %collective-permute-start.6) | collective-permute-done | bytes 786464 | tf_op jit(solution)/shard_map/ppermute | solution.py:19
  108.9 0.0 copy-done.3
  108.9 0.5 convert_add_fusion
  109.4 0.0 all-to-all-done.2
  109.4 0.1 convert_reduce_fusion
  109.6 4.4 %collective-permute-start.7 = (bf16[128,1024]{1,0:T(8,128)(2,1)S(1)}, bf16[128,1024]{1,0:T(8,128)(2,1)S(1)}, u32[]{:S(2)}, u32[]{:S(2)}) collective-permute-start(bf16[128,1024]{1,0:T(8,128)(2,1)S(1)} %fusion.3), channel_id=1, source_target_pairs={{0,448},{32,96},{64,0},{96,160},{128,64},{160,224},{192,128},{224,... | collective-permute-start | bytes 786440 | tf_op jit(solution)/shard_map/ppermute | solution.py:24
  113.9 0.6 copy.15
  114.6 9.5 %all-to-all-start.3 = ((f32[16,8,128]{2,1,0:T(8,128)}), f32[16,8,128]{2,1,0:T(8,128)S(1)}, u32[]{:S(2)}, u32[]{:S(2)}) async-start(f32[16,8,128]{2,1,0:T(8,128)} %bitcast.31), calls=%async_computation.3 | async-start | bytes 131072 | tf_op jit(solution)/shard_map/all_to_all | solution.py:47
  124.1 0.0 collective-permute-done.7
  124.1 0.1 fusion.1
  124.1 6.4 %collective-permute-start.8 = (bf16[128,1024]{1,0:T(8,128)(2,1)S(1)}, bf16[128,1024]{1,0:T(8,128)(2,1)S(1)}, u32[]{:S(2)}, u32[]{:S(2)}) collective-permute-start(bf16[128,1024]{1,0:T(8,128)(2,1)S(1)} %fusion.1), channel_id=1, source_target_pairs={{0,32},{32,0},{64,96},{96,64},{128,160},{160,128},{192,224},{224,1... | collective-permute-start | bytes 786440 | tf_op jit(solution)/shard_map/ppermute | solution.py:14
  130.5 0.5 all-to-all-done.3
  131.0 0.6 fusion.9
  131.6 10.6 %collective-permute-done.8 = bf16[128,1024]{1,0:T(8,128)(2,1)S(1)} collective-permute-done((bf16[128,1024]{1,0:T(8,128)(2,1)S(1)}, bf16[128,1024]{1,0:T(8,128)(2,1)S(1)}, u32[]{:S(2)}, u32[]{:S(2)}) %collective-permute-start.8) | collective-permute-done | bytes 262176 | tf_op jit(solution)/shard_map/ppermute | solution.py:14
  142.2 0.1 fusion.2
  142.3 0.7 slice_bitcast_fusion
  (3 shorter events, 0.1 us)
Async XLA Ops:
  0.6 58.9 %copy-start = (s32[16,32]{1,0:T(8,128)S(1)}, s32[16,32]{1,0:T(8,128)}, u32[]{:S(2)}) copy-start(s32[16,32]{1,0:T(8,128)} %param.13) | copy-start | bytes 6148
  1.7 30.8 %collective-permute-start = (bf16[128,1024]{1,0:T(8,128)(2,1)S(1)}, bf16[128,1024]{1,0:T(8,128)(2,1)S(1)}, u32[]{:S(2)}, u32[]{:S(2)}) collective-permute-start(bf16[128,1024]{1,0:T(8,128)(2,1)S(1)} %get-tuple-element.30), channel_id=1, source_target_pairs={{0,32},{32,0},{64,96},{96,64},{128,160},{160,128},{192,224},{224,1... | collective-permute-start | bytes 786440 | tf_op jit(solution)/shard_map/ppermute | solution.py:14
  33.4 23.8 %all-to-all-start.1 = ((bf16[16,16,8,128]{3,2,1,0:T(8,128)(2,1)}), bf16[16,16,8,128]{3,2,1,0:T(8,128)(2,1)S(1)}, u32[]{:S(2)}, u32[]{:S(2)}) async-start(bf16[16,16,8,128]{3,2,1,0:T(8,128)(2,1)} %broadcast_in_dim.45), calls=%async_computation.1 | async-start | bytes 1048576 | tf_op jit(solution)/shard_map/all_to_all | solution.py:62
  41.1 9.5 %collective-permute-start.1 = (bf16[128,1024]{1,0:T(8,128)(2,1)S(1)}, bf16[128,1024]{1,0:T(8,128)(2,1)S(1)}, u32[]{:S(2)}, u32[]{:S(2)}) collective-permute-start(bf16[128,1024]{1,0:T(8,128)(2,1)S(1)} %collective-permute-done), channel_id=1, source_target_pairs={{0,64},{32,480},{64,128},{96,32},{128,192},{160,96},{192,256},{224... | collective-permute-start | bytes 786440 | tf_op jit(solution)/shard_map/ppermute | solution.py:24
  50.6 20.9 %collective-permute-start.3 = (bf16[3,128,1024]{2,1,0:T(8,128)(2,1)S(1)}, bf16[3,128,1024]{2,1,0:T(8,128)(2,1)S(1)}, u32[]{:S(2)}, u32[]{:S(2)}) collective-permute-start(bf16[3,128,1024]{2,1,0:T(8,128)(2,1)S(1)} %pad_maximum_fusion.own_ref), channel_id=1, source_target_pairs={{0,31},{1,2},{2,1},{3,4},{4,3},{5,6},{6,5},{7,8},{8,7},{9,10},{10,... | collective-permute-start | bytes 2359304 | tf_op jit(solution)/shard_map/ppermute | solution.py:19
  52.6 18.9 %collective-permute-start.2 = (bf16[3,128,1024]{2,1,0:T(8,128)(2,1)S(1)}, bf16[3,128,1024]{2,1,0:T(8,128)(2,1)S(1)}, u32[]{:S(2)}, u32[]{:S(2)}) collective-permute-start(bf16[3,128,1024]{2,1,0:T(8,128)(2,1)S(1)} %pad_maximum_fusion.own_ref), channel_id=1, source_target_pairs={{0,1},{1,0},{2,3},{3,2},{4,5},{5,4},{6,7},{7,6},{8,9},{9,8},{10,11... | collective-permute-start | bytes 2359304 | tf_op jit(solution)/shard_map/ppermute | solution.py:14
  57.2 2.2 %copy-start.4 = (s32[3]{0:T(128)S(1)}, s32[3]{0:T(128)}, u32[]{:S(2)}) copy-start(s32[3]{0:T(128)} %get-tuple-element.34) | copy-start | bytes 40
  57.3 14.2 %copy-start.1 = (bf16[1,1,128,512]{3,2,1,0:T(8,128)(2,1)S(1)}, bf16[1,1,128,512]{3,2,1,0:T(8,128)(2,1)}, u32[]{:S(2)}) copy-start(bf16[1,1,128,512]{3,2,1,0:T(8,128)(2,1)} %param.7) | copy-start | bytes 393220
  57.4 14.1 %collective-permute-start.4 = (bf16[256,1024]{1,0:T(8,128)(2,1)S(1)}, bf16[256,1024]{1,0:T(8,128)(2,1)S(1)}, u32[]{:S(2)}, u32[]{:S(2)}) collective-permute-start(bf16[256,1024]{1,0:T(8,128)(2,1)S(1)} %bitcast.46), channel_id=1, source_target_pairs={{0,1},{1,0},{2,3},{3,2},{4,5},{5,4},{6,7},{7,6},{8,9},{9,8},{10,11... | collective-permute-start | bytes 1572872 | tf_op jit(solution)/shard_map/ppermute | solution.py:14
  71.5 0.9 copy-start.2
  83.2 7.5 %collective-permute-start.5 = (bf16[640,1024]{1,0:T(8,128)(2,1)}, bf16[640,1024]{1,0:T(8,128)(2,1)S(1)}, u32[]{:S(2)}, u32[]{:S(2)}) collective-permute-start(bf16[640,1024]{1,0:T(8,128)(2,1)} %get-tuple-element.18), channel_id=1, source_target_pairs={{0,1},{1,0},{2,3},{3,2},{4,5},{5,4},{6,7},{7,6},{8,9},{9,8},{10,11... | collective-permute-start | bytes 3932168 | tf_op jit(solution)/shard_map/ppermute | solution.py:14
  85.8 23.1 %collective-permute-start.6 = (bf16[3,128,1024]{2,1,0:T(8,128)(2,1)}, bf16[3,128,1024]{2,1,0:T(8,128)(2,1)S(1)}, u32[]{:S(2)}, u32[]{:S(2)}) collective-permute-start(bf16[3,128,1024]{2,1,0:T(8,128)(2,1)} %get-tuple-element.20), channel_id=1, source_target_pairs={{0,31},{1,2},{2,1},{3,4},{4,3},{5,6},{6,5},{7,8},{8,7},{9,10},{10,... | collective-permute-start | bytes 2359304 | tf_op jit(solution)/shard_map/ppermute | solution.py:19
  92.0 17.5 %all-to-all-start.2 = ((bf16[16,16,1024]{2,1,0:T(8,128)(2,1)}), bf16[16,16,1024]{2,1,0:T(8,128)(2,1)S(1)}, u32[]{:S(2)}, u32[]{:S(2)}) async-start(bf16[16,16,1024]{2,1,0:T(8,128)(2,1)} %bitcast.16), calls=%async_computation.2 | async-start | bytes 1048576 | tf_op jit(solution)/shard_map/all_to_all | solution.py:47
  96.0 12.9 %copy-start.3 = (f32[3,128,1024]{2,1,0:T(8,128)S(1)}, f32[3,128,1024]{2,1,0:T(8,128)}, u32[]{:S(2)}) copy-start(f32[3,128,1024]{2,1,0:T(8,128)} %get-tuple-element.19) | copy-start | bytes 4718596
  109.6 14.5 %collective-permute-start.7 = (bf16[128,1024]{1,0:T(8,128)(2,1)S(1)}, bf16[128,1024]{1,0:T(8,128)(2,1)S(1)}, u32[]{:S(2)}, u32[]{:S(2)}) collective-permute-start(bf16[128,1024]{1,0:T(8,128)(2,1)S(1)} %fusion.3), channel_id=1, source_target_pairs={{0,448},{32,96},{64,0},{96,160},{128,64},{160,224},{192,128},{224,... | collective-permute-start | bytes 786440 | tf_op jit(solution)/shard_map/ppermute | solution.py:24
  114.6 16.5 %all-to-all-start.3 = ((f32[16,8,128]{2,1,0:T(8,128)}), f32[16,8,128]{2,1,0:T(8,128)S(1)}, u32[]{:S(2)}, u32[]{:S(2)}) async-start(f32[16,8,128]{2,1,0:T(8,128)} %bitcast.31), calls=%async_computation.3 | async-start | bytes 131072 | tf_op jit(solution)/shard_map/all_to_all | solution.py:47
  124.1 18.1 %collective-permute-start.8 = (bf16[128,1024]{1,0:T(8,128)(2,1)S(1)}, bf16[128,1024]{1,0:T(8,128)(2,1)S(1)}, u32[]{:S(2)}, u32[]{:S(2)}) collective-permute-start(bf16[128,1024]{1,0:T(8,128)(2,1)S(1)} %fusion.1), channel_id=1, source_target_pairs={{0,32},{32,0},{64,96},{96,64},{128,160},{160,128},{192,224},{224,1... | collective-permute-start | bytes 786440 | tf_op jit(solution)/shard_map/ppermute | solution.py:14
